TPU v7x, 512 devices: a whole 4x4x16 slice. The times are simulated.
512 devices in a mesh: patch: 128 (over y, x, z_lo), head: 4 (over z_hi, core).
Axes of the slice: x: 4, y: 4, z: 16 (z_hi: 2, z_lo: 8; z = z_hi * 8 + z_lo), core: 2. Of those that a mesh axis runs over, the one named last changes fastest.
Arguments:
- q_fresh: bfloat16 [65536, 1536], P(('patch', 'head')), may hold values from -8 to 8
- k_fresh: bfloat16 [65536, 1536], P(('patch', 'head')), may hold values from -8 to 8
- v_fresh: bfloat16 [65536, 1536], P(('patch', 'head')), may hold values from -6 to 6
- k_stale: bfloat16 [2048, 1536], P('patch', 'head'), may hold values from -8 to 8
- v_stale: bfloat16 [2048, 1536], P('patch', 'head'), may hold values from -6 to 6
Outputs:
- attended: bfloat16 [65536, 1536], P(('patch', 'head'))
All inputs are finite; a program needn't handle non-finite values.
Results may differ from a plain program's by a relative error of at most 0.0045.
Values may be sent and summed in bfloat16 or wider, within the bound.
No kernel may reach another device: no remote copies, remote signals or barrier semaphores. Data moves between devices by JAX's collectives and lax.ppermute only.
A program may use at most 64 MiB of HBM per device.

v0:
```python
import math

import jax
import jax.numpy as jnp
from jax import lax
from jax.sharding import PartitionSpec as P

HD = 128


def attend_block(state_now, queries, key_rows, value_rows, kept_mask):
    max_old, denom_old, accum_old = state_now
    row_span = key_rows.shape[0]
    heads_here = queries.shape[1]
    scaling = queries.shape[2] ** (-0.5)
    key_heads = key_rows.reshape(row_span, heads_here, -1)
    value_heads = value_rows.reshape(row_span, heads_here, -1)
    scores = (
        jnp.einsum("qhd,khd->hqk", queries, key_heads, preferred_element_type=jnp.float32) * scaling
    )
    masked = jnp.where(kept_mask[None, None, :], scores, -jnp.inf)
    max_new = jnp.maximum(max_old, jnp.max(masked, axis=2))
    shrink = jnp.exp(max_old - max_new)
    weights = jnp.exp(masked - max_new[:, :, None])
    denom_new = denom_old * shrink + jnp.sum(weights, axis=2)
    mixed = jnp.einsum(
        "hqk,khd->qhd",
        weights.astype(jnp.bfloat16),
        value_heads,
        preferred_element_type=jnp.float32,
    )
    accum_new = accum_old * jnp.transpose(shrink)[:, :, None] + mixed
    return (max_new, denom_new, accum_new)


def local(q_fresh, k_fresh, v_fresh, k_stale, v_stale):
    queries, keys_new, values_new = (
        lax.all_to_all(q_fresh, "head", split_axis=1, concat_axis=0, tiled=True),
        lax.all_to_all(k_fresh, "head", split_axis=1, concat_axis=0, tiled=True),
        lax.all_to_all(v_fresh, "head", split_axis=1, concat_axis=0, tiled=True),
    )
    row_count = queries.shape[0]
    heads_here = queries.shape[1] // HD
    query_heads = queries.reshape(row_count, heads_here, HD)
    pooled_rows = k_stale.shape[0]
    own_first = lax.axis_index("patch") * pooled_rows
    start_state = (
        jnp.full((heads_here, row_count), -jnp.inf, jnp.float32),
        jnp.zeros((heads_here, row_count), jnp.float32),
        jnp.zeros((row_count, heads_here, HD), jnp.float32),
    )
    fresh_rows = math.gcd(row_count, 512)

    def visit_fresh(turn, state_now):
        first_row = turn * fresh_rows
        return attend_block(
            state_now, query_heads, keys_new, values_new, jnp.ones((fresh_rows,), jnp.bool_)
        )

    state = lax.fori_loop(0, row_count // fresh_rows, visit_fresh, start_state)

    def outside_own(positions):
        return (positions < own_first) | (positions >= own_first + pooled_rows)

    gathered_keys, gathered_values = (
        lax.all_gather(k_stale, "patch", axis=0, tiled=True),
        lax.all_gather(v_stale, "patch", axis=0, tiled=True),
    )
    block_rows = math.gcd(gathered_keys.shape[0], 512)
    turns = gathered_keys.shape[0] // block_rows

    def visit(turn, state_now):
        first_row = turn * block_rows
        key_rows = lax.dynamic_slice_in_dim(gathered_keys, first_row, block_rows, 0)
        value_rows = lax.dynamic_slice_in_dim(gathered_values, first_row, block_rows, 0)
        positions = first_row + jnp.arange(block_rows, dtype=jnp.int32)
        return attend_block(state_now, query_heads, key_rows, value_rows, outside_own(positions))

    state = lax.fori_loop(0, turns, visit, state)
    max_final, denom_final, accum_final = state
    attended = (
        (accum_final / jnp.transpose(denom_final)[:, :, None])
        .reshape(row_count, -1)
        .astype(jnp.bfloat16)
    )
    return lax.all_to_all(attended, "head", split_axis=0, concat_axis=1, tiled=True)


def solution(mesh):
    placed = (
        P(("patch", "head"), None),
        P(("patch", "head"), None),
        P(("patch", "head"), None),
        P("patch", "head"),
        P("patch", "head"),
    )
    return jax.shard_map(
        local, mesh=mesh, in_specs=placed, out_specs=P(("patch", "head"), None), check_vma=False
    )
```

profile of v0, /device:TPU:1, one launch (start us, length us, event | category | flops | bytes accessed | tf_op | source)
XLA Modules:
  0.0 2017.8 jit_solution(2284859001815713850)
XLA Ops:
  7.3 1.9 copy.44
  9.2 16.6 all-to-all-start
  25.8 1.9 copy.46
  27.7 13.6 all-to-all-done
  41.2 4.5 all-to-all-start.1
  47.4 13.8 all-to-all-done.1
  61.2 6.2 all-to-all-start.2
  68.4 14.4 all-to-all-done.2
  88.0 809.2 %all-gather.3.cloned.1.call-done = bf16[2048,384]{1,0:T(8,128)(2,1)} async-done(((bf16[16,384]{1,0:T(8,128)(2,1)}), bf16[2048,384]{1,0:T(8,128)(2,1)}) %all-gather.3.cloned.1.call-update) | async-done | bytes 1572880 | tf_op jit(solution)/shard_map/all_gather | solution.py:66
  897.2 960.8 %all-gather.5.cloned.1.call-done = bf16[2048,384]{1,0:T(8,128)(2,1)} async-done(((bf16[16,384]{1,0:T(8,128)(2,1)}), bf16[2048,384]{1,0:T(8,128)(2,1)}) %all-gather.5.cloned.1.call-update) | async-done | bytes 1572880 | tf_op jit(solution)/shard_map/all_gather | solution.py:67
  1857.9 40.3 %while.5 = (s32[]{:T(128)}, f32[3,512]{1,0:T(4,128)S(1)}, f32[3,512]{1,0:T(4,128)}, f32[512,3,128]{0,2,1:T(8,128)}, s32[]{:T(128)}, /*index=5*/s32[]{:T(128)}, b...) while((s32[]{:T(128)}, f32[3,512]{1,0:T(4,128)S(1)}, ...), condition=%wide.region_5.0_spmd, body=%wide.region_2.5_spmd.sunk | while | flops 411703808 | bytes 15489323 | solution.py:79
  1857.9 1.9 constant_dynamic-slice_fusion.3
  1860.1 1.8 bitcast_reduce_fusion.2
  1863.7 3.0 fusion.57
  1868.0 1.9 constant_dynamic-slice_fusion.3
  1870.2 1.8 bitcast_reduce_fusion.2
  1873.8 3.0 fusion.57
  1878.1 1.9 constant_dynamic-slice_fusion.3
  1880.3 1.8 bitcast_reduce_fusion.2
  1883.8 3.0 fusion.57
  1888.2 1.9 constant_dynamic-slice_fusion.3
  1890.3 1.8 bitcast_reduce_fusion.2
  1893.9 3.0 fusion.57
  1899.9 109.9 %all_to_all.64 = bf16[4,128,384]{2,1,0:T(8,128)(2,1)S(1)} all-to-all(bf16[4,128,384]{2,1,0:T(8,128)(2,1)S(1)} %copy.58), channel_id=1, replica_groups=mesh['patch'=128,'head'=4] {'head'}, dimensions={0} | all-to-all | bytes 786432 | tf_op jit(solution)/shard_map/all_to_all | solution.py:86
  (84 shorter events, 24.5 us)
Async XLA Ops:
  6.5 39.9 %copy-start.2 = (bf16[128,1536]{1,0:T(8,128)(2,1)S(1)}, bf16[128,1536]{1,0:T(8,128)(2,1)}, u32[]{:S(2)}) copy-start(bf16[128,1536]{1,0:T(8,128)(2,1)} %param.9) | copy-start | bytes 1179652
  6.5 890.7 %all-gather.3.cloned.1.call-start = ((), (), s32[]{:S(2)}) async-start(), calls=%async_computation.4 | async-start | bytes 1585152 | tf_op jit(solution)/shard_map/all_gather | solution.py:66
  9.2 32.1 %all-to-all-start = ((bf16[128,4,384]{0,2,1:T(8,128)(2,1)}), bf16[128,4,384]{0,2,1:T(8,128)(2,1)S(1)}, u32[]{:S(2)}, u32[]{:S(2)}) async-start(bf16[128,4,384]{0,2,1:T(8,128)(2,1)} %bitcast.5), calls=%async_computation | async-start | bytes 786432 | tf_op jit(solution)/shard_map/all_to_all | solution.py:38
  41.2 20.0 all-to-all-start.1
  45.7 1812.2 %all-gather.5.cloned.1.call-start = ((), (), s32[]{:S(2)}) async-start(), calls=%async_computation.5 | async-start | bytes 1585152 | tf_op jit(solution)/shard_map/all_gather | solution.py:67
  61.2 21.5 %all-to-all-start.2 = ((bf16[128,4,384]{0,2,1:T(8,128)(2,1)}), bf16[128,4,384]{0,2,1:T(8,128)(2,1)S(1)}, u32[]{:S(2)}, u32[]{:S(2)}) async-start(bf16[128,4,384]{0,2,1:T(8,128)(2,1)} %bitcast.10), calls=%async_computation.2 | async-start | bytes 786432 | tf_op jit(solution)/shard_map/all_to_all | solution.py:40
  1860.1 2.4 copy-start.3
  1863.7 3.0 copy-start.4
  1863.7 3.7 copy-start
  1867.4 0.6 copy-start.1
  1870.2 2.4 copy-start.3
  1873.8 3.0 copy-start.4
  1873.8 3.7 copy-start
  1877.5 0.6 copy-start.1
  1880.2 2.4 copy-start.3
  1883.8 3.0 copy-start.4
  1883.8 3.7 copy-start
  1887.6 0.6 copy-start.1
  1890.3 2.4 copy-start.3
  1893.9 3.0 copy-start.4
  1893.9 3.7 copy-start
  1897.6 0.6 copy-start.1
Sparse Core Ops, SparseCore 0:
  9.4 887.7 all-gather.2
  899.3 958.6 all-gather.4
where the time goes:
time: 2020 us
  waiting for transfers between devices  1810 us (90%)
  blocking collectives  110 us (5%)
  starting transfers between devices  27.3 us (1%)
  local copies, waits for them, and re-layouts  25.3 us (1%)
  matrix products  20.6 us (1%)
    all_gather x1, waiting for transfers between devices, local(): lax.all_gather(v_stale, 'patch', axis=0, tiled=True)  961 us
    all_gather x1, waiting for transfers between devices, local(): lax.all_gather(k_stale, 'patch', axis=0, tiled=True)  809 us
    all_to_all x1, blocking collectives, local(): lax.all_to_all(attended, 'head', split_axis=0, concat_axis=1, tiled=True)  110 us
  transfers between devices with their start and end apart: 5, of which 5 were waited for; matrix products, arithmetic and copies ran while one was open for 1% of the time, Pallas kernels for 0%

commit v1 on v0

v1 whole, which is shorter than its diff:
```python
import functools
import math

import jax
import jax.numpy as jnp
import numpy as np
from jax import lax
from jax.experimental import pallas as pl
from jax.experimental.pallas import tpu as pltpu
from jax.sharding import Mesh
from jax.sharding import PartitionSpec as P

HD = 128
EVERY = ("y", "x", "zl", "zh", "core")
SIZES = (4, 4, 8, 2, 2)
ROWS = 128
SCALE = HD**-0.5 * math.log2(math.e)
NT = (((1,), (1,)), ((), ()))
F32 = jnp.float32


def weigh(own_ref, q_ref, k_ref, *refs):
    keys, values = refs[0:4], refs[4:8]
    acc_ref, fresh_ref, total_ref, s_ref = refs[8:12]
    heads = q_ref.shape[1] // HD
    fresh = k_ref.shape[0]
    block = keys[0].shape[0] // 4
    first = own_ref[0]
    cols = lax.broadcasted_iota(jnp.int32, (ROWS, block), 1)
    own = (cols >= first) & (cols < first + 16)
    lane = lax.broadcasted_iota(jnp.int32, (ROWS, HD), 1)

    def rows_step(i, carry):
        rows = pl.ds(pl.multiple_of(i * ROWS, ROWS), ROWS)
        totals = jnp.zeros((ROWS, HD), F32)
        for h in range(heads):
            cs = slice(h * HD, (h + 1) * HD)
            q = q_ref[rows, cs]
            top = jnp.full((ROWS, HD), -jnp.inf, F32)
            for dy in range(4):
                s = lax.dot_general(q, keys[dy][:, cs], NT, preferred_element_type=F32)
                for dx in range(4):
                    part = s[:, dx * block : (dx + 1) * block]
                    if dy == 0 and dx == 0:
                        part = jnp.where(own, -jnp.inf, part)
                    at = (dx * 4 + dy) * block
                    s_ref[h, :, at : at + block] = part
                    top = jnp.maximum(top, part)
            s = lax.dot_general(q, k_ref[:, cs], NT, preferred_element_type=F32)
            s_ref[h, :, 16 * block :] = s
            for c in range(0, fresh, HD):
                top = jnp.maximum(top, s[:, c : c + HD])
            top = jnp.max(top, axis=1, keepdims=True) * SCALE
            sums = jnp.zeros((ROWS, HD), F32)
            acc = jnp.zeros((ROWS, HD), F32)
            for dx in range(5):
                width = 4 * block if dx < 4 else fresh
                w = jnp.exp2(s_ref[h, :, dx * 4 * block : dx * 4 * block + width] * SCALE - top)
                for c in range(0, width, HD):
                    sums = sums + w[:, c : c + HD]
                rounded = w.astype(jnp.bfloat16)
                if dx < 4:
                    acc = acc + jnp.dot(rounded, values[dx][:, cs], preferred_element_type=F32)
                else:
                    fresh_ref[h, rows, :] = rounded
            acc_ref[rows, cs] = acc
            total = jnp.sum(sums, axis=1, keepdims=True)
            totals = jnp.where(lane == h, total, totals)
        total_ref[rows, :] = totals
        return carry

    lax.fori_loop(0, q_ref.shape[0] // ROWS, rows_step, 0)


def finish(v_ref, acc_ref, fresh_ref, total_ref, out_ref):
    for h in range(acc_ref.shape[1] // HD):
        cs = slice(h * HD, (h + 1) * HD)
        acc = acc_ref[:, cs] + jnp.dot(fresh_ref[h], v_ref[:, cs], preferred_element_type=F32)
        out_ref[:, cs] = (acc / total_ref[:, h : h + 1]).astype(out_ref.dtype)


def moves(axis, step):
    pairs = []
    at = EVERY.index(axis)
    for i in range(math.prod(SIZES)):
        place = list(np.unravel_index(i, SIZES))
        place[at] = (place[at] - step) % SIZES[at]
        pairs.append((i, int(np.ravel_multi_index(place, SIZES))))
    return pairs


def ring(block, axis):
    return [block] + [lax.ppermute(block, EVERY, moves(axis, d)) for d in (1, 2, 3)]


def swap(rows_of):
    return lax.all_to_all(rows_of, ("zh", "core"), split_axis=0, concat_axis=0, tiled=False)


def local(q_fresh, k_fresh, v_fresh, k_stale, v_stale):
    tokens, width = q_fresh.shape
    mine = k_stale.shape[1]
    pooled = k_stale.shape[0]
    heads = mine // HD
    both = jnp.concatenate([k_stale, v_stale], axis=1)
    line = lax.all_to_all(
        jnp.broadcast_to(both[None], (8, pooled, 2 * mine)), "zl", split_axis=0, concat_axis=0
    ).reshape(8 * pooled, 2 * mine)

    def to_heads(a):
        return swap(a.reshape(tokens, 4, mine).transpose(1, 0, 2)).reshape(4 * tokens, mine)

    q, k, v = to_heads(q_fresh), to_heads(k_fresh), to_heads(v_fresh)
    keys = ring(jnp.concatenate(ring(line[:, :mine], "x"), axis=0), "y")
    values = ring(jnp.concatenate(ring(line[:, mine:], "y"), axis=0), "x")
    own = (lax.axis_index("zl") * pooled).astype(jnp.int32).reshape(1)

    n, f = 4 * tokens, k.shape[0]
    vm = pl.BlockSpec(memory_space=pltpu.VMEM)
    total_keys = 16 * 8 * pooled + f
    acc, fresh, totals = pl.pallas_call(
        weigh,
        out_shape=(
            jax.ShapeDtypeStruct((n, mine), F32),
            jax.ShapeDtypeStruct((heads, n, f), jnp.bfloat16),
            jax.ShapeDtypeStruct((n, HD), F32),
        ),
        in_specs=[pl.BlockSpec(memory_space=pltpu.SMEM)] + [vm] * 10,
        out_specs=(vm, vm, vm),
        scratch_shapes=[pltpu.VMEM((heads, ROWS, total_keys), F32)],
        compiler_params=pltpu.CompilerParams(vmem_limit_bytes=40 << 20),
        cost_estimate=pl.CostEstimate(
            flops=4 * n * heads * total_keys * HD, bytes_accessed=10 << 20, transcendentals=n * heads * total_keys
        ),
        name="weigh",
    )(own, q, k, *keys, *values)
    out = pl.pallas_call(
        finish,
        out_shape=jax.ShapeDtypeStruct((n, mine), jnp.bfloat16),
        in_specs=[vm] * 4,
        out_specs=vm,
        compiler_params=pltpu.CompilerParams(vmem_limit_bytes=40 << 20),
        cost_estimate=pl.CostEstimate(flops=2 * n * heads * f * HD, bytes_accessed=4 << 20, transcendentals=0),
        name="finish",
    )(v, acc, fresh, totals)
    return swap(out.reshape(4, tokens, mine)).transpose(1, 0, 2).reshape(tokens, width)


def solution(mesh):
    fine = Mesh(mesh.devices.reshape(SIZES), EVERY)
    whole = P(EVERY, None)
    part = P(("y", "x", "zl"), ("zh", "core"))
    return jax.shard_map(
        local,
        mesh=fine,
        in_specs=(whole, whole, whole, part, part),
        out_specs=whole,
        check_vma=False,
    )
```

time: 2020 us -> 194 us (0.10)
  the two profiles are of different devices: /device:TPU:1 before, /device:TPU:32 now
where the time goes in v1:
time: 194 us; the launch traced here: 192 us
  starting transfers between devices  70.4 us (36%)
  waiting for transfers between devices  60.9 us (31%)
  blocking collectives  32.3 us (17%)
  local copies, waits for them, and re-layouts  18 us (9%)
  Pallas kernels  9.68 us (5%)
    ppermute x12, starting transfers between devices, ring(): lax.ppermute(block, EVERY, moves(axis, d))  42.3 us
    all_to_all x3, waiting for transfers between devices, swap(): lax.all_to_all(rows_of, ('zh', 'core'), split_axis=0, concat_axis=0, tile...  36.3 us
    all_to_all x1, blocking collectives, swap(): lax.all_to_all(rows_of, ('zh', 'core'), split_axis=0, concat_axis=0, tile...  32.3 us
    all_to_all x3, starting transfers between devices, swap(): lax.all_to_all(rows_of, ('zh', 'core'), split_axis=0, concat_axis=0, tile...  15.5 us
    unnamed x36, local copies, waits for them, and re-layouts  13.1 us
    ppermute x12, waiting for transfers between devices, ring(): lax.ppermute(block, EVERY, moves(axis, d))  12.8 us
    all_to_all x1, starting transfers between devices, local(): lax.all_to_all(jnp.broadcast_to(both[None], (8, pooled, 2 * mine)), 'zl',...  12.6 us
    all_to_all x1, waiting for transfers between devices, local(): lax.all_to_all(jnp.broadcast_to(both[None], (8, pooled, 2 * mine)), 'zl',...  11.8 us
  transfers between devices with their start and end apart: 16, of which 6 were waited for; matrix products, arithmetic and copies ran while one was open for 2% of the time, Pallas kernels for 5%

profile of v1, /device:TPU:32, one launch (start us, length us, event | category | flops | bytes accessed | tf_op | source)
XLA Modules:
  0.0 192.3 jit_solution(16645099712646603211)
XLA Ops:
  1.5 12.6 %all-to-all-start.3 = ((bf16[8,16,768]{2,1,0:T(8,128)(2,1)}), bf16[8,16,768]{2,1,0:T(8,128)(2,1)S(1)}, u32[]{:S(2)}, u32[]{:S(2)}) async-start(bf16[8,16,768]{2,1,0:T(8,128)(2,1)} %broadcast_in_dim.2), calls=%async_computation.3 | async-start | bytes 393216 | tf_op jit(solution)/shard_map/all_to_all | solution.py:106
  14.1 1.8 copy.18
  15.9 11.8 %all-to-all-done.3 = bf16[8,16,768]{2,1,0:T(8,128)(2,1)S(1)} async-done(((bf16[8,16,768]{2,1,0:T(8,128)(2,1)}), bf16[8,16,768]{2,1,0:T(8,128)(2,1)S(1)}, u32[]{:S(2)}, u32[]{:S(2)}) %all-to-all-start.3) | async-done | bytes 196640 | tf_op jit(solution)/shard_map/all_to_all | solution.py:106
  27.7 7.6 %all-to-all-start.1 = ((bf16[4,128,384]{2,1,0:T(8,128)(2,1)}), bf16[4,128,384]{2,1,0:T(8,128)(2,1)S(1)}, u32[]{:S(2)}, u32[]{:S(2)}) async-start(bf16[4,128,384]{2,1,0:T(8,128)(2,1)} %bitcast.27), calls=%async_computation.1 | async-start | bytes 786432 | tf_op jit(solution)/shard_map/all_to_all | solution.py:97
  36.1 27.0 %all-to-all-done.1 = bf16[4,128,384]{2,1,0:T(8,128)(2,1)S(1)} async-done(((bf16[4,128,384]{2,1,0:T(8,128)(2,1)}), bf16[4,128,384]{2,1,0:T(8,128)(2,1)S(1)}, u32[]{:S(2)}, u32[]{:S(2)}) %all-to-all-start.1) | async-done | bytes 393248 | tf_op jit(solution)/shard_map/all_to_all | solution.py:97
  63.1 3.5 %all-to-all-start.2 = ((bf16[4,128,384]{2,1,0:T(8,128)(2,1)}), bf16[4,128,384]{2,1,0:T(8,128)(2,1)S(1)}, u32[]{:S(2)}, u32[]{:S(2)}) async-start(bf16[4,128,384]{2,1,0:T(8,128)(2,1)} %bitcast.25), calls=%async_computation.2 | async-start | bytes 786432 | tf_op jit(solution)/shard_map/all_to_all | solution.py:97
  66.6 4.9 %collective-permute-start.6 = (bf16[128,384]{1,0:T(8,128)(2,1)S(1)}, bf16[128,384]{1,0:T(8,128)(2,1)S(1)}, u32[]{:S(2)}, u32[]{:S(2)}) collective-permute-start(bf16[128,384]{1,0:T(8,128)(2,1)S(1)} %get-tuple-element.11), channel_id=1, source_target_pairs={{0,384},{1,385},{2,386},{3,387},{4,388},{5,389},{6,390},{7,391},{8... | collective-permute-start | bytes 294920 | tf_op jit(solution)/shard_map/ppermute | solution.py:93
  71.5 2.5 %collective-permute-start.7 = (bf16[128,384]{1,0:T(8,128)(2,1)S(1)}, bf16[128,384]{1,0:T(8,128)(2,1)S(1)}, u32[]{:S(2)}, u32[]{:S(2)}) collective-permute-start(bf16[128,384]{1,0:T(8,128)(2,1)S(1)} %get-tuple-element.11), channel_id=1, source_target_pairs={{0,256},{1,257},{2,258},{3,259},{4,260},{5,261},{6,262},{7,263},{8... | collective-permute-start | bytes 294920 | tf_op jit(solution)/shard_map/ppermute | solution.py:93
  74.1 2.9 %collective-permute-start.8 = (bf16[128,384]{1,0:T(8,128)(2,1)S(1)}, bf16[128,384]{1,0:T(8,128)(2,1)S(1)}, u32[]{:S(2)}, u32[]{:S(2)}) collective-permute-start(bf16[128,384]{1,0:T(8,128)(2,1)S(1)} %get-tuple-element.11), channel_id=1, source_target_pairs={{0,128},{1,129},{2,130},{3,131},{4,132},{5,133},{6,134},{7,135},{8... | collective-permute-start | bytes 294920 | tf_op jit(solution)/shard_map/ppermute | solution.py:93
  77.8 9.3 %all-to-all-done.2 = bf16[4,128,384]{2,1,0:T(8,128)(2,1)S(1)} async-done(((bf16[4,128,384]{2,1,0:T(8,128)(2,1)}), bf16[4,128,384]{2,1,0:T(8,128)(2,1)S(1)}, u32[]{:S(2)}, u32[]{:S(2)}) %all-to-all-start.2) | async-done | bytes 393248 | tf_op jit(solution)/shard_map/all_to_all | solution.py:97
  87.0 4.4 %all-to-all-start = ((bf16[4,128,384]{2,1,0:T(8,128)(2,1)}), bf16[4,128,384]{2,1,0:T(8,128)(2,1)S(1)}, u32[]{:S(2)}, u32[]{:S(2)}) async-start(bf16[4,128,384]{2,1,0:T(8,128)(2,1)} %bitcast.29), calls=%async_computation | async-start | bytes 786432 | tf_op jit(solution)/shard_map/all_to_all | solution.py:97
  91.5 4.9 %collective-permute-start.10 = (bf16[512,384]{1,0:T(8,128)(2,1)S(1)}, bf16[512,384]{1,0:T(8,128)(2,1)S(1)}, u32[]{:S(2)}, u32[]{:S(2)}) collective-permute-start(bf16[512,384]{1,0:T(8,128)(2,1)S(1)} %pad_maximum_fusion.1.refs_4_), channel_id=1, source_target_pairs={{0,64},{1,65},{2,66},{3,67},{4,68},{5,69},{6,70},{7,71},{8,72},{9,... | collective-permute-start | bytes 1179656 | tf_op jit(solution)/shard_map/ppermute | solution.py:93
  96.5 3.0 %collective-permute-start = (bf16[128,384]{1,0:T(8,128)(2,1)S(1)}, bf16[128,384]{1,0:T(8,128)(2,1)S(1)}, u32[]{:S(2)}, u32[]{:S(2)}) collective-permute-start(bf16[128,384]{1,0:T(8,128)(2,1)S(1)} %get-tuple-element.12), channel_id=1, source_target_pairs={{0,96},{1,97},{2,98},{3,99},{4,100},{5,101},{6,102},{7,103},{8,104... | collective-permute-start | bytes 294920 | tf_op jit(solution)/shard_map/ppermute | solution.py:93
  99.5 3.4 %collective-permute-start.1 = (bf16[128,384]{1,0:T(8,128)(2,1)S(1)}, bf16[128,384]{1,0:T(8,128)(2,1)S(1)}, u32[]{:S(2)}, u32[]{:S(2)}) collective-permute-start(bf16[128,384]{1,0:T(8,128)(2,1)S(1)} %get-tuple-element.12), channel_id=1, source_target_pairs={{0,64},{1,65},{2,66},{3,67},{4,68},{5,69},{6,70},{7,71},{8,72},{9,... | collective-permute-start | bytes 294920 | tf_op jit(solution)/shard_map/ppermute | solution.py:93
  103.0 1.9 collective-permute-start.2
  104.9 3.9 %collective-permute-start.11 = (bf16[512,384]{1,0:T(8,128)(2,1)S(1)}, bf16[512,384]{1,0:T(8,128)(2,1)S(1)}, u32[]{:S(2)}, u32[]{:S(2)}) collective-permute-start(bf16[512,384]{1,0:T(8,128)(2,1)S(1)} %pad_maximum_fusion.1.refs_4_), channel_id=1, source_target_pairs={{0,32},{1,33},{2,34},{3,35},{4,36},{5,37},{6,38},{7,39},{8,40},{9,... | collective-permute-start | bytes 1179656 | tf_op jit(solution)/shard_map/ppermute | solution.py:93
  109.1 4.5 %collective-permute-start.9 = (bf16[512,384]{1,0:T(8,128)(2,1)S(1)}, bf16[512,384]{1,0:T(8,128)(2,1)S(1)}, u32[]{:S(2)}, u32[]{:S(2)}) collective-permute-start(bf16[512,384]{1,0:T(8,128)(2,1)S(1)} %pad_maximum_fusion.1.refs_4_), channel_id=1, source_target_pairs={{0,96},{1,97},{2,98},{3,99},{4,100},{5,101},{6,102},{7,103},{8,104... | collective-permute-start | bytes 1179656 | tf_op jit(solution)/shard_map/ppermute | solution.py:93
  113.6 4.9 %collective-permute-start.3 = (bf16[512,384]{1,0:T(8,128)(2,1)S(1)}, bf16[512,384]{1,0:T(8,128)(2,1)S(1)}, u32[]{:S(2)}, u32[]{:S(2)}) collective-permute-start(bf16[512,384]{1,0:T(8,128)(2,1)S(1)} %pad_maximum_fusion.refs_0_), channel_id=1, source_target_pairs={{0,384},{1,385},{2,386},{3,387},{4,388},{5,389},{6,390},{7,391},{8... | collective-permute-start | bytes 1179656 | tf_op jit(solution)/shard_map/ppermute | solution.py:93
  118.6 2.5 %collective-permute-start.4 = (bf16[512,384]{1,0:T(8,128)(2,1)S(1)}, bf16[512,384]{1,0:T(8,128)(2,1)S(1)}, u32[]{:S(2)}, u32[]{:S(2)}) collective-permute-start(bf16[512,384]{1,0:T(8,128)(2,1)S(1)} %pad_maximum_fusion.refs_0_), channel_id=1, source_target_pairs={{0,256},{1,257},{2,258},{3,259},{4,260},{5,261},{6,262},{7,263},{8... | collective-permute-start | bytes 1179656 | tf_op jit(solution)/shard_map/ppermute | solution.py:93
  121.9 2.9 %collective-permute-start.5 = (bf16[512,384]{1,0:T(8,128)(2,1)S(1)}, bf16[512,384]{1,0:T(8,128)(2,1)}, u32[]{:S(2)}, u32[]{:S(2)}) collective-permute-start(bf16[512,384]{1,0:T(8,128)(2,1)S(1)} %pad_maximum_fusion.refs_0_), channel_id=1, source_target_pairs={{0,128},{1,129},{2,130},{3,131},{4,132},{5,133},{6,134},{7,135},{8... | collective-permute-start | bytes 1179656 | tf_op jit(solution)/shard_map/ppermute | solution.py:93
  127.0 8.2 %collective-permute-done.3.refs_1_ = bf16[512,384]{1,0:T(8,128)(2,1)S(1)} collective-permute-done((bf16[512,384]{1,0:T(8,128)(2,1)S(1)}, bf16[512,384]{1,0:T(8,128)(2,1)S(1)}, u32[]{:S(2)}, u32[]{:S(2)}) %collective-permute-start.3) | collective-permute-done | bytes 393248 | tf_op jit(solution)/shard_map/ppermute | solution.py:93
  136.7 4.2 %collective-permute-done.5.refs_3_ = bf16[512,384]{1,0:T(8,128)(2,1)} collective-permute-done((bf16[512,384]{1,0:T(8,128)(2,1)S(1)}, bf16[512,384]{1,0:T(8,128)(2,1)}, u32[]{:S(2)}, u32[]{:S(2)}) %collective-permute-start.5) | collective-permute-done | bytes 393248 | tf_op jit(solution)/shard_map/ppermute | solution.py:93
  147.9 9.1 %weigh.1 = (f32[512,384]{1,0:T(8,128)S(1)}, bf16[3,512,512]{2,1,0:T(8,128)(2,1)S(1)}, f32[512,128]{1,0:T(8,128)S(1)}) custom-call(s32[1]{0:T(128)} %bitcast.2.own_ref, bf16[512,384]{1,0:T(8,128)(2,1)S(1)} %bitcast.32, bf16[512,384]{1,0:T(8,128)(2,1)S(1)} %bitcast.33, bf16[512,384]{1,0:T(8,128)(2,1)S(1)} %copy-done.3, bf16[512,384]{1,0:T(8,128)(2,1)S(1)} %copy-done.13, ...), custom_call_target="tpu_custom_call" | custom-call | flops 2013265920 | bytes 10485760 | tf_op jit(solution)/shard_map/weigh/pallas_call | solution.py:121
  159.3 32.3 %all_to_all.25 = bf16[4,128,384]{2,1,0:T(8,128)(2,1)S(1)} all-to-all(bf16[4,128,384]{2,1,0:T(8,128)(2,1)S(1)} %bitcast.31), channel_id=1, replica_groups=mesh['y'=4,'x'=4,'zl'=8,'zh'=2,'core'=2] {'zh','core'}, dimensions={0} | all-to-all | bytes 786432 | tf_op jit(solution)/shard_map/all_to_all | solution.py:97
  (56 shorter events, 18.0 us)
Async XLA Ops:
  0.0 35.3 %copy-start.16 = (bf16[128,1536]{1,0:T(8,128)(2,1)S(1)}, bf16[128,1536]{1,0:T(8,128)(2,1)}, u32[]{:S(2)}) copy-start(bf16[128,1536]{1,0:T(8,128)(2,1)} %param.6) | copy-start | bytes 1179652
  1.5 26.2 %all-to-all-start.3 = ((bf16[8,16,768]{2,1,0:T(8,128)(2,1)}), bf16[8,16,768]{2,1,0:T(8,128)(2,1)S(1)}, u32[]{:S(2)}, u32[]{:S(2)}) async-start(bf16[8,16,768]{2,1,0:T(8,128)(2,1)} %broadcast_in_dim.2), calls=%async_computation.3 | async-start | bytes 393216 | tf_op jit(solution)/shard_map/all_to_all | solution.py:106
  15.9 61.1 %copy-start.17 = (bf16[128,1536]{1,0:T(8,128)(2,1)S(1)}, bf16[128,1536]{1,0:T(8,128)(2,1)}, u32[]{:S(2)}) copy-start(bf16[128,1536]{1,0:T(8,128)(2,1)} %param.7) | copy-start | bytes 1179652
  27.7 35.4 %all-to-all-start.1 = ((bf16[4,128,384]{2,1,0:T(8,128)(2,1)}), bf16[4,128,384]{2,1,0:T(8,128)(2,1)S(1)}, u32[]{:S(2)}, u32[]{:S(2)}) async-start(bf16[4,128,384]{2,1,0:T(8,128)(2,1)} %bitcast.27), calls=%async_computation.1 | async-start | bytes 786432 | tf_op jit(solution)/shard_map/all_to_all | solution.py:97
  63.1 23.9 %all-to-all-start.2 = ((bf16[4,128,384]{2,1,0:T(8,128)(2,1)}), bf16[4,128,384]{2,1,0:T(8,128)(2,1)S(1)}, u32[]{:S(2)}, u32[]{:S(2)}) async-start(bf16[4,128,384]{2,1,0:T(8,128)(2,1)} %bitcast.25), calls=%async_computation.2 | async-start | bytes 786432 | tf_op jit(solution)/shard_map/all_to_all | solution.py:97
  66.6 24.9 %collective-permute-start.6 = (bf16[128,384]{1,0:T(8,128)(2,1)S(1)}, bf16[128,384]{1,0:T(8,128)(2,1)S(1)}, u32[]{:S(2)}, u32[]{:S(2)}) collective-permute-start(bf16[128,384]{1,0:T(8,128)(2,1)S(1)} %get-tuple-element.11), channel_id=1, source_target_pairs={{0,384},{1,385},{2,386},{3,387},{4,388},{5,389},{6,390},{7,391},{8... | collective-permute-start | bytes 294920 | tf_op jit(solution)/shard_map/ppermute | solution.py:93
  71.5 19.9 %collective-permute-start.7 = (bf16[128,384]{1,0:T(8,128)(2,1)S(1)}, bf16[128,384]{1,0:T(8,128)(2,1)S(1)}, u32[]{:S(2)}, u32[]{:S(2)}) collective-permute-start(bf16[128,384]{1,0:T(8,128)(2,1)S(1)} %get-tuple-element.11), channel_id=1, source_target_pairs={{0,256},{1,257},{2,258},{3,259},{4,260},{5,261},{6,262},{7,263},{8... | collective-permute-start | bytes 294920 | tf_op jit(solution)/shard_map/ppermute | solution.py:93
  74.1 17.4 %collective-permute-start.8 = (bf16[128,384]{1,0:T(8,128)(2,1)S(1)}, bf16[128,384]{1,0:T(8,128)(2,1)S(1)}, u32[]{:S(2)}, u32[]{:S(2)}) collective-permute-start(bf16[128,384]{1,0:T(8,128)(2,1)S(1)} %get-tuple-element.11), channel_id=1, source_target_pairs={{0,128},{1,129},{2,130},{3,131},{4,132},{5,133},{6,134},{7,135},{8... | collective-permute-start | bytes 294920 | tf_op jit(solution)/shard_map/ppermute | solution.py:93
  87.0 70.7 %all-to-all-start = ((bf16[4,128,384]{2,1,0:T(8,128)(2,1)}), bf16[4,128,384]{2,1,0:T(8,128)(2,1)S(1)}, u32[]{:S(2)}, u32[]{:S(2)}) async-start(bf16[4,128,384]{2,1,0:T(8,128)(2,1)} %bitcast.29), calls=%async_computation | async-start | bytes 786432 | tf_op jit(solution)/shard_map/all_to_all | solution.py:97
  91.5 49.4 %copy-start = (bf16[512,384]{1,0:T(8,128)(2,1)}, bf16[512,384]{1,0:T(8,128)(2,1)S(1)}, u32[]{:S(2)}) copy-start(bf16[512,384]{1,0:T(8,128)(2,1)S(1)} %pad_maximum_fusion.1.refs_4_) | copy-start | bytes 1179652
  91.5 29.6 %collective-permute-start.10 = (bf16[512,384]{1,0:T(8,128)(2,1)S(1)}, bf16[512,384]{1,0:T(8,128)(2,1)S(1)}, u32[]{:S(2)}, u32[]{:S(2)}) collective-permute-start(bf16[512,384]{1,0:T(8,128)(2,1)S(1)} %pad_maximum_fusion.1.refs_4_), channel_id=1, source_target_pairs={{0,64},{1,65},{2,66},{3,67},{4,68},{5,69},{6,70},{7,71},{8,72},{9,... | collective-permute-start | bytes 1179656 | tf_op jit(solution)/shard_map/ppermute | solution.py:93
  96.5 12.6 %collective-permute-start = (bf16[128,384]{1,0:T(8,128)(2,1)S(1)}, bf16[128,384]{1,0:T(8,128)(2,1)S(1)}, u32[]{:S(2)}, u32[]{:S(2)}) collective-permute-start(bf16[128,384]{1,0:T(8,128)(2,1)S(1)} %get-tuple-element.12), channel_id=1, source_target_pairs={{0,96},{1,97},{2,98},{3,99},{4,100},{5,101},{6,102},{7,103},{8,104... | collective-permute-start | bytes 294920 | tf_op jit(solution)/shard_map/ppermute | solution.py:93
  99.5 14.0 %collective-permute-start.1 = (bf16[128,384]{1,0:T(8,128)(2,1)S(1)}, bf16[128,384]{1,0:T(8,128)(2,1)S(1)}, u32[]{:S(2)}, u32[]{:S(2)}) collective-permute-start(bf16[128,384]{1,0:T(8,128)(2,1)S(1)} %get-tuple-element.12), channel_id=1, source_target_pairs={{0,64},{1,65},{2,66},{3,67},{4,68},{5,69},{6,70},{7,71},{8,72},{9,... | collective-permute-start | bytes 294920 | tf_op jit(solution)/shard_map/ppermute | solution.py:93
  103.0 10.6 %collective-permute-start.2 = (bf16[128,384]{1,0:T(8,128)(2,1)S(1)}, bf16[128,384]{1,0:T(8,128)(2,1)S(1)}, u32[]{:S(2)}, u32[]{:S(2)}) collective-permute-start(bf16[128,384]{1,0:T(8,128)(2,1)S(1)} %get-tuple-element.12), channel_id=1, source_target_pairs={{0,32},{1,33},{2,34},{3,35},{4,36},{5,37},{6,38},{7,39},{8,40},{9,... | collective-permute-start | bytes 294920 | tf_op jit(solution)/shard_map/ppermute | solution.py:93
  104.9 20.6 %collective-permute-start.11 = (bf16[512,384]{1,0:T(8,128)(2,1)S(1)}, bf16[512,384]{1,0:T(8,128)(2,1)S(1)}, u32[]{:S(2)}, u32[]{:S(2)}) collective-permute-start(bf16[512,384]{1,0:T(8,128)(2,1)S(1)} %pad_maximum_fusion.1.refs_4_), channel_id=1, source_target_pairs={{0,32},{1,33},{2,34},{3,35},{4,36},{5,37},{6,38},{7,39},{8,40},{9,... | collective-permute-start | bytes 1179656 | tf_op jit(solution)/shard_map/ppermute | solution.py:93
  109.1 17.2 %collective-permute-start.9 = (bf16[512,384]{1,0:T(8,128)(2,1)S(1)}, bf16[512,384]{1,0:T(8,128)(2,1)S(1)}, u32[]{:S(2)}, u32[]{:S(2)}) collective-permute-start(bf16[512,384]{1,0:T(8,128)(2,1)S(1)} %pad_maximum_fusion.1.refs_4_), channel_id=1, source_target_pairs={{0,96},{1,97},{2,98},{3,99},{4,100},{5,101},{6,102},{7,103},{8,104... | collective-permute-start | bytes 1179656 | tf_op jit(solution)/shard_map/ppermute | solution.py:93
  113.6 21.6 %collective-permute-start.3 = (bf16[512,384]{1,0:T(8,128)(2,1)S(1)}, bf16[512,384]{1,0:T(8,128)(2,1)S(1)}, u32[]{:S(2)}, u32[]{:S(2)}) collective-permute-start(bf16[512,384]{1,0:T(8,128)(2,1)S(1)} %pad_maximum_fusion.refs_0_), channel_id=1, source_target_pairs={{0,384},{1,385},{2,386},{3,387},{4,388},{5,389},{6,390},{7,391},{8... | collective-permute-start | bytes 1179656 | tf_op jit(solution)/shard_map/ppermute | solution.py:93
  118.6 17.4 %collective-permute-start.4 = (bf16[512,384]{1,0:T(8,128)(2,1)S(1)}, bf16[512,384]{1,0:T(8,128)(2,1)S(1)}, u32[]{:S(2)}, u32[]{:S(2)}) collective-permute-start(bf16[512,384]{1,0:T(8,128)(2,1)S(1)} %pad_maximum_fusion.refs_0_), channel_id=1, source_target_pairs={{0,256},{1,257},{2,258},{3,259},{4,260},{5,261},{6,262},{7,263},{8... | collective-permute-start | bytes 1179656 | tf_op jit(solution)/shard_map/ppermute | solution.py:93
  121.9 19.1 %collective-permute-start.5 = (bf16[512,384]{1,0:T(8,128)(2,1)S(1)}, bf16[512,384]{1,0:T(8,128)(2,1)}, u32[]{:S(2)}, u32[]{:S(2)}) collective-permute-start(bf16[512,384]{1,0:T(8,128)(2,1)S(1)} %pad_maximum_fusion.refs_0_), channel_id=1, source_target_pairs={{0,128},{1,129},{2,130},{3,131},{4,132},{5,133},{6,134},{7,135},{8... | collective-permute-start | bytes 1179656 | tf_op jit(solution)/shard_map/ppermute | solution.py:93
  140.9 1.0 copy-start.1
  141.9 1.0 copy-start.3
  142.9 1.0 copy-start.7
  143.9 1.0 copy-start.9
  146.9 1.0 copy-start.15
  (10 other events, 8.1 us)

commit v2 on v1

v2 whole, which is shorter than its diff:
```python
import math

import jax
import jax.numpy as jnp
import numpy as np
from jax import lax
from jax.experimental import pallas as pl
from jax.experimental.pallas import tpu as pltpu
from jax.sharding import Mesh
from jax.sharding import PartitionSpec as P

HD = 128
EVERY = ("y", "x", "zl", "zh", "core")
SIZES = (4, 4, 8, 2, 2)
ROWS = 128
SCALE = HD**-0.5 * math.log2(math.e)
NT = (((1,), (1,)), ((), ()))
F32 = jnp.float32
BF16 = jnp.bfloat16
ANY = pl.BlockSpec(memory_space=pl.ANY)
SMEM = pl.BlockSpec(memory_space=pltpu.SMEM)


def pack(at_ref, q_ref, k_ref, v_ref, ks_ref, vs_ref, *refs):
    parts, pooled_ref, sem = refs[0:4], refs[4], refs[5]
    mine = ks_ref.shape[1]
    copies = []
    for j in range(pooled_ref.shape[0]):
        copies.append((ks_ref, pooled_ref.at[j, :, 0:mine]))
        copies.append((vs_ref, pooled_ref.at[j, :, mine : 2 * mine]))
    for p, part in enumerate(parts):
        cols = pl.ds(pl.multiple_of(at_ref[p] * mine, HD), mine)
        for t, ref in enumerate((q_ref, k_ref, v_ref)):
            copies.append((ref.at[:, cols], part.at[:, t * mine : (t + 1) * mine]))
    copies = [pltpu.make_async_copy(a, b, sem.at[i]) for i, (a, b) in enumerate(copies)]
    for c in copies:
        c.start()
    for c in copies:
        c.wait()


def attend(at_ref, p0, p1, p2, p3, pool_ref, out_ref, part_ref, keys_ref, s_ref, res_ref, sem_p, sem_k, sem_o):
    tokens = p0.shape[0]
    mine = p0.shape[1] // 3
    heads = mine // HD
    blocks, block = pool_ref.shape[0], pool_ref.shape[1]
    here = at_ref[5]
    loads = [pltpu.make_async_copy(r, part_ref.at[i], sem_p.at[i]) for i, r in enumerate((p0, p1, p2, p3))]
    for c in loads:
        c.start()
    for j in range(blocks):
        pltpu.make_async_copy(
            pool_ref.at[lax.rem(here + j, blocks)], keys_ref.at[pl.ds(j * block, block)], sem_k.at[j]
        ).start()
    for c in loads:
        c.wait()
    for j in range(blocks):
        pltpu.make_async_copy(pool_ref.at[0], keys_ref.at[pl.ds(j * block, block)], sem_k.at[j]).wait()
    first = at_ref[4]
    cols = lax.broadcasted_iota(jnp.int32, (ROWS, block), 1)
    own = (cols >= first) & (cols < first + 16)
    chunk = 512
    stale = blocks * block

    def rows_step(i, carry):
        for h in range(heads):
            cs = slice(h * HD, (h + 1) * HD)
            ks = slice(mine + h * HD, mine + (h + 1) * HD)
            vs = slice(2 * mine + h * HD, 2 * mine + (h + 1) * HD)
            vcs = slice(mine + h * HD, mine + (h + 1) * HD)
            q = part_ref[i, :, cs]
            top = jnp.full((ROWS, HD), -jnp.inf, F32)
            for c in range(0, stale, chunk):
                s = lax.dot_general(q, keys_ref[c : c + chunk, cs], NT, preferred_element_type=F32)
                for d in range(0, chunk, HD):
                    piece = s[:, d : d + HD]
                    if c + d == 0:
                        piece = jnp.where(own, -jnp.inf, piece)
                    s_ref[h, :, c + d : c + d + HD] = piece
                    top = jnp.maximum(top, piece)
            for p in range(4):
                s = lax.dot_general(q, part_ref[p, :, ks], NT, preferred_element_type=F32)
                s_ref[h, :, stale + p * tokens : stale + (p + 1) * tokens] = s
                top = jnp.maximum(top, s)
            top = jnp.max(top, axis=1, keepdims=True) * SCALE
            sums = jnp.zeros((ROWS, HD), F32)
            acc = jnp.zeros((ROWS, HD), F32)
            for c in range(0, stale + 4 * tokens, chunk):
                w = jnp.exp2(s_ref[h, :, c : c + chunk] * SCALE - top)
                for d in range(0, chunk, HD):
                    sums = sums + w[:, d : d + HD]
                rounded = w.astype(BF16)
                if c < stale:
                    values = keys_ref[c : c + chunk, vcs]
                else:
                    values = jnp.concatenate([part_ref[p, :, vs] for p in range(4)], axis=0)
                acc = acc + jnp.dot(rounded, values, preferred_element_type=F32)
            total = jnp.sum(sums, axis=1, keepdims=True)
            res_ref[i, :, cs] = (acc / total).astype(BF16)
        pltpu.make_async_copy(res_ref.at[i], out_ref.at[at_ref[i]], sem_o.at[i]).start()
        return carry

    lax.fori_loop(0, 4, rows_step, 0)
    for i in range(4):
        pltpu.make_async_copy(res_ref.at[i], out_ref.at[0], sem_o.at[i]).wait()


def flips(zh, core):
    pairs = []
    for i in range(math.prod(SIZES)):
        place = list(np.unravel_index(i, SIZES))
        place[3] ^= zh
        place[4] ^= core
        pairs.append((i, int(np.ravel_multi_index(place, SIZES))))
    return pairs


def local(q_fresh, k_fresh, v_fresh, k_stale, v_stale):
    tokens, width = q_fresh.shape
    pooled, mine = k_stale.shape
    heads = mine // HD
    zh, core = lax.axis_index("zh"), lax.axis_index("core")
    zl, here = lax.axis_index("zl"), lax.axis_index("y") * 4 + lax.axis_index("x")
    places = [zh * 2 + core, zh * 2 + 1 - core, (1 - zh) * 2 + core, (1 - zh) * 2 + 1 - core, zl * pooled, here]
    at = jnp.stack(places).astype(jnp.int32)

    part = jax.ShapeDtypeStruct((tokens, 3 * mine), BF16)
    *parts, copies = pl.pallas_call(
        pack,
        out_shape=(part, part, part, part, jax.ShapeDtypeStruct((8, pooled, 2 * mine), BF16)),
        in_specs=[SMEM] + [ANY] * 5,
        out_specs=(ANY,) * 5,
        scratch_shapes=[pltpu.SemaphoreType.DMA((28,))],
        cost_estimate=pl.CostEstimate(flops=0, bytes_accessed=3 << 20, transcendentals=0),
        name="pack",
    )(at, q_fresh, k_fresh, v_fresh, k_stale, v_stale)
    line = lax.all_to_all(copies, "zl", split_axis=0, concat_axis=0).reshape(8 * pooled, 2 * mine)
    arrived = [
        parts[0],
        lax.ppermute(parts[1], EVERY, flips(0, 1)),
        lax.ppermute(parts[2], EVERY, flips(1, 0)),
        lax.ppermute(parts[3], EVERY, flips(1, 1)),
    ]
    pool = lax.all_to_all(
        jnp.broadcast_to(line[None], (16, 8 * pooled, 2 * mine)), ("y", "x"), split_axis=0, concat_axis=0
    )
    total_keys = 16 * 8 * pooled + 4 * tokens
    out = pl.pallas_call(
        attend,
        out_shape=jax.ShapeDtypeStruct((4, tokens, mine), BF16),
        in_specs=[SMEM] + [ANY] * 5,
        out_specs=ANY,
        scratch_shapes=[
            pltpu.VMEM((4, tokens, 3 * mine), BF16),
            pltpu.VMEM((16 * 8 * pooled, 2 * mine), BF16),
            pltpu.VMEM((heads, ROWS, total_keys), F32),
            pltpu.VMEM((4, tokens, mine), BF16),
            pltpu.SemaphoreType.DMA((4,)),
            pltpu.SemaphoreType.DMA((16,)),
            pltpu.SemaphoreType.DMA((4,)),
        ],
        compiler_params=pltpu.CompilerParams(vmem_limit_bytes=40 << 20),
        cost_estimate=pl.CostEstimate(
            flops=4 * 4 * tokens * heads * total_keys * HD,
            bytes_accessed=6 << 20,
            transcendentals=4 * tokens * heads * total_keys,
        ),
        name="attend",
    )(at, *arrived, pool)
    back = lax.all_to_all(out, ("zh", "core"), split_axis=0, concat_axis=0)
    return back.transpose(1, 0, 2).reshape(tokens, width)


def solution(mesh):
    fine = Mesh(mesh.devices.reshape(SIZES), EVERY)
    whole = P(EVERY, None)
    part = P(("y", "x", "zl"), ("zh", "core"))
    return jax.shard_map(
        local,
        mesh=fine,
        in_specs=(whole, whole, whole, part, part),
        out_specs=whole,
        check_vma=False,
    )
```

time: 194 us -> 189 us (0.974)
  the two profiles are of different devices: /device:TPU:32 before, /device:TPU:34 now
where the time goes in v2:
time: 189 us; the launch traced here: 188 us
  Pallas kernels  58 us (31%)
  blocking collectives  49.6 us (26%)
  waiting for transfers between devices  47.8 us (25%)
  starting transfers between devices  23.9 us (13%)
  local copies, waits for them, and re-layouts  8.7 us (5%)
    pallas_call x1, Pallas kernels, local(): pl.pallas_call(pack, out_shape=(part, part, part, part, jax.ShapeDtypeStr...  43.7 us
    ppermute x1, waiting for transfers between devices, local(): lax.ppermute(parts[2], EVERY, flips(1, 0))  42.3 us
    all_to_all x1, blocking collectives, local(): lax.all_to_all(copies, 'zl', split_axis=0, concat_axis=0)  26.2 us
    all_to_all x1, blocking collectives, local(): back = lax.all_to_all(out, ('zh', 'core'), split_axis=0, concat_axis=0)  23.4 us
    pallas_call x1, Pallas kernels, local(): pl.pallas_call(attend, out_shape=jax.ShapeDtypeStruct((4, tokens, mine),...  14.3 us
    ppermute x1, starting transfers between devices, local(): lax.ppermute(parts[2], EVERY, flips(1, 0))  8.22 us
    all_to_all x1, starting transfers between devices, local(): lax.all_to_all(jnp.broadcast_to(line[None], (16, 8 * pooled, 2 * mine)),...  7.61 us
    ppermute x1, starting transfers between devices, local(): lax.ppermute(parts[3], EVERY, flips(1, 1))  6.16 us
  transfers between devices with their start and end apart: 4, of which 2 were waited for; matrix products, arithmetic and copies ran while one was open for 0% of the time, Pallas kernels for 0%

profile of v2, /device:TPU:34, one launch (start us, length us, event | category | flops | bytes accessed | tf_op | source)
XLA Modules:
  0.0 188.2 jit_solution(17978999207435257164)
XLA Ops:
  0.0 0.6 stack.27.at_ref
  0.6 43.7 %pack.1 = (bf16[128,1152]{1,0:T(8,128)(2,1)}, bf16[128,1152]{1,0:T(8,128)(2,1)}, bf16[128,1152]{1,0:T(8,128)(2,1)}, bf16[128,1152]{1,0:T(8,128)(2,1)}, bf16[8,16,768]{2,1,0:T(8,128)(2,1)}) custom-call(s32[6]{0:T(128)} %stack.27.at_ref, bf16[128,1536]{1,0:T(8,128)(2,1)} %q_ref.1, bf16[128,1536]{1,0:T(8,128)(2,1)} %k_ref.1, bf16[128,1536]{1,0:T(8,128)(2,1)} %v_ref.1, ...), custom_call_target="tpu_custom_call" | custom-call | bytes 3145728 | tf_op jit(solution)/shard_map/pack/pallas_call | solution.py:128
  44.3 26.2 %all_to_all.15 = bf16[8,16,768]{2,1,0:T(8,128)(2,1)S(1)} all-to-all(bf16[8,16,768]{2,1,0:T(8,128)(2,1)} %get-tuple-element.14), channel_id=1, replica_groups=mesh['y'=4,'x'=4,'zl'=8,'zh'=2,'core'=2] {'zl'}, dimensions={0} | all-to-all | bytes 393216 | tf_op jit(solution)/shard_map/all_to_all | solution.py:137
  70.6 1.9 %broadcast_in_dim.8 = bf16[16,128,768]{2,1,0:T(8,128)(2,1)} broadcast(bf16[128,768]{1,0:T(8,128)(2,1)S(1)} %bitcast.11), dimensions={1,2} | broadcast | bytes 3342336 | tf_op jit(solution)/shard_map/broadcast_in_dim | solution.py:145
  72.5 7.6 %all-to-all-start.1 = ((bf16[16,128,768]{2,1,0:T(8,128)(2,1)}), bf16[16,128,768]{2,1,0:T(8,128)(2,1)S(1)}, u32[]{:S(2)}, u32[]{:S(2)}) async-start(bf16[16,128,768]{2,1,0:T(8,128)(2,1)} %broadcast_in_dim.8), calls=%async_computation.1 | async-start | bytes 6291456 | tf_op jit(solution)/shard_map/all_to_all | solution.py:144
  80.1 1.9 %collective-permute-start = (bf16[128,1152]{1,0:T(8,128)(2,1)}, bf16[128,1152]{1,0:T(8,128)(2,1)S(1)}, u32[]{:S(2)}, u32[]{:S(2)}) collective-permute-start(bf16[128,1152]{1,0:T(8,128)(2,1)} %get-tuple-element.11), channel_id=1, source_target_pairs={{0,1},{1,0},{2,3},{3,2},{4,5},{5,4},{6,7},{7,6},{8,9},{9,8},{10,11... | collective-permute-start | bytes 884744 | tf_op jit(solution)/shard_map/ppermute | solution.py:140
  82.0 8.2 %collective-permute-start.1 = (bf16[128,1152]{1,0:T(8,128)(2,1)}, bf16[128,1152]{1,0:T(8,128)(2,1)S(1)}, u32[]{:S(2)}, u32[]{:S(2)}) collective-permute-start(bf16[128,1152]{1,0:T(8,128)(2,1)} %get-tuple-element.12), channel_id=1, source_target_pairs={{0,2},{1,3},{2,0},{3,1},{4,6},{5,7},{6,4},{7,5},{8,10},{9,11},{10,... | collective-permute-start | bytes 884744 | tf_op jit(solution)/shard_map/ppermute | solution.py:141
  90.3 6.2 %collective-permute-start.2 = (bf16[128,1152]{1,0:T(8,128)(2,1)}, bf16[128,1152]{1,0:T(8,128)(2,1)S(1)}, u32[]{:S(2)}, u32[]{:S(2)}) collective-permute-start(bf16[128,1152]{1,0:T(8,128)(2,1)} %get-tuple-element.13), channel_id=1, source_target_pairs={{0,3},{1,2},{2,1},{3,0},{4,7},{5,6},{6,5},{7,4},{8,11},{9,10},{10,... | collective-permute-start | bytes 884744 | tf_op jit(solution)/shard_map/ppermute | solution.py:142
  96.4 0.0 collective-permute-done.p1
  96.4 0.0 copy-start.2
  96.4 0.7 copy-done.2
  97.1 42.3 %collective-permute-done.1.p2 = bf16[128,1152]{1,0:T(8,128)(2,1)S(1)} collective-permute-done((bf16[128,1152]{1,0:T(8,128)(2,1)}, bf16[128,1152]{1,0:T(8,128)(2,1)S(1)}, u32[]{:S(2)}, u32[]{:S(2)}) %collective-permute-start.1) | collective-permute-done | bytes 294944 | tf_op jit(solution)/shard_map/ppermute | solution.py:141
  139.4 0.7 copy-done.4
  140.1 5.5 %collective-permute-done.2.p3 = bf16[128,1152]{1,0:T(8,128)(2,1)S(1)} collective-permute-done((bf16[128,1152]{1,0:T(8,128)(2,1)}, bf16[128,1152]{1,0:T(8,128)(2,1)S(1)}, u32[]{:S(2)}, u32[]{:S(2)}) %collective-permute-start.2) | collective-permute-done | bytes 294944 | tf_op jit(solution)/shard_map/ppermute | solution.py:142
  145.7 0.7 copy-done.6
  146.4 0.0 all-to-all-done.1.pool_ref
  146.4 0.0 copy-done.1
  146.4 1.0 copy-done.3
  147.3 1.0 copy-done.5
  148.3 1.0 copy-done.7
  149.3 14.3 %attend.1 = bf16[4,128,384]{2,1,0:T(8,128)(2,1)S(1)} custom-call(s32[6]{0:T(128)S(1)} %copy-done, bf16[128,1152]{1,0:T(8,128)(2,1)S(1)} %copy-done.1, bf16[128,1152]{1,0:T(8,128)(2,1)S(1)} %copy-done.3, bf16[128,1152]{1,0:T(8,128)(2,1)S(1)} %copy-done.5, bf16[128,1152]{1,0:T(8,128)(2,1)S(1)} %copy-done.7, bf16[16,128,768]{2,1,0:T(8,128)(2,1)S(1)} %all-to-all-done.1.pool_ref), custom_call_target="tpu_custom_call" | custom-call | flops 2013265920 | bytes 6291456 | tf_op jit(solution)/shard_map/attend/pallas_call | solution.py:148
  163.6 23.4 %all_to_all.16 = bf16[4,128,384]{2,1,0:T(8,128)(2,1)S(1)} all-to-all(bf16[4,128,384]{2,1,0:T(8,128)(2,1)S(1)} %attend.1), channel_id=1, replica_groups=mesh['y'=4,'x'=4,'zl'=8,'zh'=2,'core'=2] {'zh','core'}, dimensions={0} | all-to-all | bytes 786432 | tf_op jit(solution)/shard_map/all_to_all | solution.py:170
  187.0 0.2 copy.6
  187.3 0.9 copy.7
  (8 shorter events, 0.0 us)
Async XLA Ops:
  72.5 73.9 %copy-start = (s32[6]{0:T(128)S(1)}, s32[6]{0:T(128)}, u32[]{:S(2)}) copy-start(s32[6]{0:T(128)} %stack.27.at_ref) | copy-start | bytes 76
  72.5 73.9 %copy-start.1 = (bf16[128,1152]{1,0:T(8,128)(2,1)S(1)}, bf16[128,1152]{1,0:T(8,128)(2,1)}, u32[]{:S(2)}) copy-start(bf16[128,1152]{1,0:T(8,128)(2,1)} %get-tuple-element.10.p0) | copy-start | bytes 884740
  72.5 73.9 %all-to-all-start.1 = ((bf16[16,128,768]{2,1,0:T(8,128)(2,1)}), bf16[16,128,768]{2,1,0:T(8,128)(2,1)S(1)}, u32[]{:S(2)}, u32[]{:S(2)}) async-start(bf16[16,128,768]{2,1,0:T(8,128)(2,1)} %broadcast_in_dim.8), calls=%async_computation.1 | async-start | bytes 6291456 | tf_op jit(solution)/shard_map/all_to_all | solution.py:144
  80.1 16.3 %collective-permute-start = (bf16[128,1152]{1,0:T(8,128)(2,1)}, bf16[128,1152]{1,0:T(8,128)(2,1)S(1)}, u32[]{:S(2)}, u32[]{:S(2)}) collective-permute-start(bf16[128,1152]{1,0:T(8,128)(2,1)} %get-tuple-element.11), channel_id=1, source_target_pairs={{0,1},{1,0},{2,3},{3,2},{4,5},{5,4},{6,7},{7,6},{8,9},{9,8},{10,11... | collective-permute-start | bytes 884744 | tf_op jit(solution)/shard_map/ppermute | solution.py:140
  82.0 57.4 %collective-permute-start.1 = (bf16[128,1152]{1,0:T(8,128)(2,1)}, bf16[128,1152]{1,0:T(8,128)(2,1)S(1)}, u32[]{:S(2)}, u32[]{:S(2)}) collective-permute-start(bf16[128,1152]{1,0:T(8,128)(2,1)} %get-tuple-element.12), channel_id=1, source_target_pairs={{0,2},{1,3},{2,0},{3,1},{4,6},{5,7},{6,4},{7,5},{8,10},{9,11},{10,... | collective-permute-start | bytes 884744 | tf_op jit(solution)/shard_map/ppermute | solution.py:141
  90.3 55.4 %collective-permute-start.2 = (bf16[128,1152]{1,0:T(8,128)(2,1)}, bf16[128,1152]{1,0:T(8,128)(2,1)S(1)}, u32[]{:S(2)}, u32[]{:S(2)}) collective-permute-start(bf16[128,1152]{1,0:T(8,128)(2,1)} %get-tuple-element.13), channel_id=1, source_target_pairs={{0,3},{1,2},{2,1},{3,0},{4,7},{5,6},{6,5},{7,4},{8,11},{9,10},{10,... | collective-permute-start | bytes 884744 | tf_op jit(solution)/shard_map/ppermute | solution.py:142
  96.4 0.7 copy-start.2
  139.4 0.7 copy-start.4
  145.7 0.7 copy-start.6
  146.4 1.0 copy-start.3
  147.3 1.0 copy-start.5
  148.3 1.0 copy-start.7

commit v3 on v2

v3 whole, which is shorter than its diff:
```python
import math

import jax
import jax.numpy as jnp
import numpy as np
from jax import lax
from jax.experimental import pallas as pl
from jax.experimental.pallas import tpu as pltpu
from jax.sharding import Mesh
from jax.sharding import PartitionSpec as P

HD = 128
EVERY = ("y", "x", "zl", "zh", "core")
SIZES = (4, 4, 8, 2, 2)
ROWS = 128
SCALE = HD**-0.5 * math.log2(math.e)
NT = (((1,), (1,)), ((), ()))
F32 = jnp.float32
BF16 = jnp.bfloat16
ANY = pl.BlockSpec(memory_space=pl.ANY)
SMEM = pl.BlockSpec(memory_space=pltpu.SMEM)


def pack(at_ref, qa, ka, va, ksa, vsa, own_ref, near_ref, qz_ref, kvz_ref, pooled_ref, *scratch):
    q_ref, k_ref, v_ref, ks_ref, vs_ref, sem = scratch
    loads = zip((qa, ka, va, ksa, vsa), scratch[:5])
    loads = [pltpu.make_async_copy(a, b, sem.at[i]) for i, (a, b) in enumerate(loads)]
    for c in loads:
        c.start()
    for c in loads:
        c.wait()
    mine = ks_ref.shape[1]

    def cols(p):
        return pl.ds(pl.multiple_of(at_ref[p] * mine, HD), mine)

    for t, ref in enumerate((q_ref, k_ref, v_ref)):
        own_ref[:, t * mine : (t + 1) * mine] = ref[:, cols(0)]
        near_ref[:, t * mine : (t + 1) * mine] = ref[:, cols(1)]
    for r in range(2):
        qz_ref[r] = q_ref[:, cols(2 + r)]
        kvz_ref[r, :, 0:mine] = k_ref[:, cols(2 + r)]
        kvz_ref[r, :, mine : 2 * mine] = v_ref[:, cols(2 + r)]
    for j in range(pooled_ref.shape[0]):
        pooled_ref[j, :, 0:mine] = ks_ref[...]
        pooled_ref[j, :, mine : 2 * mine] = vs_ref[...]


def spread(line_ref, near_ref, qz_ref, out_ref):
    out_ref[0] = line_ref[...]


def attend(at_ref, own_ref, near_ref, qz_ref, kvz_ref, qc_ref, kvc_ref, pool_ref, out_ref, *scratch):
    q_ref, keys_ref, values_ref, s_ref, res_ref, sem_f, sem_k, sem_o = scratch
    tokens, mine = res_ref.shape[1:]
    heads = mine // HD
    blocks, block = pool_ref.shape[0], pool_ref.shape[1]
    stale = blocks * block
    here = at_ref[5]
    fresh = []
    for i, ref in enumerate((own_ref, near_ref)):
        fresh += [(i, t, ref.at[:, t * mine : (t + 1) * mine]) for t in range(3)]
    fresh += [(2, 0, qz_ref.at[0]), (2, 1, kvz_ref.at[0, :, 0:mine]), (2, 2, kvz_ref.at[0, :, mine : 2 * mine])]
    fresh += [(3, 0, qc_ref.at[1]), (3, 1, kvc_ref.at[1, :, 0:mine]), (3, 2, kvc_ref.at[1, :, mine : 2 * mine])]
    loads = []
    for n, (i, t, ref) in enumerate(fresh):
        rows = pl.ds(stale + i * tokens, tokens)
        to = (q_ref.at[i], keys_ref.at[rows], values_ref.at[rows])[t]
        loads.append(pltpu.make_async_copy(ref, to, sem_f.at[n]))
    for j in range(blocks):
        src = pool_ref.at[lax.rem(here + j, blocks)]
        rows = pl.ds(j * block, block)
        loads.append(pltpu.make_async_copy(src.at[:, 0:mine], keys_ref.at[rows], sem_k.at[j]))
        loads.append(pltpu.make_async_copy(src.at[:, mine : 2 * mine], values_ref.at[rows], sem_k.at[blocks + j]))
    for c in loads:
        c.start()
    for c in loads:
        c.wait()
    first = at_ref[4]
    cols = lax.broadcasted_iota(jnp.int32, (ROWS, block), 1)
    own = (cols >= first) & (cols < first + 16)
    chunk = 512
    total_keys = keys_ref.shape[0]

    def rows_step(i, carry):
        for h in range(heads):
            cs = slice(h * HD, (h + 1) * HD)
            q = q_ref[i, :, cs]
            top = jnp.full((ROWS, HD), -jnp.inf, F32)
            for c in range(0, total_keys, chunk):
                s = lax.dot_general(q, keys_ref[c : c + chunk, cs], NT, preferred_element_type=F32)
                for d in range(0, chunk, HD):
                    piece = s[:, d : d + HD]
                    if c + d == 0:
                        piece = jnp.where(own, -jnp.inf, piece)
                    s_ref[h, :, c + d : c + d + HD] = piece
                    top = jnp.maximum(top, piece)
            top = jnp.max(top, axis=1, keepdims=True) * SCALE
            sums = jnp.zeros((ROWS, HD), F32)
            acc = jnp.zeros((ROWS, HD), F32)
            for c in range(0, total_keys, chunk):
                w = jnp.exp2(s_ref[h, :, c : c + chunk] * SCALE - top)
                for d in range(0, chunk, HD):
                    sums = sums + w[:, d : d + HD]
                acc = acc + jnp.dot(w.astype(BF16), values_ref[c : c + chunk, cs], preferred_element_type=F32)
            total = jnp.sum(sums, axis=1, keepdims=True)
            res_ref[i, :, cs] = (acc / total).astype(BF16)
        pltpu.make_async_copy(res_ref.at[i], out_ref.at[at_ref[i]], sem_o.at[i]).start()
        return carry

    lax.fori_loop(0, 4, rows_step, 0)
    for i in range(4):
        pltpu.make_async_copy(res_ref.at[i], out_ref.at[0], sem_o.at[i]).wait()


def flips(zh, core):
    pairs = []
    for i in range(math.prod(SIZES)):
        place = list(np.unravel_index(i, SIZES))
        place[3] ^= zh
        place[4] ^= core
        pairs.append((i, int(np.ravel_multi_index(place, SIZES))))
    return pairs


def local(q_fresh, k_fresh, v_fresh, k_stale, v_stale):
    tokens, width = q_fresh.shape
    pooled, mine = k_stale.shape
    heads = mine // HD
    zh, core = lax.axis_index("zh"), lax.axis_index("core")
    zl, here = lax.axis_index("zl"), lax.axis_index("y") * 4 + lax.axis_index("x")
    places = [zh * 2 + core, zh * 2 + 1 - core, (1 - zh) * 2 + core, (1 - zh) * 2 + 1 - core, zl * pooled, here]
    at = jnp.stack(places).astype(jnp.int32)

    part = jax.ShapeDtypeStruct((tokens, 3 * mine), BF16)
    parts = (
        part,
        part,
        jax.ShapeDtypeStruct((2, tokens, mine), BF16),
        jax.ShapeDtypeStruct((2, tokens, 2 * mine), BF16),
        jax.ShapeDtypeStruct((8, pooled, 2 * mine), BF16),
    )
    own, near, qz, kvz, copies = pl.pallas_call(
        pack,
        out_shape=parts,
        in_specs=[SMEM] + [ANY] * 5,
        out_specs=(pl.BlockSpec(),) * 5,
        scratch_shapes=[pltpu.VMEM((tokens, width), BF16)] * 3
        + [pltpu.VMEM((pooled, mine), BF16)] * 2
        + [pltpu.SemaphoreType.DMA((5,))],
        cost_estimate=pl.CostEstimate(flops=0, bytes_accessed=3 << 20, transcendentals=0),
        name="pack",
    )(at, q_fresh, k_fresh, v_fresh, k_stale, v_stale)
    line = lax.all_to_all(copies, "zl", split_axis=0, concat_axis=0).reshape(8 * pooled, 2 * mine)
    near = lax.ppermute(near, EVERY, flips(0, 1))
    qz = lax.ppermute(qz, EVERY, flips(1, 0))
    kvz = lax.ppermute(kvz, EVERY, flips(1, 0))
    block = (1, 8 * pooled, 2 * mine)
    planes = pl.pallas_call(
        spread,
        out_shape=jax.ShapeDtypeStruct((16, *block[1:]), BF16),
        grid=(16,),
        in_specs=[pl.BlockSpec(block[1:], lambda i: (0, 0)), ANY, ANY],
        out_specs=pl.BlockSpec(block, lambda i: (i, 0, 0)),
        compiler_params=pltpu.CompilerParams(vmem_limit_bytes=60 << 20),
        cost_estimate=pl.CostEstimate(flops=0, bytes_accessed=3 << 20, transcendentals=0),
        name="spread",
    )(line, near, qz)
    qc = lax.ppermute(qz, EVERY, flips(0, 1))
    kvc = lax.ppermute(kvz, EVERY, flips(0, 1))
    pool = lax.all_to_all(planes, ("y", "x"), split_axis=0, concat_axis=0)
    total_keys = 16 * 8 * pooled + 4 * tokens
    out = pl.pallas_call(
        attend,
        out_shape=jax.ShapeDtypeStruct((4, tokens, mine), BF16),
        in_specs=[SMEM] + [ANY] * 7,
        out_specs=ANY,
        scratch_shapes=[
            pltpu.VMEM((4, tokens, mine), BF16),
            pltpu.VMEM((total_keys, mine), BF16),
            pltpu.VMEM((total_keys, mine), BF16),
            pltpu.VMEM((heads, ROWS, total_keys), F32),
            pltpu.VMEM((4, tokens, mine), BF16),
            pltpu.SemaphoreType.DMA((12,)),
            pltpu.SemaphoreType.DMA((32,)),
            pltpu.SemaphoreType.DMA((4,)),
        ],
        compiler_params=pltpu.CompilerParams(vmem_limit_bytes=60 << 20),
        cost_estimate=pl.CostEstimate(
            flops=4 * 4 * tokens * heads * total_keys * HD,
            bytes_accessed=6 << 20,
            transcendentals=4 * tokens * heads * total_keys,
        ),
        name="attend",
    )(at, own, near, qz, kvz, qc, kvc, pool)
    back = lax.all_to_all(out, ("zh", "core"), split_axis=0, concat_axis=0)
    return back.transpose(1, 0, 2).reshape(tokens, width)


def solution(mesh):
    fine = Mesh(mesh.devices.reshape(SIZES), EVERY)
    whole = P(EVERY, None)
    part = P(("y", "x", "zl"), ("zh", "core"))
    return jax.shard_map(
        local,
        mesh=fine,
        in_specs=(whole, whole, whole, part, part),
        out_specs=whole,
        check_vma=False,
    )
```

time: 189 us -> 152 us (0.80)
  the two profiles are of different devices: /device:TPU:34 before, /device:TPU:161 now
where the time goes in v3:
time: 152 us
  waiting for transfers between devices  55.8 us (37%)
  starting transfers between devices  40.6 us (27%)
  blocking collectives  29.1 us (19%)
  Pallas kernels  22 us (14%)
  local copies, waits for them, and re-layouts  4.32 us (3%)
    ppermute x1, waiting for transfers between devices, local(): kvz = lax.ppermute(kvz, EVERY, flips(1, 0))  31.6 us
    all_to_all x1, blocking collectives, local(): back = lax.all_to_all(out, ('zh', 'core'), split_axis=0, concat_axis=0)  29.1 us
    ppermute x1, waiting for transfers between devices, local(): qz = lax.ppermute(qz, EVERY, flips(1, 0))  22 us
    pallas_call x1, Pallas kernels, local(): pl.pallas_call(attend, out_shape=jax.ShapeDtypeStruct((4, tokens, mine),...  12.3 us
    all_to_all x1, starting transfers between devices, local(): lax.all_to_all(copies, 'zl', split_axis=0, concat_axis=0)  10.3 us
    ppermute x1, starting transfers between devices, local(): kvz = lax.ppermute(kvz, EVERY, flips(1, 0))  8.02 us
    ppermute x1, starting transfers between devices, local(): qz = lax.ppermute(qz, EVERY, flips(1, 0))  7.94 us
    all_to_all x1, starting transfers between devices, local(): pool = lax.all_to_all(planes, ('y', 'x'), split_axis=0, concat_axis=0)  6.89 us
  transfers between devices with their start and end apart: 7, of which 4 were waited for; matrix products, arithmetic and copies ran while one was open for 0% of the time, Pallas kernels for 0%

profile of v3, /device:TPU:161, one launch (start us, length us, event | category | flops | bytes accessed | tf_op | source)
XLA Modules:
  0.0 151.9 jit_solution(7039733162229900612)
XLA Ops:
  0.0 0.7 stack.27.at_ref
  0.7 3.1 %pack.1 = (bf16[128,1152]{1,0:T(8,128)(2,1)}, bf16[128,1152]{1,0:T(8,128)(2,1)}, bf16[2,128,384]{2,1,0:T(8,128)(2,1)}, bf16[2,128,768]{2,1,0:T(8,128)(2,1)}, bf16[8,16,768]{2,1,0:T(8,128)(2,1)}) custom-call(s32[6]{0:T(128)} %stack.27.at_ref, bf16[128,1536]{1,0:T(8,128)(2,1)} %qa.1, bf16[128,1536]{1,0:T(8,128)(2,1)} %ka.1, bf16[128,1536]{1,0:T(8,128)(2,1)} %va.1, ...), custom_call_target="tpu_custom_call" | custom-call | bytes 3145728 | tf_op jit(solution)/shard_map/pack/pallas_call | solution.py:143
  3.8 10.3 %all-to-all-start = ((bf16[8,16,768]{2,1,0:T(8,128)(2,1)}), bf16[8,16,768]{2,1,0:T(8,128)(2,1)S(1)}, u32[]{:S(2)}, u32[]{:S(2)}) async-start(bf16[8,16,768]{2,1,0:T(8,128)(2,1)} %get-tuple-element.14), calls=%async_computation | async-start | bytes 393216 | tf_op jit(solution)/shard_map/all_to_all | solution.py:154
  14.1 3.1 %collective-permute-start = (bf16[128,1152]{1,0:T(8,128)(2,1)}, bf16[128,1152]{1,0:T(8,128)(2,1)S(1)}, u32[]{:S(2)}, u32[]{:S(2)}) collective-permute-start(bf16[128,1152]{1,0:T(8,128)(2,1)} %get-tuple-element.11), channel_id=1, source_target_pairs={{0,1},{1,0},{2,3},{3,2},{4,5},{5,4},{6,7},{7,6},{8,9},{9,8},{10,11... | collective-permute-start | bytes 884744 | tf_op jit(solution)/shard_map/ppermute | solution.py:155
  17.2 7.9 %collective-permute-start.1 = (bf16[2,128,384]{2,1,0:T(8,128)(2,1)}, bf16[2,128,384]{2,1,0:T(8,128)(2,1)S(1)}, u32[]{:S(2)}, u32[]{:S(2)}) collective-permute-start(bf16[2,128,384]{2,1,0:T(8,128)(2,1)} %get-tuple-element.12), channel_id=1, source_target_pairs={{0,2},{1,3},{2,0},{3,1},{4,6},{5,7},{6,4},{7,5},{8,10},{9,11},{10,... | collective-permute-start | bytes 589832 | tf_op jit(solution)/shard_map/ppermute | solution.py:156
  25.1 22.0 %collective-permute-done.1.qz_ref = bf16[2,128,384]{2,1,0:T(8,128)(2,1)S(1)} collective-permute-done((bf16[2,128,384]{2,1,0:T(8,128)(2,1)}, bf16[2,128,384]{2,1,0:T(8,128)(2,1)S(1)}, u32[]{:S(2)}, u32[]{:S(2)}) %collective-permute-start.1) | collective-permute-done | bytes 196640 | tf_op jit(solution)/shard_map/ppermute | solution.py:156
  47.2 0.0 collective-permute-done.near_ref
  47.2 0.0 all-to-all-done
  47.2 0.7 copy-done.3
  47.9 0.1 copy-done.2
  48.0 0.1 copy-done.1
  48.0 6.6 %spread.1 = bf16[16,128,768]{2,1,0:T(8,128)(2,1)} custom-call(bf16[128,768]{1,0:T(8,128)(2,1)} %bitcast.11, bf16[128,1152]{1,0:T(8,128)(2,1)} %copy-done.2, bf16[2,128,384]{2,1,0:T(8,128)(2,1)} %copy-done.3), custom_call_target="tpu_custom_call" | custom-call | bytes 3145728 | tf_op jit(solution)/shard_map/spread/pallas_call | solution.py:159
  54.6 6.9 %all-to-all-start.1 = ((bf16[16,128,768]{2,1,0:T(8,128)(2,1)}), bf16[16,128,768]{2,1,0:T(8,128)(2,1)S(1)}, u32[]{:S(2)}, u32[]{:S(2)}) async-start(bf16[16,128,768]{2,1,0:T(8,128)(2,1)} %spread.1), calls=%async_computation.1 | async-start | bytes 6291456 | tf_op jit(solution)/shard_map/all_to_all | solution.py:171
  61.5 8.0 %collective-permute-start.2 = (bf16[2,128,768]{2,1,0:T(8,128)(2,1)}, bf16[2,128,768]{2,1,0:T(8,128)(2,1)S(1)}, u32[]{:S(2)}, u32[]{:S(2)}) collective-permute-start(bf16[2,128,768]{2,1,0:T(8,128)(2,1)} %get-tuple-element.13), channel_id=1, source_target_pairs={{0,2},{1,3},{2,0},{3,1},{4,6},{5,7},{6,4},{7,5},{8,10},{9,11},{10,... | collective-permute-start | bytes 1179656 | tf_op jit(solution)/shard_map/ppermute | solution.py:157
  69.5 31.6 %collective-permute-done.2.kvz_ref = bf16[2,128,768]{2,1,0:T(8,128)(2,1)S(1)} collective-permute-done((bf16[2,128,768]{2,1,0:T(8,128)(2,1)}, bf16[2,128,768]{2,1,0:T(8,128)(2,1)S(1)}, u32[]{:S(2)}, u32[]{:S(2)}) %collective-permute-start.2) | collective-permute-done | bytes 393248 | tf_op jit(solution)/shard_map/ppermute | solution.py:157
  101.2 2.4 %collective-permute-start.4 = (bf16[2,128,768]{2,1,0:T(8,128)(2,1)S(1)}, bf16[2,128,768]{2,1,0:T(8,128)(2,1)}, u32[]{:S(2)}, u32[]{:S(2)}) collective-permute-start(bf16[2,128,768]{2,1,0:T(8,128)(2,1)S(1)} %collective-permute-done.2.kvz_ref), channel_id=1, source_target_pairs={{0,1},{1,0},{2,3},{3,2},{4,5},{5,4},{6,7},{7,6},{8,9},{9,8},{10,11... | collective-permute-start | bytes 1179656 | tf_op jit(solution)/shard_map/ppermute | solution.py:170
  103.6 1.9 %collective-permute-start.3 = (bf16[2,128,384]{2,1,0:T(8,128)(2,1)S(1)}, bf16[2,128,384]{2,1,0:T(8,128)(2,1)S(1)}, u32[]{:S(2)}, u32[]{:S(2)}) collective-permute-start(bf16[2,128,384]{2,1,0:T(8,128)(2,1)S(1)} %copy-done.4), channel_id=1, source_target_pairs={{0,1},{1,0},{2,3},{3,2},{4,5},{5,4},{6,7},{7,6},{8,9},{9,8},{10,11... | collective-permute-start | bytes 589832 | tf_op jit(solution)/shard_map/ppermute | solution.py:169
  105.5 1.4 collective-permute-done.3.qc_ref
  106.9 0.8 all-to-all-done.1.pool_ref
  107.7 1.7 %copy-done = bf16[16,128,768]{2,1,0:T(8,128)(2,1)} copy-done((bf16[16,128,768]{2,1,0:T(8,128)(2,1)}, bf16[16,128,768]{2,1,0:T(8,128)(2,1)S(1)}, u32[]{:S(2)}) %copy-start) | copy-done | bytes 3145752
  109.3 12.3 %attend.1 = bf16[4,128,384]{2,1,0:T(8,128)(2,1)} custom-call(s32[6]{0:T(128)} %stack.27.at_ref, bf16[128,1152]{1,0:T(8,128)(2,1)} %get-tuple-element.10.own_ref, bf16[128,1152]{1,0:T(8,128)(2,1)} %copy-done.2, bf16[2,128,384]{2,1,0:T(8,128)(2,1)} %copy-done.3, bf16[2,128,768]{2,1,0:T(8,128)(2,1)} %copy-done.5, bf16[2,128,384]{2,1,0:T(8,128)(2,1)} %copy-done.6, ...), custom_call_target="tpu_custom_call" | custom-call | flops 2013265920 | bytes 6291456 | tf_op jit(solution)/shard_map/attend/pallas_call | solution.py:173
  121.6 29.1 %all_to_all.15 = bf16[4,128,384]{2,1,0:T(8,128)(2,1)S(1)} all-to-all(bf16[4,128,384]{2,1,0:T(8,128)(2,1)} %attend.1), channel_id=1, replica_groups=mesh['y'=4,'x'=4,'zl'=8,'zh'=2,'core'=2] {'zh','core'}, dimensions={0} | all-to-all | bytes 786432 | tf_op jit(solution)/shard_map/all_to_all | solution.py:196
  150.7 0.2 copy.6
  151.0 0.9 copy.7
  (11 shorter events, 0.0 us)
Async XLA Ops:
  3.8 43.4 %all-to-all-start = ((bf16[8,16,768]{2,1,0:T(8,128)(2,1)}), bf16[8,16,768]{2,1,0:T(8,128)(2,1)S(1)}, u32[]{:S(2)}, u32[]{:S(2)}) async-start(bf16[8,16,768]{2,1,0:T(8,128)(2,1)} %get-tuple-element.14), calls=%async_computation | async-start | bytes 393216 | tf_op jit(solution)/shard_map/all_to_all | solution.py:154
  14.1 33.1 %collective-permute-start = (bf16[128,1152]{1,0:T(8,128)(2,1)}, bf16[128,1152]{1,0:T(8,128)(2,1)S(1)}, u32[]{:S(2)}, u32[]{:S(2)}) collective-permute-start(bf16[128,1152]{1,0:T(8,128)(2,1)} %get-tuple-element.11), channel_id=1, source_target_pairs={{0,1},{1,0},{2,3},{3,2},{4,5},{5,4},{6,7},{7,6},{8,9},{9,8},{10,11... | collective-permute-start | bytes 884744 | tf_op jit(solution)/shard_map/ppermute | solution.py:155
  17.2 30.0 %collective-permute-start.1 = (bf16[2,128,384]{2,1,0:T(8,128)(2,1)}, bf16[2,128,384]{2,1,0:T(8,128)(2,1)S(1)}, u32[]{:S(2)}, u32[]{:S(2)}) collective-permute-start(bf16[2,128,384]{2,1,0:T(8,128)(2,1)} %get-tuple-element.12), channel_id=1, source_target_pairs={{0,2},{1,3},{2,0},{3,1},{4,6},{5,7},{6,4},{7,5},{8,10},{9,11},{10,... | collective-permute-start | bytes 589832 | tf_op jit(solution)/shard_map/ppermute | solution.py:156
  47.2 0.7 copy-start.3
  47.2 0.8 copy-start.2
  47.2 0.8 copy-start.1
  54.6 48.9 %copy-start.4 = (bf16[2,128,384]{2,1,0:T(8,128)(2,1)S(1)}, bf16[2,128,384]{2,1,0:T(8,128)(2,1)}, u32[]{:S(2)}) copy-start(bf16[2,128,384]{2,1,0:T(8,128)(2,1)} %copy-done.3) | copy-start | bytes 589828
  54.6 53.1 %all-to-all-start.1 = ((bf16[16,128,768]{2,1,0:T(8,128)(2,1)}), bf16[16,128,768]{2,1,0:T(8,128)(2,1)S(1)}, u32[]{:S(2)}, u32[]{:S(2)}) async-start(bf16[16,128,768]{2,1,0:T(8,128)(2,1)} %spread.1), calls=%async_computation.1 | async-start | bytes 6291456 | tf_op jit(solution)/shard_map/all_to_all | solution.py:171
  61.5 39.6 %collective-permute-start.2 = (bf16[2,128,768]{2,1,0:T(8,128)(2,1)}, bf16[2,128,768]{2,1,0:T(8,128)(2,1)S(1)}, u32[]{:S(2)}, u32[]{:S(2)}) collective-permute-start(bf16[2,128,768]{2,1,0:T(8,128)(2,1)} %get-tuple-element.13), channel_id=1, source_target_pairs={{0,2},{1,3},{2,0},{3,1},{4,6},{5,7},{6,4},{7,5},{8,10},{9,11},{10,... | collective-permute-start | bytes 1179656 | tf_op jit(solution)/shard_map/ppermute | solution.py:157
  101.2 5.7 %copy-start.5 = (bf16[2,128,768]{2,1,0:T(8,128)(2,1)}, bf16[2,128,768]{2,1,0:T(8,128)(2,1)S(1)}, u32[]{:S(2)}) copy-start(bf16[2,128,768]{2,1,0:T(8,128)(2,1)S(1)} %collective-permute-done.2.kvz_ref) | copy-start | bytes 1179652
  101.2 5.8 %collective-permute-start.4 = (bf16[2,128,768]{2,1,0:T(8,128)(2,1)S(1)}, bf16[2,128,768]{2,1,0:T(8,128)(2,1)}, u32[]{:S(2)}, u32[]{:S(2)}) collective-permute-start(bf16[2,128,768]{2,1,0:T(8,128)(2,1)S(1)} %collective-permute-done.2.kvz_ref), channel_id=1, source_target_pairs={{0,1},{1,0},{2,3},{3,2},{4,5},{5,4},{6,7},{7,6},{8,9},{9,8},{10,11... | collective-permute-start | bytes 1179656 | tf_op jit(solution)/shard_map/ppermute | solution.py:170
  103.6 3.3 %collective-permute-start.3 = (bf16[2,128,384]{2,1,0:T(8,128)(2,1)S(1)}, bf16[2,128,384]{2,1,0:T(8,128)(2,1)S(1)}, u32[]{:S(2)}, u32[]{:S(2)}) collective-permute-start(bf16[2,128,384]{2,1,0:T(8,128)(2,1)S(1)} %copy-done.4), channel_id=1, source_target_pairs={{0,1},{1,0},{2,3},{3,2},{4,5},{5,4},{6,7},{7,6},{8,9},{9,8},{10,11... | collective-permute-start | bytes 589832 | tf_op jit(solution)/shard_map/ppermute | solution.py:169
  106.9 0.8 copy-start.6
  107.7 1.7 %copy-start = (bf16[16,128,768]{2,1,0:T(8,128)(2,1)}, bf16[16,128,768]{2,1,0:T(8,128)(2,1)S(1)}, u32[]{:S(2)}) copy-start(bf16[16,128,768]{2,1,0:T(8,128)(2,1)S(1)} %all-to-all-done.1.pool_ref) | copy-start | bytes 9437188

commit v4 on v3

v4 whole, which is shorter than its diff:
```python
import math

import jax
import jax.numpy as jnp
import numpy as np
from jax import lax
from jax.experimental import pallas as pl
from jax.experimental.pallas import tpu as pltpu
from jax.sharding import Mesh
from jax.sharding import PartitionSpec as P

HD = 128
EVERY = ("y", "x", "zl", "zh", "core")
SIZES = (4, 4, 8, 2, 2)
ROWS = 128
SCALE = HD**-0.5 * math.log2(math.e)
NT = (((1,), (1,)), ((), ()))
F32 = jnp.float32
LIMIT = 60 << 20
FRESH_COST = 60 << 30
BF16 = jnp.bfloat16
ANY = pl.BlockSpec(memory_space=pl.ANY)
SMEM = pl.BlockSpec(memory_space=pltpu.SMEM)


def pack(at_ref, qa, ka, va, ksa, vsa, *refs):
    parts, pooled_ref = refs[0:4], refs[4]
    q_ref, k_ref, v_ref, ks_ref, vs_ref, sem = refs[5:]
    loads = zip((ksa, vsa, qa, ka, va), (ks_ref, vs_ref, q_ref, k_ref, v_ref))
    loads = [pltpu.make_async_copy(a, b, sem.at[i]) for i, (a, b) in enumerate(loads)]
    for c in loads:
        c.start()
    mine = ks_ref.shape[1]
    for c in loads[:2]:
        c.wait()
    for j in range(pooled_ref.shape[0]):
        pooled_ref[j, :, 0:mine] = ks_ref[...]
        pooled_ref[j, :, mine : 2 * mine] = vs_ref[...]
    for t, ref in enumerate((q_ref, k_ref, v_ref)):
        loads[2 + t].wait()
        for p, part in enumerate(parts):
            cols = pl.ds(pl.multiple_of(at_ref[p] * mine, HD), mine)
            part[:, t * mine : (t + 1) * mine] = ref[:, cols]


def spread(line_ref, out_ref, here_ref, sem):
    load = pltpu.make_async_copy(line_ref, here_ref, sem.at[0])
    load.start()
    load.wait()
    copies = [pltpu.make_async_copy(here_ref, out_ref.at[j], sem.at[j]) for j in range(out_ref.shape[0])]
    for c in copies:
        c.start()
    for c in copies:
        c.wait()


def attend_fresh(p0, p1, p2, p3, acc_ref, stat_ref, q_ref, keys_ref, values_ref, sem):
    tokens, mine = q_ref.shape[1:]
    loads = []
    for i, ref in enumerate((p0, p1, p2, p3)):
        rows = pl.ds(i * tokens, tokens)
        for t, to in enumerate((q_ref.at[i], keys_ref.at[rows], values_ref.at[rows])):
            loads.append(pltpu.make_async_copy(ref.at[:, t * mine : (t + 1) * mine], to, sem.at[3 * i + t]))
    for c in loads:
        c.start()
    for c in loads:
        c.wait()
    lane = lax.broadcasted_iota(jnp.int32, (tokens, HD), 1)
    heads = mine // HD

    def rows_step(i, carry):
        stat = jnp.zeros((tokens, HD), F32)
        for h in range(heads):
            cs = slice(h * HD, (h + 1) * HD)
            s = lax.dot_general(q_ref[i, :, cs], keys_ref[:, cs], NT, preferred_element_type=F32)
            top = jnp.max(s, axis=1, keepdims=True)
            w = jnp.exp2(s * SCALE - top * SCALE)
            acc_ref[i, :, cs] = jnp.dot(w.astype(BF16), values_ref[:, cs], preferred_element_type=F32)
            stat = jnp.where(lane == 2 * h, top, stat)
            stat = jnp.where(lane == 2 * h + 1, jnp.sum(w, axis=1, keepdims=True), stat)
        stat_ref[i] = stat
        return carry

    lax.fori_loop(0, 4, rows_step, 0)


def attend(at_ref, p0, p1, p2, p3, acc_in, stat_in, pool_ref, out_ref, *scratch):
    q_ref, acc_ref, stat_ref, keys_ref, values_ref, s_ref, res_ref, sem_f, sem_k, sem_o = scratch
    tokens, mine = res_ref.shape[1:]
    heads = mine // HD
    blocks, block = pool_ref.shape[0], pool_ref.shape[1]
    here = at_ref[5]
    loads = []
    for i, ref in enumerate((p0, p1, p2, p3)):
        loads.append(pltpu.make_async_copy(ref.at[:, 0:mine], q_ref.at[i], sem_f.at[i]))
    loads.append(pltpu.make_async_copy(acc_in, acc_ref, sem_f.at[4]))
    loads.append(pltpu.make_async_copy(stat_in, stat_ref, sem_f.at[5]))
    for t, to in enumerate((keys_ref, values_ref)):
        for j in range(blocks):
            src = pool_ref.at[lax.rem(here + j, blocks)]
            rows = pl.ds(j * block, block)
            loads.append(
                pltpu.make_async_copy(src.at[:, t * mine : (t + 1) * mine], to.at[rows], sem_k.at[t * blocks + j])
            )
    for c in loads:
        c.start()
    for c in loads:
        c.wait()
    first = at_ref[4]
    cols = lax.broadcasted_iota(jnp.int32, (ROWS, block), 1)
    own = (cols >= first) & (cols < first + 16)
    chunk = 512
    total_keys = keys_ref.shape[0]

    def rows_step(i, carry):
        for h in range(heads):
            cs = slice(h * HD, (h + 1) * HD)
            q = q_ref[i, :, cs]
            before = stat_ref[i, :, 2 * h : 2 * h + 1]
            top = jnp.broadcast_to(before, (ROWS, HD))
            for c in range(0, total_keys, chunk):
                s = lax.dot_general(q, keys_ref[c : c + chunk, cs], NT, preferred_element_type=F32)
                for d in range(0, chunk, HD):
                    piece = s[:, d : d + HD]
                    if c + d == 0:
                        piece = jnp.where(own, -jnp.inf, piece)
                    s_ref[h, :, c + d : c + d + HD] = piece
                    top = jnp.maximum(top, piece)
            top = jnp.max(top, axis=1, keepdims=True)
            shrink = jnp.exp2((before - top) * SCALE)
            top = top * SCALE
            sums = jnp.zeros((ROWS, HD), F32)
            acc = acc_ref[i, :, cs] * shrink
            for c in range(0, total_keys, chunk):
                w = jnp.exp2(s_ref[h, :, c : c + chunk] * SCALE - top)
                for d in range(0, chunk, HD):
                    sums = sums + w[:, d : d + HD]
                acc = acc + jnp.dot(w.astype(BF16), values_ref[c : c + chunk, cs], preferred_element_type=F32)
            total = jnp.sum(sums, axis=1, keepdims=True) + stat_ref[i, :, 2 * h + 1 : 2 * h + 2] * shrink
            res_ref[i, :, cs] = (acc / total).astype(BF16)
        pltpu.make_async_copy(res_ref.at[i], out_ref.at[at_ref[i]], sem_o.at[i]).start()
        return carry

    lax.fori_loop(0, 4, rows_step, 0)
    for i in range(4):
        pltpu.make_async_copy(res_ref.at[i], out_ref.at[0], sem_o.at[i]).wait()


def flips(zh, core):
    pairs = []
    for i in range(math.prod(SIZES)):
        place = list(np.unravel_index(i, SIZES))
        place[3] ^= zh
        place[4] ^= core
        pairs.append((i, int(np.ravel_multi_index(place, SIZES))))
    return pairs


def local(q_fresh, k_fresh, v_fresh, k_stale, v_stale):
    tokens, width = q_fresh.shape
    pooled, mine = k_stale.shape
    heads = mine // HD
    zh, core = lax.axis_index("zh"), lax.axis_index("core")
    zl, here = lax.axis_index("zl"), lax.axis_index("y") * 4 + lax.axis_index("x")
    places = [zh * 2 + core, zh * 2 + 1 - core, (1 - zh) * 2 + core, (1 - zh) * 2 + 1 - core, zl * pooled, here]
    at = jnp.stack(places).astype(jnp.int32)

    dma = pltpu.SemaphoreType.DMA
    part = jax.ShapeDtypeStruct((tokens, 3 * mine), BF16)
    own, near, same, other, copies = pl.pallas_call(
        pack,
        out_shape=(part,) * 4 + (jax.ShapeDtypeStruct((8, pooled, 2 * mine), BF16),),
        in_specs=[SMEM] + [ANY] * 5,
        out_specs=(pl.BlockSpec(),) * 5,
        scratch_shapes=[pltpu.VMEM((tokens, width), BF16)] * 3 + [pltpu.VMEM((pooled, mine), BF16)] * 2 + [dma((5,))],
        compiler_params=pltpu.CompilerParams(vmem_limit_bytes=LIMIT),
        cost_estimate=pl.CostEstimate(flops=0, bytes_accessed=3 << 20, transcendentals=0),
        name="pack",
    )(at, q_fresh, k_fresh, v_fresh, k_stale, v_stale)
    near = lax.ppermute(near, EVERY, flips(0, 1))
    same = lax.ppermute(same, EVERY, flips(1, 0))
    other = lax.ppermute(other, EVERY, flips(1, 1))
    line = lax.all_to_all(copies, "zl", split_axis=0, concat_axis=0).reshape(8 * pooled, 2 * mine)
    planes = pl.pallas_call(
        spread,
        out_shape=jax.ShapeDtypeStruct((16, 8 * pooled, 2 * mine), BF16),
        in_specs=[ANY],
        out_specs=ANY,
        scratch_shapes=[pltpu.VMEM((8 * pooled, 2 * mine), BF16), dma((16,))],
        compiler_params=pltpu.CompilerParams(vmem_limit_bytes=LIMIT),
        cost_estimate=pl.CostEstimate(flops=0, bytes_accessed=3 << 20, transcendentals=0),
        name="spread",
    )(line)
    pool = lax.all_to_all(planes, ("y", "x"), split_axis=0, concat_axis=0)

    fresh = 4 * tokens
    block = (4, tokens, mine)
    acc, stat = pl.pallas_call(
        attend_fresh,
        out_shape=(jax.ShapeDtypeStruct(block, F32), jax.ShapeDtypeStruct((4, tokens, HD), F32)),
        in_specs=[ANY] * 4,
        out_specs=(pl.BlockSpec(),) * 2,
        scratch_shapes=[pltpu.VMEM(block, BF16)] + [pltpu.VMEM((fresh, mine), BF16)] * 2 + [dma((12,))],
        compiler_params=pltpu.CompilerParams(vmem_limit_bytes=LIMIT),
        cost_estimate=pl.CostEstimate(flops=FRESH_COST, bytes_accessed=3 << 20, transcendentals=0),
        name="attend_fresh",
    )(own, near, same, other)
    total_keys = 16 * 8 * pooled
    out = pl.pallas_call(
        attend,
        out_shape=jax.ShapeDtypeStruct(block, BF16),
        in_specs=[SMEM] + [ANY] * 7,
        out_specs=ANY,
        scratch_shapes=[
            pltpu.VMEM(block, BF16),
            pltpu.VMEM(block, F32),
            pltpu.VMEM((4, tokens, HD), F32),
            pltpu.VMEM((total_keys, mine), BF16),
            pltpu.VMEM((total_keys, mine), BF16),
            pltpu.VMEM((heads, ROWS, total_keys), F32),
            pltpu.VMEM(block, BF16),
            dma((6,)),
            dma((32,)),
            dma((4,)),
        ],
        compiler_params=pltpu.CompilerParams(vmem_limit_bytes=LIMIT),
        cost_estimate=pl.CostEstimate(
            flops=4 * fresh * heads * total_keys * HD,
            bytes_accessed=6 << 20,
            transcendentals=fresh * heads * total_keys,
        ),
        name="attend",
    )(at, own, near, same, other, acc, stat, pool)
    back = lax.all_to_all(out, ("zh", "core"), split_axis=0, concat_axis=0)
    return back.transpose(1, 0, 2).reshape(tokens, width)


def solution(mesh):
    fine = Mesh(mesh.devices.reshape(SIZES), EVERY)
    whole = P(EVERY, None)
    part = P(("y", "x", "zl"), ("zh", "core"))
    return jax.shard_map(
        local,
        mesh=fine,
        in_specs=(whole, whole, whole, part, part),
        out_specs=whole,
        check_vma=False,
    )
```

time: 152 us -> 143 us (0.941)
  the two profiles are of different devices: /device:TPU:161 before, /device:TPU:32 now
where the time goes in v4:
time: 143 us
  waiting for transfers between devices  42.6 us (30%)
  blocking collectives  36.4 us (25%)
  starting transfers between devices  36 us (25%)
  Pallas kernels  23.6 us (17%)
  local copies, waits for them, and re-layouts  4.13 us (3%)
    all_to_all x1, blocking collectives, local(): back = lax.all_to_all(out, ('zh', 'core'), split_axis=0, concat_axis=0)  36.4 us
    all_to_all x1, waiting for transfers between devices, local(): pool = lax.all_to_all(planes, ('y', 'x'), split_axis=0, concat_axis=0)  22.8 us
    ppermute x1, waiting for transfers between devices, local(): other = lax.ppermute(other, EVERY, flips(1, 1))  13.4 us
    all_to_all x1, starting transfers between devices, local(): lax.all_to_all(copies, 'zl', split_axis=0, concat_axis=0)  12.6 us
    pallas_call x1, Pallas kernels, local(): pl.pallas_call(attend, out_shape=jax.ShapeDtypeStruct(block, BF16), in_sp...  11.7 us
    ppermute x1, starting transfers between devices, local(): same = lax.ppermute(same, EVERY, flips(1, 0))  8.22 us
    all_to_all x1, starting transfers between devices, local(): pool = lax.all_to_all(planes, ('y', 'x'), split_axis=0, concat_axis=0)  7.05 us
    ppermute x1, waiting for transfers between devices, local(): same = lax.ppermute(same, EVERY, flips(1, 0))  6.39 us
  transfers between devices with their start and end apart: 5, of which 3 were waited for; matrix products, arithmetic and copies ran while one was open for 0% of the time, Pallas kernels for 6%

profile of v4, /device:TPU:32, one launch (start us, length us, event | category | flops | bytes accessed | tf_op | source)
XLA Modules:
  0.0 142.8 jit_solution(7812196495241641776)
XLA Ops:
  0.0 0.7 stack.27.at_ref
  0.7 3.1 %pack.1 = (bf16[128,1152]{1,0:T(8,128)(2,1)}, bf16[128,1152]{1,0:T(8,128)(2,1)}, bf16[128,1152]{1,0:T(8,128)(2,1)}, bf16[128,1152]{1,0:T(8,128)(2,1)}, bf16[8,16,768]{2,1,0:T(8,128)(2,1)}) custom-call(s32[6]{0:T(128)} %stack.27.at_ref, bf16[128,1536]{1,0:T(8,128)(2,1)} %qa.1, bf16[128,1536]{1,0:T(8,128)(2,1)} %ka.1, bf16[128,1536]{1,0:T(8,128)(2,1)} %va.1, ...), custom_call_target="tpu_custom_call" | custom-call | bytes 3145728 | tf_op jit(solution)/shard_map/pack/pallas_call | solution.py:170
  3.8 12.6 %all-to-all-start = ((bf16[8,16,768]{2,1,0:T(8,128)(2,1)}), bf16[8,16,768]{2,1,0:T(8,128)(2,1)S(1)}, u32[]{:S(2)}, u32[]{:S(2)}) async-start(bf16[8,16,768]{2,1,0:T(8,128)(2,1)} %get-tuple-element.18), calls=%async_computation | async-start | bytes 393216 | tf_op jit(solution)/shard_map/all_to_all | solution.py:183
  16.4 1.9 %collective-permute-start = (bf16[128,1152]{1,0:T(8,128)(2,1)}, bf16[128,1152]{1,0:T(8,128)(2,1)S(1)}, u32[]{:S(2)}, u32[]{:S(2)}) collective-permute-start(bf16[128,1152]{1,0:T(8,128)(2,1)} %get-tuple-element.13), channel_id=1, source_target_pairs={{0,1},{1,0},{2,3},{3,2},{4,5},{5,4},{6,7},{7,6},{8,9},{9,8},{10,11... | collective-permute-start | bytes 884744 | tf_op jit(solution)/shard_map/ppermute | solution.py:180
  18.3 8.2 %collective-permute-start.1 = (bf16[128,1152]{1,0:T(8,128)(2,1)}, bf16[128,1152]{1,0:T(8,128)(2,1)}, u32[]{:S(2)}, u32[]{:S(2)}) collective-permute-start(bf16[128,1152]{1,0:T(8,128)(2,1)} %get-tuple-element.14), channel_id=1, source_target_pairs={{0,2},{1,3},{2,0},{3,1},{4,6},{5,7},{6,4},{7,5},{8,10},{9,11},{10,... | collective-permute-start | bytes 884744 | tf_op jit(solution)/shard_map/ppermute | solution.py:181
  26.5 6.2 %collective-permute-start.2 = (bf16[128,1152]{1,0:T(8,128)(2,1)}, bf16[128,1152]{1,0:T(8,128)(2,1)}, u32[]{:S(2)}, u32[]{:S(2)}) collective-permute-start(bf16[128,1152]{1,0:T(8,128)(2,1)} %get-tuple-element.15), channel_id=1, source_target_pairs={{0,3},{1,2},{2,1},{3,0},{4,7},{5,6},{6,5},{7,4},{8,11},{9,10},{10,... | collective-permute-start | bytes 884744 | tf_op jit(solution)/shard_map/ppermute | solution.py:182
  32.7 0.0 all-to-all-done
  32.7 0.0 copy-start.1
  32.7 0.7 copy-done.1
  33.4 2.7 %spread.1 = bf16[16,128,768]{2,1,0:T(8,128)(2,1)} custom-call(bf16[128,768]{1,0:T(8,128)(2,1)} %bitcast.11), custom_call_target="tpu_custom_call" | custom-call | bytes 3145728 | tf_op jit(solution)/shard_map/spread/pallas_call | solution.py:184
  36.1 7.0 %all-to-all-start.1 = ((bf16[16,128,768]{2,1,0:T(8,128)(2,1)}), bf16[16,128,768]{2,1,0:T(8,128)(2,1)S(1)}, u32[]{:S(2)}, u32[]{:S(2)}) async-start(bf16[16,128,768]{2,1,0:T(8,128)(2,1)} %spread.1), calls=%async_computation.1 | async-start | bytes 6291456 | tf_op jit(solution)/shard_map/all_to_all | solution.py:194
  43.1 0.0 collective-permute-done.p1
  43.2 0.0 copy-start.2
  43.2 6.4 %collective-permute-done.1.p2 = bf16[128,1152]{1,0:T(8,128)(2,1)} collective-permute-done((bf16[128,1152]{1,0:T(8,128)(2,1)}, bf16[128,1152]{1,0:T(8,128)(2,1)}, u32[]{:S(2)}, u32[]{:S(2)}) %collective-permute-start.1) | collective-permute-done | bytes 294944 | tf_op jit(solution)/shard_map/ppermute | solution.py:181
  49.6 13.4 %collective-permute-done.2.p3 = bf16[128,1152]{1,0:T(8,128)(2,1)} collective-permute-done((bf16[128,1152]{1,0:T(8,128)(2,1)}, bf16[128,1152]{1,0:T(8,128)(2,1)}, u32[]{:S(2)}, u32[]{:S(2)}) %collective-permute-start.2) | collective-permute-done | bytes 294944 | tf_op jit(solution)/shard_map/ppermute | solution.py:182
  63.0 0.0 copy-done.2
  63.0 6.1 %attend_fresh.1 = (f32[4,128,384]{2,1,0:T(8,128)}, f32[4,128,128]{2,1,0:T(8,128)}) custom-call(bf16[128,1152]{1,0:T(8,128)(2,1)} %get-tuple-element.12.p0, bf16[128,1152]{1,0:T(8,128)(2,1)} %copy-done.2, bf16[128,1152]{1,0:T(8,128)(2,1)} %collective-permute-done.1.p2, bf16[128,1152]{1,0:T(8,128)(2,1)} %collective-permute-done.2.p3), custom_call_target="tpu_custom_call" | custom-call | flops 64424509440 | bytes 3145728 | tf_op jit(solution)/shard_map/attend_fresh/pallas_call | solution.py:198
  69.1 22.8 %all-to-all-done.1.pool_ref = bf16[16,128,768]{2,1,0:T(8,128)(2,1)S(1)} async-done(((bf16[16,128,768]{2,1,0:T(8,128)(2,1)}), bf16[16,128,768]{2,1,0:T(8,128)(2,1)S(1)}, u32[]{:S(2)}, u32[]{:S(2)}) %all-to-all-start.1) | async-done | bytes 3145760 | tf_op jit(solution)/shard_map/all_to_all | solution.py:194
  91.9 0.0 copy-start
  91.9 1.6 %copy-done = bf16[16,128,768]{2,1,0:T(8,128)(2,1)} copy-done((bf16[16,128,768]{2,1,0:T(8,128)(2,1)}, bf16[16,128,768]{2,1,0:T(8,128)(2,1)S(1)}, u32[]{:S(2)}) %copy-start) | copy-done | bytes 3145752
  93.5 11.7 %attend.1 = bf16[4,128,384]{2,1,0:T(8,128)(2,1)} custom-call(s32[6]{0:T(128)} %stack.27.at_ref, bf16[128,1152]{1,0:T(8,128)(2,1)} %get-tuple-element.12.p0, bf16[128,1152]{1,0:T(8,128)(2,1)} %copy-done.2, bf16[128,1152]{1,0:T(8,128)(2,1)} %collective-permute-done.1.p2, bf16[128,1152]{1,0:T(8,128)(2,1)} %collective-permute-done.2.p3, ...), custom_call_target="tpu_custom_call" | custom-call | flops 1610612736 | bytes 6291456 | tf_op jit(solution)/shard_map/attend/pallas_call | solution.py:209
  105.2 36.4 %all_to_all.15 = bf16[4,128,384]{2,1,0:T(8,128)(2,1)S(1)} all-to-all(bf16[4,128,384]{2,1,0:T(8,128)(2,1)} %attend.1), channel_id=1, replica_groups=mesh['y'=4,'x'=4,'zl'=8,'zh'=2,'core'=2] {'zh','core'}, dimensions={0} | all-to-all | bytes 786432 | tf_op jit(solution)/shard_map/all_to_all | solution.py:234
  141.6 0.2 copy.6
  141.8 0.9 copy.7
Async XLA Ops:
  3.8 29.0 %all-to-all-start = ((bf16[8,16,768]{2,1,0:T(8,128)(2,1)}), bf16[8,16,768]{2,1,0:T(8,128)(2,1)S(1)}, u32[]{:S(2)}, u32[]{:S(2)}) async-start(bf16[8,16,768]{2,1,0:T(8,128)(2,1)} %get-tuple-element.18), calls=%async_computation | async-start | bytes 393216 | tf_op jit(solution)/shard_map/all_to_all | solution.py:183
  16.4 26.8 %collective-permute-start = (bf16[128,1152]{1,0:T(8,128)(2,1)}, bf16[128,1152]{1,0:T(8,128)(2,1)S(1)}, u32[]{:S(2)}, u32[]{:S(2)}) collective-permute-start(bf16[128,1152]{1,0:T(8,128)(2,1)} %get-tuple-element.13), channel_id=1, source_target_pairs={{0,1},{1,0},{2,3},{3,2},{4,5},{5,4},{6,7},{7,6},{8,9},{9,8},{10,11... | collective-permute-start | bytes 884744 | tf_op jit(solution)/shard_map/ppermute | solution.py:180
  18.3 31.2 %collective-permute-start.1 = (bf16[128,1152]{1,0:T(8,128)(2,1)}, bf16[128,1152]{1,0:T(8,128)(2,1)}, u32[]{:S(2)}, u32[]{:S(2)}) collective-permute-start(bf16[128,1152]{1,0:T(8,128)(2,1)} %get-tuple-element.14), channel_id=1, source_target_pairs={{0,2},{1,3},{2,0},{3,1},{4,6},{5,7},{6,4},{7,5},{8,10},{9,11},{10,... | collective-permute-start | bytes 884744 | tf_op jit(solution)/shard_map/ppermute | solution.py:181
  26.5 36.4 %collective-permute-start.2 = (bf16[128,1152]{1,0:T(8,128)(2,1)}, bf16[128,1152]{1,0:T(8,128)(2,1)}, u32[]{:S(2)}, u32[]{:S(2)}) collective-permute-start(bf16[128,1152]{1,0:T(8,128)(2,1)} %get-tuple-element.15), channel_id=1, source_target_pairs={{0,3},{1,2},{2,1},{3,0},{4,7},{5,6},{6,5},{7,4},{8,11},{9,10},{10,... | collective-permute-start | bytes 884744 | tf_op jit(solution)/shard_map/ppermute | solution.py:182
  32.7 0.7 copy-start.1
  36.1 55.8 %all-to-all-start.1 = ((bf16[16,128,768]{2,1,0:T(8,128)(2,1)}), bf16[16,128,768]{2,1,0:T(8,128)(2,1)S(1)}, u32[]{:S(2)}, u32[]{:S(2)}) async-start(bf16[16,128,768]{2,1,0:T(8,128)(2,1)} %spread.1), calls=%async_computation.1 | async-start | bytes 6291456 | tf_op jit(solution)/shard_map/all_to_all | solution.py:194
  43.2 19.8 %copy-start.2 = (bf16[128,1152]{1,0:T(8,128)(2,1)}, bf16[128,1152]{1,0:T(8,128)(2,1)S(1)}, u32[]{:S(2)}) copy-start(bf16[128,1152]{1,0:T(8,128)(2,1)S(1)} %collective-permute-done.p1) | copy-start | bytes 884740
  91.9 1.6 %copy-start = (bf16[16,128,768]{2,1,0:T(8,128)(2,1)}, bf16[16,128,768]{2,1,0:T(8,128)(2,1)S(1)}, u32[]{:S(2)}) copy-start(bf16[16,128,768]{2,1,0:T(8,128)(2,1)S(1)} %all-to-all-done.1.pool_ref) | copy-start | bytes 9437188

commit v5 on v4

v5 whole, which is shorter than its diff:
```python
import math

import jax
import jax.numpy as jnp
import numpy as np
from jax import lax
from jax.experimental import pallas as pl
from jax.experimental.pallas import tpu as pltpu
from jax.sharding import Mesh
from jax.sharding import PartitionSpec as P

HD = 128
EVERY = ("y", "x", "zl", "zh", "core")
SIZES = (4, 4, 8, 2, 2)
SCALE = HD**-0.5 * math.log2(math.e)
NT = (((1,), (1,)), ((), ()))
F32 = jnp.float32
LIMIT = 60 << 20
SPREAD_LIMIT = 48 << 20
ATTEND_LIMIT = 48 << 20
FRESH_COST = 60 << 30
BF16 = jnp.bfloat16
ANY = pl.BlockSpec(memory_space=pl.ANY)
VMEM = pl.BlockSpec(memory_space=pltpu.VMEM)


def peers():
    zh, core = lax.axis_index("zh"), lax.axis_index("core")
    return [a * 2 + b for a in (zh, 1 - zh) for b in (core, 1 - core)]


def pack(qa, ka, va, ksa, vsa, *refs):
    parts, pooled_ref = refs[0:4], refs[4]
    q_ref, k_ref, v_ref, ks_ref, vs_ref, sem = refs[5:]
    loads = zip((ksa, vsa, qa, ka, va), (ks_ref, vs_ref, q_ref, k_ref, v_ref))
    loads = [pltpu.make_async_copy(a, b, sem.at[i]) for i, (a, b) in enumerate(loads)]
    for c in loads:
        c.start()
    mine = ks_ref.shape[1]
    for c in loads[:2]:
        c.wait()
    for j in range(pooled_ref.shape[0]):
        pooled_ref[j, :, 0:mine] = ks_ref[...]
        pooled_ref[j, :, mine : 2 * mine] = vs_ref[...]
    places = peers()
    for t, ref in enumerate((q_ref, k_ref, v_ref)):
        loads[2 + t].wait()
        for p, part in enumerate(parts):
            cols = pl.ds(pl.multiple_of(places[p] * mine, HD), mine)
            part[:, t * mine : (t + 1) * mine] = ref[:, cols]


def spread(line_ref, near_ref, out_ref, same_ref, sem):
    copies = [pltpu.make_async_copy(line_ref, out_ref.at[j], sem.at[j]) for j in range(out_ref.shape[0])]
    for c in copies:
        c.start()
    for c in copies:
        c.wait()


def attend_fresh(p0, p1, p2, p3, carry_ref, q_ref, keys_ref, values_ref, sem):
    tokens, mine = q_ref.shape[1:]
    loads = []
    for i, ref in enumerate((p0, p1, p2, p3)):
        rows = pl.ds(i * tokens, tokens)
        for t, to in enumerate((q_ref.at[i], keys_ref.at[rows], values_ref.at[rows])):
            loads.append(pltpu.make_async_copy(ref.at[:, t * mine : (t + 1) * mine], to, sem.at[3 * i + t]))
    for c in loads:
        c.start()
    for c in loads:
        c.wait()
    lane = lax.broadcasted_iota(jnp.int32, (tokens, HD), 1)
    heads = mine // HD

    def rows_step(i, carry):
        stat = jnp.zeros((tokens, HD), F32)
        rows = pl.ds(pl.multiple_of(i * tokens, tokens), tokens)
        for h in range(heads):
            cs = slice(h * HD, (h + 1) * HD)
            q = q_ref[i, :, cs]
            s = lax.dot_general(q, keys_ref[:, cs], NT, preferred_element_type=F32)
            top = jnp.max(s, axis=1, keepdims=True)
            w = jnp.exp2(s * SCALE - top * SCALE)
            carry_ref[rows, cs] = q.astype(F32)
            carry_ref[rows, mine + h * HD : mine + (h + 1) * HD] = jnp.dot(
                w.astype(BF16), values_ref[:, cs], preferred_element_type=F32
            )
            stat = jnp.where(lane == 2 * h, top, stat)
            stat = jnp.where(lane == 2 * h + 1, jnp.sum(w, axis=1, keepdims=True), stat)
        carry_ref[rows, 2 * mine :] = stat
        return carry

    lax.fori_loop(0, 4, rows_step, 0)


def attend(carry_ref, pool_ref, out_ref, s_ref):
    tokens, mine = out_ref.shape[1:]
    heads = mine // HD
    blocks, block = pool_ref.shape[0], pool_ref.shape[1]
    stale = blocks * block
    here = lax.axis_index("y") * 4 + lax.axis_index("x")
    first = here * block + lax.axis_index("zl") * (block // 8)
    col = lax.broadcasted_iota(jnp.int32, (tokens, block), 1)
    places = peers()
    steps = [(h, i) for i in range(4) for h in range(heads)]
    tops = {}

    def own(b):
        return (col >= first - b * block) & (col < first - b * block + block // 8)

    def scores(n):
        h, i = steps[n]
        rows = slice(i * tokens, (i + 1) * tokens)
        cs = slice(h * HD, (h + 1) * HD)
        q = carry_ref[rows, cs].astype(BF16)
        before = carry_ref[rows, 2 * mine + 2 * h : 2 * mine + 2 * h + 1]
        top = jnp.broadcast_to(before, (tokens, HD))
        for b in range(0, blocks, 4):
            keys = pool_ref[b : b + 4, :, cs].reshape(4 * block, HD)
            s = lax.dot_general(q, keys, NT, preferred_element_type=F32)
            for d in range(4):
                piece = jnp.where(own(b + d), -jnp.inf, s[:, d * block : (d + 1) * block])
                s_ref[n % 2, :, (b + d) * block : (b + d + 1) * block] = piece
                top = jnp.maximum(top, piece)
        tops[n] = (before, jnp.max(top, axis=1, keepdims=True))

    def weigh(n):
        h, i = steps[n]
        rows = slice(i * tokens, (i + 1) * tokens)
        cs = slice(mine + h * HD, mine + (h + 1) * HD)
        before, top = tops.pop(n)
        shrink = jnp.exp2((before - top) * SCALE)
        top = top * SCALE
        sums = jnp.zeros((tokens, HD), F32)
        acc = carry_ref[rows, cs] * shrink
        for b in range(0, blocks, 4):
            w = jnp.exp2(s_ref[n % 2, :, b * block : (b + 4) * block] * SCALE - top)
            for d in range(4):
                sums = sums + w[:, d * block : (d + 1) * block]
            values = pool_ref[b : b + 4, :, cs].reshape(4 * block, HD)
            acc = acc + jnp.dot(w.astype(BF16), values, preferred_element_type=F32)
        total = carry_ref[rows, 2 * mine + 2 * h + 1 : 2 * mine + 2 * h + 2] * shrink
        total = total + jnp.sum(sums, axis=1, keepdims=True)
        out_ref[places[i], :, h * HD : (h + 1) * HD] = (acc / total).astype(BF16)

    scores(0)
    for n in range(len(steps)):
        if n + 1 < len(steps):
            scores(n + 1)
        weigh(n)


def flips(zh, core):
    pairs = []
    for i in range(math.prod(SIZES)):
        place = list(np.unravel_index(i, SIZES))
        place[3] ^= zh
        place[4] ^= core
        pairs.append((i, int(np.ravel_multi_index(place, SIZES))))
    return pairs


def local(q_fresh, k_fresh, v_fresh, k_stale, v_stale):
    tokens, width = q_fresh.shape
    pooled, mine = k_stale.shape
    heads = mine // HD
    dma = pltpu.SemaphoreType.DMA
    part = jax.ShapeDtypeStruct((tokens, 3 * mine), BF16)
    own, near, same, other, copies = pl.pallas_call(
        pack,
        out_shape=(part,) * 4 + (jax.ShapeDtypeStruct((8, pooled, 2 * mine), BF16),),
        in_specs=[ANY] * 5,
        out_specs=(pl.BlockSpec(),) * 5,
        scratch_shapes=[pltpu.VMEM((tokens, width), BF16)] * 3 + [pltpu.VMEM((pooled, mine), BF16)] * 2 + [dma((5,))],
        compiler_params=pltpu.CompilerParams(vmem_limit_bytes=LIMIT),
        cost_estimate=pl.CostEstimate(flops=0, bytes_accessed=3 << 20, transcendentals=0),
        name="pack",
    )(q_fresh, k_fresh, v_fresh, k_stale, v_stale)
    same = lax.ppermute(same, EVERY, flips(1, 0))
    other = lax.ppermute(other, EVERY, flips(1, 1))
    line = lax.all_to_all(copies, "zl", split_axis=0, concat_axis=0).reshape(8 * pooled, 2 * mine)
    planes, near = pl.pallas_call(
        spread,
        out_shape=(jax.ShapeDtypeStruct((16, 8 * pooled, 2 * mine), BF16), part),
        in_specs=[VMEM, ANY],
        out_specs=(ANY, ANY),
        scratch_shapes=[dma((16,))],
        input_output_aliases={1: 1},
        compiler_params=pltpu.CompilerParams(vmem_limit_bytes=SPREAD_LIMIT),
        cost_estimate=pl.CostEstimate(flops=0, bytes_accessed=3 << 20, transcendentals=0),
        name="spread",
    )(line, near)
    near = lax.ppermute(near, EVERY, flips(0, 1))
    pool = lax.all_to_all(planes, ("y", "x"), split_axis=0, concat_axis=0)

    fresh = 4 * tokens
    carry = jax.ShapeDtypeStruct((fresh, 2 * mine + HD), F32)
    carry = pl.pallas_call(
        attend_fresh,
        out_shape=carry,
        in_specs=[ANY] * 4,
        scratch_shapes=[pltpu.VMEM((4, tokens, mine), BF16)] + [pltpu.VMEM((fresh, mine), BF16)] * 2 + [dma((12,))],
        compiler_params=pltpu.CompilerParams(vmem_limit_bytes=LIMIT),
        cost_estimate=pl.CostEstimate(flops=FRESH_COST, bytes_accessed=3 << 20, transcendentals=0),
        name="attend_fresh",
    )(own, near, same, other)
    total_keys = 16 * 8 * pooled
    out = pl.pallas_call(
        attend,
        out_shape=jax.ShapeDtypeStruct((4, tokens, mine), BF16),
        in_specs=[VMEM, VMEM],
        out_specs=VMEM,
        scratch_shapes=[pltpu.VMEM((2, tokens, total_keys), F32)],
        compiler_params=pltpu.CompilerParams(vmem_limit_bytes=ATTEND_LIMIT),
        cost_estimate=pl.CostEstimate(
            flops=4 * fresh * heads * total_keys * HD,
            bytes_accessed=6 << 20,
            transcendentals=fresh * heads * total_keys,
        ),
        name="attend",
    )(carry, pool)
    back = lax.all_to_all(out, ("zh", "core"), split_axis=0, concat_axis=0)
    return back.transpose(1, 0, 2).reshape(tokens, width)


def solution(mesh):
    fine = Mesh(mesh.devices.reshape(SIZES), EVERY)
    whole = P(EVERY, None)
    part = P(("y", "x", "zl"), ("zh", "core"))
    return jax.shard_map(
        local,
        mesh=fine,
        in_specs=(whole, whole, whole, part, part),
        out_specs=whole,
        check_vma=False,
    )
```

time: 143 us -> 164 us (1.15)
  waiting for transfers between devices: 42.6 us -> 77 us
  Pallas kernels: 23.6 us -> 16.2 us
  blocking collectives: 36.4 us -> 31.8 us
    all_to_all x1, waiting for transfers between devices: 0.01 us -> 34.7 us  [local(): lax.all_to_all(copies, 'zl', split_axis=0, concat_axis=0)]
    all_to_all x1, waiting for transfers between devices: 22.8 us -> 42.2 us  [local(): pool = lax.all_to_all(planes, ('y', 'x'), split_axis=0, concat_axis=0)]
    ppermute x1, waiting for transfers between devices: 13.4 us -> 0.01 us  [local(): other = lax.ppermute(other, EVERY, flips(1, 1))]
    pallas_call x3, Pallas kernels: 20.5 us -> 13.8 us  [the longest x1 6.44 us: local(): pl.pallas_call(attend_fresh, out_shape=carry, in_specs=[ANY] * 4, scratch...]
    ppermute x1, waiting for transfers between devices: 6.39 us -> 0.01 us  [local(): same = lax.ppermute(same, EVERY, flips(1, 0))]
    all_to_all x1, blocking collectives: 36.4 us -> 31.8 us  [local(): back = lax.all_to_all(out, ('zh', 'core'), split_axis=0, concat_axis=0)]
  transfers between devices with their start and end apart: 5 -> 5, of which waited for: 3 -> 2; matrix products, arithmetic and copies ran while one was open for 0% -> 0% of each run, Pallas kernels for 6% -> 5%
where the time goes in v5:
time: 164 us; the launch traced here: 163 us
  waiting for transfers between devices  77 us (47%)
  starting transfers between devices  34.8 us (21%)
  blocking collectives  31.8 us (19%)
  Pallas kernels  16.2 us (10%)
  local copies, waits for them, and re-layouts  3.36 us (2%)
    all_to_all x1, waiting for transfers between devices, local(): pool = lax.all_to_all(planes, ('y', 'x'), split_axis=0, concat_axis=0)  42.2 us
    all_to_all x1, waiting for transfers between devices, local(): lax.all_to_all(copies, 'zl', split_axis=0, concat_axis=0)  34.7 us
    all_to_all x1, blocking collectives, local(): back = lax.all_to_all(out, ('zh', 'core'), split_axis=0, concat_axis=0)  31.8 us
    all_to_all x1, starting transfers between devices, local(): lax.all_to_all(copies, 'zl', split_axis=0, concat_axis=0)  12.6 us
    ppermute x1, starting transfers between devices, local(): same = lax.ppermute(same, EVERY, flips(1, 0))  8.21 us
    all_to_all x1, starting transfers between devices, local(): pool = lax.all_to_all(planes, ('y', 'x'), split_axis=0, concat_axis=0)  7.05 us
    pallas_call x1, Pallas kernels, local(): pl.pallas_call(attend_fresh, out_shape=carry, in_specs=[ANY] * 4, scratch...  6.44 us
    pallas_call x1, Pallas kernels, local(): pl.pallas_call(attend, out_shape=jax.ShapeDtypeStruct((4, tokens, mine),...  5.54 us
  transfers between devices with their start and end apart: 5, of which 2 were waited for; matrix products, arithmetic and copies ran while one was open for 0% of the time, Pallas kernels for 5%

profile of v5, /device:TPU:32, one launch (start us, length us, event | category | flops | bytes accessed | tf_op | source)
XLA Modules:
  0.0 163.1 jit_solution(15384012897898123670)
XLA Ops:
  0.0 2.4 %pack.1 = (bf16[128,1152]{1,0:T(8,128)(2,1)}, bf16[128,1152]{1,0:T(8,128)(2,1)}, bf16[128,1152]{1,0:T(8,128)(2,1)}, bf16[128,1152]{1,0:T(8,128)(2,1)}, bf16[8,16,768]{2,1,0:T(8,128)(2,1)}) custom-call(bf16[128,1536]{1,0:T(8,128)(2,1)} %qa.1, bf16[128,1536]{1,0:T(8,128)(2,1)} %ka.1, bf16[128,1536]{1,0:T(8,128)(2,1)} %va.1, bf16[16,384]{1,0:T(8,128)(2,1)} %ksa.1, ...), custom_call_target="tpu_custom_call" | custom-call | bytes 3145728 | tf_op jit(solution)/shard_map/pack/pallas_call | solution.py:169
  2.4 12.6 %all-to-all-start = ((bf16[8,16,768]{2,1,0:T(8,128)(2,1)}), bf16[8,16,768]{2,1,0:T(8,128)(2,1)S(1)}, u32[]{:S(2)}, u32[]{:S(2)}) async-start(bf16[8,16,768]{2,1,0:T(8,128)(2,1)} %get-tuple-element.13), calls=%async_computation | async-start | bytes 393216 | tf_op jit(solution)/shard_map/all_to_all | solution.py:181
  15.1 8.2 %collective-permute-start.1 = (bf16[128,1152]{1,0:T(8,128)(2,1)}, bf16[128,1152]{1,0:T(8,128)(2,1)S(1)}, u32[]{:S(2)}, u32[]{:S(2)}) collective-permute-start(bf16[128,1152]{1,0:T(8,128)(2,1)} %get-tuple-element.16), channel_id=1, source_target_pairs={{0,2},{1,3},{2,0},{3,1},{4,6},{5,7},{6,4},{7,5},{8,10},{9,11},{10,... | collective-permute-start | bytes 884744 | tf_op jit(solution)/shard_map/ppermute | solution.py:179
  23.3 4.9 %collective-permute-start.2 = (bf16[128,1152]{1,0:T(8,128)(2,1)}, bf16[128,1152]{1,0:T(8,128)(2,1)}, u32[]{:S(2)}, u32[]{:S(2)}) collective-permute-start(bf16[128,1152]{1,0:T(8,128)(2,1)} %get-tuple-element.17), channel_id=1, source_target_pairs={{0,3},{1,2},{2,1},{3,0},{4,7},{5,6},{6,5},{7,4},{8,11},{9,10},{10,... | collective-permute-start | bytes 884744 | tf_op jit(solution)/shard_map/ppermute | solution.py:180
  28.2 34.7 %all-to-all-done = bf16[8,16,768]{2,1,0:T(8,128)(2,1)S(1)} async-done(((bf16[8,16,768]{2,1,0:T(8,128)(2,1)}), bf16[8,16,768]{2,1,0:T(8,128)(2,1)S(1)}, u32[]{:S(2)}, u32[]{:S(2)}) %all-to-all-start) | async-done | bytes 196640 | tf_op jit(solution)/shard_map/all_to_all | solution.py:181
  62.9 1.8 %spread.1 = (bf16[16,128,768]{2,1,0:T(8,128)(2,1)}, bf16[128,1152]{1,0:T(8,128)(2,1)}) custom-call(bf16[128,768]{1,0:T(8,128)(2,1)S(1)} %bitcast.3, bf16[128,1152]{1,0:T(8,128)(2,1)} %get-tuple-element.14.near_ref), custom_call_target="tpu_custom_call", output_to_operand_aliasing={{1}: (1, {})} | custom-call | bytes 3145728 | tf_op jit(solution)/shard_map/spread/pallas_call | solution.py:182
  64.7 1.9 %collective-permute-start = (bf16[128,1152]{1,0:T(8,128)(2,1)}, bf16[128,1152]{1,0:T(8,128)(2,1)}, u32[]{:S(2)}, u32[]{:S(2)}) collective-permute-start(bf16[128,1152]{1,0:T(8,128)(2,1)} %get-tuple-element.15), channel_id=1, source_target_pairs={{0,1},{1,0},{2,3},{3,2},{4,5},{5,4},{6,7},{7,6},{8,9},{9,8},{10,11... | collective-permute-start | bytes 884744 | tf_op jit(solution)/shard_map/ppermute | solution.py:193
  66.7 7.0 %all-to-all-start.1 = ((bf16[16,128,768]{2,1,0:T(8,128)(2,1)}), bf16[16,128,768]{2,1,0:T(8,128)(2,1)S(1)}, u32[]{:S(2)}, u32[]{:S(2)}) async-start(bf16[16,128,768]{2,1,0:T(8,128)(2,1)} %get-tuple-element.18), calls=%async_computation.1 | async-start | bytes 6291456 | tf_op jit(solution)/shard_map/all_to_all | solution.py:194
  73.7 0.0 collective-permute-done.1.p2
  73.7 0.0 copy-start.1
  73.7 0.0 collective-permute-done.2.p3
  73.7 0.0 collective-permute-done.p1
  73.7 0.7 copy-done.1
  74.5 6.4 %attend_fresh.1.carry_ref = f32[512,896]{1,0:T(8,128)} custom-call(bf16[128,1152]{1,0:T(8,128)(2,1)} %get-tuple-element.12.p0, bf16[128,1152]{1,0:T(8,128)(2,1)} %collective-permute-done.p1, bf16[128,1152]{1,0:T(8,128)(2,1)} %copy-done.1, bf16[128,1152]{1,0:T(8,128)(2,1)} %collective-permute-done.2.p3), custom_call_target="tpu_custom_call" | custom-call | flops 64424509440 | bytes 3145728 | tf_op jit(solution)/shard_map/attend_fresh/pallas_call | solution.py:198
  80.9 42.2 %all-to-all-done.1.pool_ref = bf16[16,128,768]{2,1,0:T(8,128)(2,1)S(1)} async-done(((bf16[16,128,768]{2,1,0:T(8,128)(2,1)}), bf16[16,128,768]{2,1,0:T(8,128)(2,1)S(1)}, u32[]{:S(2)}, u32[]{:S(2)}) %all-to-all-start.1) | async-done | bytes 3145760 | tf_op jit(solution)/shard_map/all_to_all | solution.py:194
  123.1 0.0 copy-start
  123.1 1.5 copy-done
  124.6 5.5 %attend.1 = bf16[4,128,384]{2,1,0:T(8,128)(2,1)S(1)} custom-call(f32[512,896]{1,0:T(8,128)S(1)} %copy-done, bf16[16,128,768]{2,1,0:T(8,128)(2,1)S(1)} %all-to-all-done.1.pool_ref), custom_call_target="tpu_custom_call" | custom-call | flops 1610612736 | bytes 6291456 | tf_op jit(solution)/shard_map/attend/pallas_call | solution.py:208
  130.2 31.8 %all_to_all.15 = bf16[4,128,384]{2,1,0:T(8,128)(2,1)S(1)} all-to-all(bf16[4,128,384]{2,1,0:T(8,128)(2,1)S(1)} %attend.1), channel_id=1, replica_groups=mesh['y'=4,'x'=4,'zl'=8,'zh'=2,'core'=2] {'zh','core'}, dimensions={0} | all-to-all | bytes 786432 | tf_op jit(solution)/shard_map/all_to_all | solution.py:222
  161.9 0.2 copy.7
  162.2 0.9 copy.8
Async XLA Ops:
  2.4 60.5 %all-to-all-start = ((bf16[8,16,768]{2,1,0:T(8,128)(2,1)}), bf16[8,16,768]{2,1,0:T(8,128)(2,1)S(1)}, u32[]{:S(2)}, u32[]{:S(2)}) async-start(bf16[8,16,768]{2,1,0:T(8,128)(2,1)} %get-tuple-element.13), calls=%async_computation | async-start | bytes 393216 | tf_op jit(solution)/shard_map/all_to_all | solution.py:181
  15.1 58.7 %collective-permute-start.1 = (bf16[128,1152]{1,0:T(8,128)(2,1)}, bf16[128,1152]{1,0:T(8,128)(2,1)S(1)}, u32[]{:S(2)}, u32[]{:S(2)}) collective-permute-start(bf16[128,1152]{1,0:T(8,128)(2,1)} %get-tuple-element.16), channel_id=1, source_target_pairs={{0,2},{1,3},{2,0},{3,1},{4,6},{5,7},{6,4},{7,5},{8,10},{9,11},{10,... | collective-permute-start | bytes 884744 | tf_op jit(solution)/shard_map/ppermute | solution.py:179
  23.3 50.5 %collective-permute-start.2 = (bf16[128,1152]{1,0:T(8,128)(2,1)}, bf16[128,1152]{1,0:T(8,128)(2,1)}, u32[]{:S(2)}, u32[]{:S(2)}) collective-permute-start(bf16[128,1152]{1,0:T(8,128)(2,1)} %get-tuple-element.17), channel_id=1, source_target_pairs={{0,3},{1,2},{2,1},{3,0},{4,7},{5,6},{6,5},{7,4},{8,11},{9,10},{10,... | collective-permute-start | bytes 884744 | tf_op jit(solution)/shard_map/ppermute | solution.py:180
  64.7 9.0 %collective-permute-start = (bf16[128,1152]{1,0:T(8,128)(2,1)}, bf16[128,1152]{1,0:T(8,128)(2,1)}, u32[]{:S(2)}, u32[]{:S(2)}) collective-permute-start(bf16[128,1152]{1,0:T(8,128)(2,1)} %get-tuple-element.15), channel_id=1, source_target_pairs={{0,1},{1,0},{2,3},{3,2},{4,5},{5,4},{6,7},{7,6},{8,9},{9,8},{10,11... | collective-permute-start | bytes 884744 | tf_op jit(solution)/shard_map/ppermute | solution.py:193
  66.7 56.5 %all-to-all-start.1 = ((bf16[16,128,768]{2,1,0:T(8,128)(2,1)}), bf16[16,128,768]{2,1,0:T(8,128)(2,1)S(1)}, u32[]{:S(2)}, u32[]{:S(2)}) async-start(bf16[16,128,768]{2,1,0:T(8,128)(2,1)} %get-tuple-element.18), calls=%async_computation.1 | async-start | bytes 6291456 | tf_op jit(solution)/shard_map/all_to_all | solution.py:194
  73.7 0.7 copy-start.1
  123.1 1.5 copy-start

commit v6 on v5

--- a/solution.py
+++ b/solution.py
@@ -50,7 +50,7 @@
             part[:, t * mine : (t + 1) * mine] = ref[:, cols]
 
 
-def spread(line_ref, near_ref, out_ref, same_ref, sem):
+def spread(line_ref, out_ref, sem):
     copies = [pltpu.make_async_copy(line_ref, out_ref.at[j], sem.at[j]) for j in range(out_ref.shape[0])]
     for c in copies:
         c.start()
@@ -176,21 +176,20 @@
         cost_estimate=pl.CostEstimate(flops=0, bytes_accessed=3 << 20, transcendentals=0),
         name="pack",
     )(q_fresh, k_fresh, v_fresh, k_stale, v_stale)
+    near = lax.ppermute(near, EVERY, flips(0, 1))
     same = lax.ppermute(same, EVERY, flips(1, 0))
     other = lax.ppermute(other, EVERY, flips(1, 1))
     line = lax.all_to_all(copies, "zl", split_axis=0, concat_axis=0).reshape(8 * pooled, 2 * mine)
-    planes, near = pl.pallas_call(
+    planes = pl.pallas_call(
         spread,
-        out_shape=(jax.ShapeDtypeStruct((16, 8 * pooled, 2 * mine), BF16), part),
-        in_specs=[VMEM, ANY],
-        out_specs=(ANY, ANY),
+        out_shape=jax.ShapeDtypeStruct((16, 8 * pooled, 2 * mine), BF16),
+        in_specs=[VMEM],
+        out_specs=ANY,
         scratch_shapes=[dma((16,))],
-        input_output_aliases={1: 1},
         compiler_params=pltpu.CompilerParams(vmem_limit_bytes=SPREAD_LIMIT),
         cost_estimate=pl.CostEstimate(flops=0, bytes_accessed=3 << 20, transcendentals=0),
         name="spread",
-    )(line, near)
-    near = lax.ppermute(near, EVERY, flips(0, 1))
+    )(line)
     pool = lax.all_to_all(planes, ("y", "x"), split_axis=0, concat_axis=0)
 
     fresh = 4 * tokens

time: 164 us -> 134 us (0.82)
  waiting for transfers between devices: 77 us -> 42.3 us
  blocking collectives: 31.8 us -> 36.2 us
    all_to_all x1, waiting for transfers between devices: 34.7 us -> 0.01 us  [local(): lax.all_to_all(copies, 'zl', split_axis=0, concat_axis=0)]
    all_to_all x1, waiting for transfers between devices: 42.2 us -> 20.9 us  [local(): pool = lax.all_to_all(planes, ('y', 'x'), split_axis=0, concat_axis=0)]
    ppermute x1, waiting for transfers between devices: 0.01 us -> 13.4 us  [local(): other = lax.ppermute(other, EVERY, flips(1, 1))]
    ppermute x1, waiting for transfers between devices: 0.01 us -> 7.97 us  [local(): same = lax.ppermute(same, EVERY, flips(1, 0))]
    all_to_all x1, blocking collectives: 31.8 us -> 36.2 us  [local(): back = lax.all_to_all(out, ('zh', 'core'), split_axis=0, concat_axis=0)]
  transfers between devices with their start and end apart: 5 -> 5, of which waited for: 2 -> 3; matrix products, arithmetic and copies ran while one was open for 0% -> 0% of each run, Pallas kernels for 5% -> 6%
where the time goes in v6:
time: 134 us; the launch traced here: 133 us
  waiting for transfers between devices  42.3 us (32%)
  blocking collectives  36.2 us (27%)
  starting transfers between devices  36 us (27%)
  Pallas kernels  16.1 us (12%)
  local copies, waits for them, and re-layouts  2.66 us (2%)
    all_to_all x1, blocking collectives, local(): back = lax.all_to_all(out, ('zh', 'core'), split_axis=0, concat_axis=0)  36.2 us
    all_to_all x1, waiting for transfers between devices, local(): pool = lax.all_to_all(planes, ('y', 'x'), split_axis=0, concat_axis=0)  20.9 us
    ppermute x1, waiting for transfers between devices, local(): other = lax.ppermute(other, EVERY, flips(1, 1))  13.4 us
    all_to_all x1, starting transfers between devices, local(): lax.all_to_all(copies, 'zl', split_axis=0, concat_axis=0)  12.6 us
    ppermute x1, starting transfers between devices, local(): same = lax.ppermute(same, EVERY, flips(1, 0))  8.22 us
    ppermute x1, waiting for transfers between devices, local(): same = lax.ppermute(same, EVERY, flips(1, 0))  7.97 us
    all_to_all x1, starting transfers between devices, local(): pool = lax.all_to_all(planes, ('y', 'x'), split_axis=0, concat_axis=0)  7.05 us
    pallas_call x1, Pallas kernels, local(): pl.pallas_call(attend_fresh, out_shape=carry, in_specs=[ANY] * 4, scratch...  6.43 us
  transfers between devices with their start and end apart: 5, of which 3 were waited for; matrix products, arithmetic and copies ran while one was open for 0% of the time, Pallas kernels for 6%

profile of v6, /device:TPU:32, one launch (start us, length us, event | category | flops | bytes accessed | tf_op | source)
XLA Modules:
  0.0 133.4 jit_solution(18193017900469547412)
XLA Ops:
  0.0 2.4 %pack.1 = (bf16[128,1152]{1,0:T(8,128)(2,1)}, bf16[128,1152]{1,0:T(8,128)(2,1)}, bf16[128,1152]{1,0:T(8,128)(2,1)}, bf16[128,1152]{1,0:T(8,128)(2,1)}, bf16[8,16,768]{2,1,0:T(8,128)(2,1)}) custom-call(bf16[128,1536]{1,0:T(8,128)(2,1)} %qa.1, bf16[128,1536]{1,0:T(8,128)(2,1)} %ka.1, bf16[128,1536]{1,0:T(8,128)(2,1)} %va.1, bf16[16,384]{1,0:T(8,128)(2,1)} %ksa.1, ...), custom_call_target="tpu_custom_call" | custom-call | bytes 3145728 | tf_op jit(solution)/shard_map/pack/pallas_call | solution.py:169
  2.4 12.6 %all-to-all-start = ((bf16[8,16,768]{2,1,0:T(8,128)(2,1)}), bf16[8,16,768]{2,1,0:T(8,128)(2,1)S(1)}, u32[]{:S(2)}, u32[]{:S(2)}) async-start(bf16[8,16,768]{2,1,0:T(8,128)(2,1)} %get-tuple-element.14), calls=%async_computation | async-start | bytes 393216 | tf_op jit(solution)/shard_map/all_to_all | solution.py:182
  15.1 1.9 %collective-permute-start = (bf16[128,1152]{1,0:T(8,128)(2,1)}, bf16[128,1152]{1,0:T(8,128)(2,1)S(1)}, u32[]{:S(2)}, u32[]{:S(2)}) collective-permute-start(bf16[128,1152]{1,0:T(8,128)(2,1)} %get-tuple-element.11), channel_id=1, source_target_pairs={{0,1},{1,0},{2,3},{3,2},{4,5},{5,4},{6,7},{7,6},{8,9},{9,8},{10,11... | collective-permute-start | bytes 884744 | tf_op jit(solution)/shard_map/ppermute | solution.py:179
  17.0 8.2 %collective-permute-start.1 = (bf16[128,1152]{1,0:T(8,128)(2,1)}, bf16[128,1152]{1,0:T(8,128)(2,1)}, u32[]{:S(2)}, u32[]{:S(2)}) collective-permute-start(bf16[128,1152]{1,0:T(8,128)(2,1)} %get-tuple-element.12), channel_id=1, source_target_pairs={{0,2},{1,3},{2,0},{3,1},{4,6},{5,7},{6,4},{7,5},{8,10},{9,11},{10,... | collective-permute-start | bytes 884744 | tf_op jit(solution)/shard_map/ppermute | solution.py:180
  25.2 6.2 %collective-permute-start.2 = (bf16[128,1152]{1,0:T(8,128)(2,1)}, bf16[128,1152]{1,0:T(8,128)(2,1)}, u32[]{:S(2)}, u32[]{:S(2)}) collective-permute-start(bf16[128,1152]{1,0:T(8,128)(2,1)} %get-tuple-element.13), channel_id=1, source_target_pairs={{0,3},{1,2},{2,1},{3,0},{4,7},{5,6},{6,5},{7,4},{8,11},{9,10},{10,... | collective-permute-start | bytes 884744 | tf_op jit(solution)/shard_map/ppermute | solution.py:181
  31.4 0.0 all-to-all-done
  31.4 1.8 %spread.1 = bf16[16,128,768]{2,1,0:T(8,128)(2,1)} custom-call(bf16[128,768]{1,0:T(8,128)(2,1)S(1)} %bitcast.3), custom_call_target="tpu_custom_call" | custom-call | bytes 3145728 | tf_op jit(solution)/shard_map/spread/pallas_call | solution.py:183
  33.2 7.0 %all-to-all-start.1 = ((bf16[16,128,768]{2,1,0:T(8,128)(2,1)}), bf16[16,128,768]{2,1,0:T(8,128)(2,1)S(1)}, u32[]{:S(2)}, u32[]{:S(2)}) async-start(bf16[16,128,768]{2,1,0:T(8,128)(2,1)} %spread.1), calls=%async_computation.1 | async-start | bytes 6291456 | tf_op jit(solution)/shard_map/all_to_all | solution.py:193
  40.2 0.0 collective-permute-done.p1
  40.2 0.0 copy-start.1
  40.2 8.0 %collective-permute-done.1.p2 = bf16[128,1152]{1,0:T(8,128)(2,1)} collective-permute-done((bf16[128,1152]{1,0:T(8,128)(2,1)}, bf16[128,1152]{1,0:T(8,128)(2,1)}, u32[]{:S(2)}, u32[]{:S(2)}) %collective-permute-start.1) | collective-permute-done | bytes 294944 | tf_op jit(solution)/shard_map/ppermute | solution.py:180
  48.2 13.4 %collective-permute-done.2.p3 = bf16[128,1152]{1,0:T(8,128)(2,1)} collective-permute-done((bf16[128,1152]{1,0:T(8,128)(2,1)}, bf16[128,1152]{1,0:T(8,128)(2,1)}, u32[]{:S(2)}, u32[]{:S(2)}) %collective-permute-start.2) | collective-permute-done | bytes 294944 | tf_op jit(solution)/shard_map/ppermute | solution.py:181
  61.6 0.0 copy-done.1
  61.6 6.4 %attend_fresh.1.carry_ref = f32[512,896]{1,0:T(8,128)} custom-call(bf16[128,1152]{1,0:T(8,128)(2,1)} %get-tuple-element.10.p0, bf16[128,1152]{1,0:T(8,128)(2,1)} %copy-done.1, bf16[128,1152]{1,0:T(8,128)(2,1)} %collective-permute-done.1.p2, bf16[128,1152]{1,0:T(8,128)(2,1)} %collective-permute-done.2.p3), custom_call_target="tpu_custom_call" | custom-call | flops 64424509440 | bytes 3145728 | tf_op jit(solution)/shard_map/attend_fresh/pallas_call | solution.py:197
  68.1 20.9 %all-to-all-done.1.pool_ref = bf16[16,128,768]{2,1,0:T(8,128)(2,1)S(1)} async-done(((bf16[16,128,768]{2,1,0:T(8,128)(2,1)}), bf16[16,128,768]{2,1,0:T(8,128)(2,1)S(1)}, u32[]{:S(2)}, u32[]{:S(2)}) %all-to-all-start.1) | async-done | bytes 3145760 | tf_op jit(solution)/shard_map/all_to_all | solution.py:193
  89.0 0.0 copy-start
  89.0 1.5 %copy-done = f32[512,896]{1,0:T(8,128)S(1)} copy-done((f32[512,896]{1,0:T(8,128)S(1)}, f32[512,896]{1,0:T(8,128)}, u32[]{:S(2)}) %copy-start) | copy-done | bytes 1835032
  90.5 5.5 %attend.1 = bf16[4,128,384]{2,1,0:T(8,128)(2,1)S(1)} custom-call(f32[512,896]{1,0:T(8,128)S(1)} %copy-done, bf16[16,128,768]{2,1,0:T(8,128)(2,1)S(1)} %all-to-all-done.1.pool_ref), custom_call_target="tpu_custom_call" | custom-call | flops 1610612736 | bytes 6291456 | tf_op jit(solution)/shard_map/attend/pallas_call | solution.py:207
  96.0 36.2 %all_to_all.15 = bf16[4,128,384]{2,1,0:T(8,128)(2,1)S(1)} all-to-all(bf16[4,128,384]{2,1,0:T(8,128)(2,1)S(1)} %attend.1), channel_id=1, replica_groups=mesh['y'=4,'x'=4,'zl'=8,'zh'=2,'core'=2] {'zh','core'}, dimensions={0} | all-to-all | bytes 786432 | tf_op jit(solution)/shard_map/all_to_all | solution.py:221
  132.2 0.2 copy.6
  132.5 0.9 copy.7
Async XLA Ops:
  2.4 29.0 %all-to-all-start = ((bf16[8,16,768]{2,1,0:T(8,128)(2,1)}), bf16[8,16,768]{2,1,0:T(8,128)(2,1)S(1)}, u32[]{:S(2)}, u32[]{:S(2)}) async-start(bf16[8,16,768]{2,1,0:T(8,128)(2,1)} %get-tuple-element.14), calls=%async_computation | async-start | bytes 393216 | tf_op jit(solution)/shard_map/all_to_all | solution.py:182
  15.1 25.2 %collective-permute-start = (bf16[128,1152]{1,0:T(8,128)(2,1)}, bf16[128,1152]{1,0:T(8,128)(2,1)S(1)}, u32[]{:S(2)}, u32[]{:S(2)}) collective-permute-start(bf16[128,1152]{1,0:T(8,128)(2,1)} %get-tuple-element.11), channel_id=1, source_target_pairs={{0,1},{1,0},{2,3},{3,2},{4,5},{5,4},{6,7},{7,6},{8,9},{9,8},{10,11... | collective-permute-start | bytes 884744 | tf_op jit(solution)/shard_map/ppermute | solution.py:179
  17.0 31.2 %collective-permute-start.1 = (bf16[128,1152]{1,0:T(8,128)(2,1)}, bf16[128,1152]{1,0:T(8,128)(2,1)}, u32[]{:S(2)}, u32[]{:S(2)}) collective-permute-start(bf16[128,1152]{1,0:T(8,128)(2,1)} %get-tuple-element.12), channel_id=1, source_target_pairs={{0,2},{1,3},{2,0},{3,1},{4,6},{5,7},{6,4},{7,5},{8,10},{9,11},{10,... | collective-permute-start | bytes 884744 | tf_op jit(solution)/shard_map/ppermute | solution.py:180
  25.2 36.4 %collective-permute-start.2 = (bf16[128,1152]{1,0:T(8,128)(2,1)}, bf16[128,1152]{1,0:T(8,128)(2,1)}, u32[]{:S(2)}, u32[]{:S(2)}) collective-permute-start(bf16[128,1152]{1,0:T(8,128)(2,1)} %get-tuple-element.13), channel_id=1, source_target_pairs={{0,3},{1,2},{2,1},{3,0},{4,7},{5,6},{6,5},{7,4},{8,11},{9,10},{10,... | collective-permute-start | bytes 884744 | tf_op jit(solution)/shard_map/ppermute | solution.py:181
  33.2 55.8 %all-to-all-start.1 = ((bf16[16,128,768]{2,1,0:T(8,128)(2,1)}), bf16[16,128,768]{2,1,0:T(8,128)(2,1)S(1)}, u32[]{:S(2)}, u32[]{:S(2)}) async-start(bf16[16,128,768]{2,1,0:T(8,128)(2,1)} %spread.1), calls=%async_computation.1 | async-start | bytes 6291456 | tf_op jit(solution)/shard_map/all_to_all | solution.py:193
  40.2 21.4 %copy-start.1 = (bf16[128,1152]{1,0:T(8,128)(2,1)}, bf16[128,1152]{1,0:T(8,128)(2,1)S(1)}, u32[]{:S(2)}) copy-start(bf16[128,1152]{1,0:T(8,128)(2,1)S(1)} %collective-permute-done.p1) | copy-start | bytes 884740
  89.0 1.5 %copy-start = (f32[512,896]{1,0:T(8,128)S(1)}, f32[512,896]{1,0:T(8,128)}, u32[]{:S(2)}) copy-start(f32[512,896]{1,0:T(8,128)} %attend_fresh.1.carry_ref) | copy-start | bytes 5505028

commit v7 on v5

--- a/solution.py
+++ b/solution.py
@@ -16,9 +16,10 @@
 NT = (((1,), (1,)), ((), ()))
 F32 = jnp.float32
 LIMIT = 60 << 20
-SPREAD_LIMIT = 48 << 20
+SPREAD_LIMIT = 55 << 20
 ATTEND_LIMIT = 48 << 20
-FRESH_COST = 60 << 30
+FRESH_COST = 1 << 30
+ARRIVE_COST = 60 << 30
 BF16 = jnp.bfloat16
 ANY = pl.BlockSpec(memory_space=pl.ANY)
 VMEM = pl.BlockSpec(memory_space=pltpu.VMEM)
@@ -50,12 +51,16 @@
             part[:, t * mine : (t + 1) * mine] = ref[:, cols]
 
 
-def spread(line_ref, near_ref, out_ref, same_ref, sem):
+def spread(line_ref, other_ref, out_ref, same_ref, sem):
     copies = [pltpu.make_async_copy(line_ref, out_ref.at[j], sem.at[j]) for j in range(out_ref.shape[0])]
     for c in copies:
         c.start()
     for c in copies:
         c.wait()
+
+
+def arrive(near_ref, same_ref, near_out, same_out):
+    pass
 
 
 def attend_fresh(p0, p1, p2, p3, carry_ref, q_ref, keys_ref, values_ref, sem):
@@ -176,10 +181,10 @@
         cost_estimate=pl.CostEstimate(flops=0, bytes_accessed=3 << 20, transcendentals=0),
         name="pack",
     )(q_fresh, k_fresh, v_fresh, k_stale, v_stale)
+    near = lax.ppermute(near, EVERY, flips(0, 1))
     same = lax.ppermute(same, EVERY, flips(1, 0))
-    other = lax.ppermute(other, EVERY, flips(1, 1))
     line = lax.all_to_all(copies, "zl", split_axis=0, concat_axis=0).reshape(8 * pooled, 2 * mine)
-    planes, near = pl.pallas_call(
+    planes, other = pl.pallas_call(
         spread,
         out_shape=(jax.ShapeDtypeStruct((16, 8 * pooled, 2 * mine), BF16), part),
         in_specs=[VMEM, ANY],
@@ -189,8 +194,18 @@
         compiler_params=pltpu.CompilerParams(vmem_limit_bytes=SPREAD_LIMIT),
         cost_estimate=pl.CostEstimate(flops=0, bytes_accessed=3 << 20, transcendentals=0),
         name="spread",
-    )(line, near)
-    near = lax.ppermute(near, EVERY, flips(0, 1))
+    )(line, other)
+    other = lax.ppermute(other, EVERY, flips(1, 1))
+    near, same = pl.pallas_call(
+        arrive,
+        out_shape=(part, part),
+        in_specs=[ANY, ANY],
+        out_specs=(ANY, ANY),
+        input_output_aliases={0: 0, 1: 1},
+        compiler_params=pltpu.CompilerParams(vmem_limit_bytes=LIMIT),
+        cost_estimate=pl.CostEstimate(flops=ARRIVE_COST, bytes_accessed=0, transcendentals=0),
+        name="arrive",
+    )(near, same)
     pool = lax.all_to_all(planes, ("y", "x"), split_axis=0, concat_axis=0)
 
     fresh = 4 * tokens

time: 164 us -> 126 us (0.77)
  the two profiles are of different devices: /device:TPU:32 before, /device:TPU:65 now
where the time goes in v7:
time: 126 us
  waiting for transfers between devices  40.4 us (32%)
  starting transfers between devices  40.1 us (32%)
  blocking collectives  24 us (19%)
  Pallas kernels  17.1 us (14%)
  local copies, waits for them, and re-layouts  4.04 us (3%)
    ppermute x1, waiting for transfers between devices, local(): other = lax.ppermute(other, EVERY, flips(1, 1))  40.2 us
    all_to_all x1, blocking collectives, local(): back = lax.all_to_all(out, ('zh', 'core'), split_axis=0, concat_axis=0)  24 us
    all_to_all x1, starting transfers between devices, local(): lax.all_to_all(copies, 'zl', split_axis=0, concat_axis=0)  11.6 us
    ppermute x1, starting transfers between devices, local(): other = lax.ppermute(other, EVERY, flips(1, 1))  10.5 us
    ppermute x1, starting transfers between devices, local(): same = lax.ppermute(same, EVERY, flips(1, 0))  7.94 us
    all_to_all x1, starting transfers between devices, local(): pool = lax.all_to_all(planes, ('y', 'x'), split_axis=0, concat_axis=0)  6.9 us
    pallas_call x1, Pallas kernels, local(): pl.pallas_call(attend_fresh, out_shape=carry, in_specs=[ANY] * 4, scratch...  6.45 us
    pallas_call x1, Pallas kernels, local(): pl.pallas_call(attend, out_shape=jax.ShapeDtypeStruct((4, tokens, mine),...  5.54 us
  transfers between devices with their start and end apart: 5, of which 2 were waited for; matrix products, arithmetic and copies ran while one was open for 0% of the time, Pallas kernels for 7%

profile of v7, /device:TPU:65, one launch (start us, length us, event | category | flops | bytes accessed | tf_op | source)
XLA Modules:
  0.0 125.7 jit_solution(2447541043958708341)
XLA Ops:
  0.0 2.4 %pack.1 = (bf16[128,1152]{1,0:T(8,128)(2,1)}, bf16[128,1152]{1,0:T(8,128)(2,1)}, bf16[128,1152]{1,0:T(8,128)(2,1)}, bf16[128,1152]{1,0:T(8,128)(2,1)}, bf16[8,16,768]{2,1,0:T(8,128)(2,1)}) custom-call(bf16[128,1536]{1,0:T(8,128)(2,1)} %qa.1, bf16[128,1536]{1,0:T(8,128)(2,1)} %ka.1, bf16[128,1536]{1,0:T(8,128)(2,1)} %va.1, bf16[16,384]{1,0:T(8,128)(2,1)} %ksa.1, ...), custom_call_target="tpu_custom_call" | custom-call | bytes 3145728 | tf_op jit(solution)/shard_map/pack/pallas_call | solution.py:174
  2.4 11.6 %all-to-all-start = ((bf16[8,16,768]{2,1,0:T(8,128)(2,1)}), bf16[8,16,768]{2,1,0:T(8,128)(2,1)S(1)}, u32[]{:S(2)}, u32[]{:S(2)}) async-start(bf16[8,16,768]{2,1,0:T(8,128)(2,1)} %get-tuple-element.19), calls=%async_computation | async-start | bytes 393216 | tf_op jit(solution)/shard_map/all_to_all | solution.py:186
  14.0 3.1 %collective-permute-start = (bf16[128,1152]{1,0:T(8,128)(2,1)}, bf16[128,1152]{1,0:T(8,128)(2,1)}, u32[]{:S(2)}, u32[]{:S(2)}) collective-permute-start(bf16[128,1152]{1,0:T(8,128)(2,1)} %get-tuple-element.15), channel_id=1, source_target_pairs={{0,1},{1,0},{2,3},{3,2},{4,5},{5,4},{6,7},{7,6},{8,9},{9,8},{10,11... | collective-permute-start | bytes 884744 | tf_op jit(solution)/shard_map/ppermute | solution.py:184
  17.2 7.9 %collective-permute-start.1 = (bf16[128,1152]{1,0:T(8,128)(2,1)}, bf16[128,1152]{1,0:T(8,128)(2,1)}, u32[]{:S(2)}, u32[]{:S(2)}) collective-permute-start(bf16[128,1152]{1,0:T(8,128)(2,1)} %get-tuple-element.16), channel_id=1, source_target_pairs={{0,2},{1,3},{2,0},{3,1},{4,6},{5,7},{6,4},{7,5},{8,10},{9,11},{10,... | collective-permute-start | bytes 884744 | tf_op jit(solution)/shard_map/ppermute | solution.py:185
  25.1 0.2 all-to-all-done
  25.3 0.0 copy-start.1
  25.3 0.7 copy-done.1
  26.0 2.7 %spread.1 = (bf16[16,128,768]{2,1,0:T(8,128)(2,1)}, bf16[128,1152]{1,0:T(8,128)(2,1)}) custom-call(bf16[128,768]{1,0:T(8,128)(2,1)} %bitcast.5, bf16[128,1152]{1,0:T(8,128)(2,1)} %get-tuple-element.20.other_ref), custom_call_target="tpu_custom_call", output_to_operand_aliasing={{1}: (1, {})} | custom-call | bytes 3145728 | tf_op jit(solution)/shard_map/spread/pallas_call | solution.py:187
  28.7 0.0 copy-start.2
  28.7 6.9 %all-to-all-start.1 = ((bf16[16,128,768]{2,1,0:T(8,128)(2,1)}), bf16[16,128,768]{2,1,0:T(8,128)(2,1)S(1)}, u32[]{:S(2)}, u32[]{:S(2)}) async-start(bf16[16,128,768]{2,1,0:T(8,128)(2,1)} %get-tuple-element.22), calls=%async_computation.1 | async-start | bytes 6291456 | tf_op jit(solution)/shard_map/all_to_all | solution.py:209
  35.6 0.0 copy-done.2
  35.6 10.5 %collective-permute-start.2 = (bf16[128,1152]{1,0:T(8,128)(2,1)S(1)}, bf16[128,1152]{1,0:T(8,128)(2,1)S(1)}, u32[]{:S(2)}, u32[]{:S(2)}) collective-permute-start(bf16[128,1152]{1,0:T(8,128)(2,1)S(1)} %copy-done.2), channel_id=1, source_target_pairs={{0,3},{1,2},{2,1},{3,0},{4,7},{5,6},{6,5},{7,4},{8,11},{9,10},{10,... | collective-permute-start | bytes 884744 | tf_op jit(solution)/shard_map/ppermute | solution.py:198
  46.1 0.0 collective-permute-done.near_ref
  46.1 0.0 collective-permute-done.1.same_ref
  46.2 40.2 %collective-permute-done.2.p3 = bf16[128,1152]{1,0:T(8,128)(2,1)S(1)} collective-permute-done((bf16[128,1152]{1,0:T(8,128)(2,1)S(1)}, bf16[128,1152]{1,0:T(8,128)(2,1)S(1)}, u32[]{:S(2)}, u32[]{:S(2)}) %collective-permute-start.2) | collective-permute-done | bytes 294944 | tf_op jit(solution)/shard_map/ppermute | solution.py:198
  86.4 0.7 copy-done.3
  87.1 6.4 %attend_fresh.1.carry_ref = f32[512,896]{1,0:T(8,128)} custom-call(bf16[128,1152]{1,0:T(8,128)(2,1)} %get-tuple-element.14.p0, bf16[128,1152]{1,0:T(8,128)(2,1)} %get-tuple-element.17.p1, bf16[128,1152]{1,0:T(8,128)(2,1)} %get-tuple-element.18.p2, bf16[128,1152]{1,0:T(8,128)(2,1)} %copy-done.3), custom_call_target="tpu_custom_call" | custom-call | flops 1073741824 | bytes 3145728 | tf_op jit(solution)/shard_map/attend_fresh/pallas_call | solution.py:213
  93.5 0.0 all-to-all-done.1.pool_ref
  93.5 0.0 copy-start
  93.6 1.5 %copy-done = f32[512,896]{1,0:T(8,128)S(1)} copy-done((f32[512,896]{1,0:T(8,128)S(1)}, f32[512,896]{1,0:T(8,128)}, u32[]{:S(2)}) %copy-start) | copy-done | bytes 1835032
  95.0 5.5 %attend.1 = bf16[4,128,384]{2,1,0:T(8,128)(2,1)S(1)} custom-call(f32[512,896]{1,0:T(8,128)S(1)} %copy-done, bf16[16,128,768]{2,1,0:T(8,128)(2,1)S(1)} %all-to-all-done.1.pool_ref), custom_call_target="tpu_custom_call" | custom-call | flops 1610612736 | bytes 6291456 | tf_op jit(solution)/shard_map/attend/pallas_call | solution.py:223
  100.6 24.0 %all_to_all.15 = bf16[4,128,384]{2,1,0:T(8,128)(2,1)S(1)} all-to-all(bf16[4,128,384]{2,1,0:T(8,128)(2,1)S(1)} %attend.1), channel_id=1, replica_groups=mesh['y'=4,'x'=4,'zl'=8,'zh'=2,'core'=2] {'zh','core'}, dimensions={0} | all-to-all | bytes 786432 | tf_op jit(solution)/shard_map/all_to_all | solution.py:237
  124.5 0.2 copy.9
  124.8 0.9 copy.10
  (2 shorter events, 0.0 us)
Async XLA Ops:
  2.4 22.9 %all-to-all-start = ((bf16[8,16,768]{2,1,0:T(8,128)(2,1)}), bf16[8,16,768]{2,1,0:T(8,128)(2,1)S(1)}, u32[]{:S(2)}, u32[]{:S(2)}) async-start(bf16[8,16,768]{2,1,0:T(8,128)(2,1)} %get-tuple-element.19), calls=%async_computation | async-start | bytes 393216 | tf_op jit(solution)/shard_map/all_to_all | solution.py:186
  14.0 32.1 %collective-permute-start = (bf16[128,1152]{1,0:T(8,128)(2,1)}, bf16[128,1152]{1,0:T(8,128)(2,1)}, u32[]{:S(2)}, u32[]{:S(2)}) collective-permute-start(bf16[128,1152]{1,0:T(8,128)(2,1)} %get-tuple-element.15), channel_id=1, source_target_pairs={{0,1},{1,0},{2,3},{3,2},{4,5},{5,4},{6,7},{7,6},{8,9},{9,8},{10,11... | collective-permute-start | bytes 884744 | tf_op jit(solution)/shard_map/ppermute | solution.py:184
  17.2 29.0 %collective-permute-start.1 = (bf16[128,1152]{1,0:T(8,128)(2,1)}, bf16[128,1152]{1,0:T(8,128)(2,1)}, u32[]{:S(2)}, u32[]{:S(2)}) collective-permute-start(bf16[128,1152]{1,0:T(8,128)(2,1)} %get-tuple-element.16), channel_id=1, source_target_pairs={{0,2},{1,3},{2,0},{3,1},{4,6},{5,7},{6,4},{7,5},{8,10},{9,11},{10,... | collective-permute-start | bytes 884744 | tf_op jit(solution)/shard_map/ppermute | solution.py:185
  25.3 0.7 copy-start.1
  28.7 6.9 %copy-start.2 = (bf16[128,1152]{1,0:T(8,128)(2,1)S(1)}, bf16[128,1152]{1,0:T(8,128)(2,1)}, u32[]{:S(2)}) copy-start(bf16[128,1152]{1,0:T(8,128)(2,1)} %get-tuple-element.21) | copy-start | bytes 884740
  28.7 64.8 %all-to-all-start.1 = ((bf16[16,128,768]{2,1,0:T(8,128)(2,1)}), bf16[16,128,768]{2,1,0:T(8,128)(2,1)S(1)}, u32[]{:S(2)}, u32[]{:S(2)}) async-start(bf16[16,128,768]{2,1,0:T(8,128)(2,1)} %get-tuple-element.22), calls=%async_computation.1 | async-start | bytes 6291456 | tf_op jit(solution)/shard_map/all_to_all | solution.py:209
  35.6 50.7 %collective-permute-start.2 = (bf16[128,1152]{1,0:T(8,128)(2,1)S(1)}, bf16[128,1152]{1,0:T(8,128)(2,1)S(1)}, u32[]{:S(2)}, u32[]{:S(2)}) collective-permute-start(bf16[128,1152]{1,0:T(8,128)(2,1)S(1)} %copy-done.2), channel_id=1, source_target_pairs={{0,3},{1,2},{2,1},{3,0},{4,7},{5,6},{6,5},{7,4},{8,11},{9,10},{10,... | collective-permute-start | bytes 884744 | tf_op jit(solution)/shard_map/ppermute | solution.py:198
  86.4 0.7 copy-start.3
  93.5 1.5 %copy-start = (f32[512,896]{1,0:T(8,128)S(1)}, f32[512,896]{1,0:T(8,128)}, u32[]{:S(2)}) copy-start(f32[512,896]{1,0:T(8,128)} %attend_fresh.1.carry_ref) | copy-start | bytes 5505028

commit v8 on v7

--- a/solution.py
+++ b/solution.py
@@ -16,7 +16,7 @@
 NT = (((1,), (1,)), ((), ()))
 F32 = jnp.float32
 LIMIT = 60 << 20
-SPREAD_LIMIT = 55 << 20
+SPREAD_LIMIT = 48 << 20
 ATTEND_LIMIT = 48 << 20
 FRESH_COST = 1 << 30
 ARRIVE_COST = 60 << 30
@@ -51,7 +51,7 @@
             part[:, t * mine : (t + 1) * mine] = ref[:, cols]
 
 
-def spread(line_ref, other_ref, out_ref, same_ref, sem):
+def spread(line_ref, out_ref, sem):
     copies = [pltpu.make_async_copy(line_ref, out_ref.at[j], sem.at[j]) for j in range(out_ref.shape[0])]
     for c in copies:
         c.start()
@@ -59,43 +59,67 @@
         c.wait()
 
 
+def follow(first_ref, ref, out_ref):
+    pass
+
+
 def arrive(near_ref, same_ref, near_out, same_out):
     pass
 
 
-def attend_fresh(p0, p1, p2, p3, carry_ref, q_ref, keys_ref, values_ref, sem):
-    tokens, mine = q_ref.shape[1:]
-    loads = []
-    for i, ref in enumerate((p0, p1, p2, p3)):
+def attend_fresh(p0, p1, p2, p3, out_ref, part_ref, carry_ref, s_ref, sem, sem_o):
+    tokens = part_ref.shape[1]
+    mine = part_ref.shape[2] // 3
+    heads = mine // HD
+    loads = [pltpu.make_async_copy(ref, part_ref.at[i], sem.at[i]) for i, ref in enumerate((p0, p1, p2, p3))]
+    stores = []
+    for i in range(4):
         rows = pl.ds(i * tokens, tokens)
-        for t, to in enumerate((q_ref.at[i], keys_ref.at[rows], values_ref.at[rows])):
-            loads.append(pltpu.make_async_copy(ref.at[:, t * mine : (t + 1) * mine], to, sem.at[3 * i + t]))
+        stores.append(pltpu.make_async_copy(carry_ref.at[rows], out_ref.at[rows], sem_o.at[i]))
     for c in loads:
         c.start()
+    lane = lax.broadcasted_iota(jnp.int32, (tokens, HD), 1)
+    steps = [(h, i) for i in range(4) for h in range(heads)]
+    tops, stats = {}, {}
+
+    def scores(n):
+        h, i = steps[n]
+        q = part_ref[i, :, h * HD : (h + 1) * HD]
+        top = jnp.full((tokens, HD), -jnp.inf, F32)
+        keys = part_ref[:, :, mine + h * HD : mine + (h + 1) * HD].reshape(4 * tokens, HD)
+        s = lax.dot_general(q, keys, NT, preferred_element_type=F32)
+        s_ref[n % 2] = s
+        for d in range(0, 4 * tokens, HD):
+            top = jnp.maximum(top, s[:, d : d + HD])
+        tops[n] = jnp.max(top, axis=1, keepdims=True)
+        carry_ref[i * tokens : (i + 1) * tokens, h * HD : (h + 1) * HD] = q.astype(F32)
+
+    def weigh(n):
+        h, i = steps[n]
+        rows = slice(i * tokens, (i + 1) * tokens)
+        top = tops.pop(n)
+        w = jnp.exp2(s_ref[n % 2] * SCALE - top * SCALE)
+        sums = jnp.zeros((tokens, HD), F32)
+        for d in range(0, 4 * tokens, HD):
+            sums = sums + w[:, d : d + HD]
+        values = part_ref[:, :, 2 * mine + h * HD : 2 * mine + (h + 1) * HD].reshape(4 * tokens, HD)
+        acc = jnp.dot(w.astype(BF16), values, preferred_element_type=F32)
+        carry_ref[rows, mine + h * HD : mine + (h + 1) * HD] = acc
+        stat = jnp.where(lane == 2 * h, top, stats.get(i, 0.0))
+        stats[i] = jnp.where(lane == 2 * h + 1, jnp.sum(sums, axis=1, keepdims=True), stat)
+        if h == heads - 1:
+            carry_ref[rows, 2 * mine :] = stats.pop(i)
+            stores[i].start()
+
     for c in loads:
         c.wait()
-    lane = lax.broadcasted_iota(jnp.int32, (tokens, HD), 1)
-    heads = mine // HD
-
-    def rows_step(i, carry):
-        stat = jnp.zeros((tokens, HD), F32)
-        rows = pl.ds(pl.multiple_of(i * tokens, tokens), tokens)
-        for h in range(heads):
-            cs = slice(h * HD, (h + 1) * HD)
-            q = q_ref[i, :, cs]
-            s = lax.dot_general(q, keys_ref[:, cs], NT, preferred_element_type=F32)
-            top = jnp.max(s, axis=1, keepdims=True)
-            w = jnp.exp2(s * SCALE - top * SCALE)
-            carry_ref[rows, cs] = q.astype(F32)
-            carry_ref[rows, mine + h * HD : mine + (h + 1) * HD] = jnp.dot(
-                w.astype(BF16), values_ref[:, cs], preferred_element_type=F32
-            )
-            stat = jnp.where(lane == 2 * h, top, stat)
-            stat = jnp.where(lane == 2 * h + 1, jnp.sum(w, axis=1, keepdims=True), stat)
-        carry_ref[rows, 2 * mine :] = stat
-        return carry
-
-    lax.fori_loop(0, 4, rows_step, 0)
+    scores(0)
+    for n in range(len(steps)):
+        if n + 1 < len(steps):
+            scores(n + 1)
+        weigh(n)
+    for c in stores:
+        c.wait()
 
 
 def attend(carry_ref, pool_ref, out_ref, s_ref):
@@ -184,17 +208,26 @@
     near = lax.ppermute(near, EVERY, flips(0, 1))
     same = lax.ppermute(same, EVERY, flips(1, 0))
     line = lax.all_to_all(copies, "zl", split_axis=0, concat_axis=0).reshape(8 * pooled, 2 * mine)
-    planes, other = pl.pallas_call(
+    planes = pl.pallas_call(
         spread,
-        out_shape=(jax.ShapeDtypeStruct((16, 8 * pooled, 2 * mine), BF16), part),
-        in_specs=[VMEM, ANY],
-        out_specs=(ANY, ANY),
+        out_shape=jax.ShapeDtypeStruct((16, 8 * pooled, 2 * mine), BF16),
+        in_specs=[VMEM],
+        out_specs=ANY,
         scratch_shapes=[dma((16,))],
-        input_output_aliases={1: 1},
         compiler_params=pltpu.CompilerParams(vmem_limit_bytes=SPREAD_LIMIT),
         cost_estimate=pl.CostEstimate(flops=0, bytes_accessed=3 << 20, transcendentals=0),
         name="spread",
-    )(line, other)
+    )(line)
+    other = pl.pallas_call(
+        follow,
+        out_shape=part,
+        in_specs=[ANY, ANY],
+        out_specs=ANY,
+        input_output_aliases={1: 0},
+        compiler_params=pltpu.CompilerParams(vmem_limit_bytes=LIMIT),
+        cost_estimate=pl.CostEstimate(flops=0, bytes_accessed=0, transcendentals=0),
+        name="follow",
+    )(planes, other)
     other = lax.ppermute(other, EVERY, flips(1, 1))
     near, same = pl.pallas_call(
         arrive,
@@ -214,7 +247,14 @@
         attend_fresh,
         out_shape=carry,
         in_specs=[ANY] * 4,
-        scratch_shapes=[pltpu.VMEM((4, tokens, mine), BF16)] + [pltpu.VMEM((fresh, mine), BF16)] * 2 + [dma((12,))],
+        out_specs=ANY,
+        scratch_shapes=[
+            pltpu.VMEM((4, tokens, 3 * mine), BF16),
+            pltpu.VMEM(carry.shape, F32),
+            pltpu.VMEM((2, tokens, fresh), F32),
+            dma((4,)),
+            dma((4,)),
+        ],
         compiler_params=pltpu.CompilerParams(vmem_limit_bytes=LIMIT),
         cost_estimate=pl.CostEstimate(flops=FRESH_COST, bytes_accessed=3 << 20, transcendentals=0),
         name="attend_fresh",

time: 126 us -> 126 us (level)
  the two profiles are of different devices: /device:TPU:65 before, /device:TPU:95 now
where the time goes in v8:
time: 126 us; the launch traced here: 125 us
  starting transfers between devices  40 us (32%)
  waiting for transfers between devices  34.9 us (28%)
  blocking collectives  32.2 us (26%)
  Pallas kernels  13.9 us (11%)
  local copies, waits for them, and re-layouts  4.09 us (3%)
    ppermute x1, waiting for transfers between devices, local(): other = lax.ppermute(other, EVERY, flips(1, 1))  34.7 us
    all_to_all x1, blocking collectives, local(): back = lax.all_to_all(out, ('zh', 'core'), split_axis=0, concat_axis=0)  32.2 us
    all_to_all x1, starting transfers between devices, local(): lax.all_to_all(copies, 'zl', split_axis=0, concat_axis=0)  11.6 us
    ppermute x1, starting transfers between devices, local(): other = lax.ppermute(other, EVERY, flips(1, 1))  10.8 us
    ppermute x1, starting transfers between devices, local(): same = lax.ppermute(same, EVERY, flips(1, 0))  7.94 us
    all_to_all x1, starting transfers between devices, local(): pool = lax.all_to_all(planes, ('y', 'x'), split_axis=0, concat_axis=0)  6.54 us
    pallas_call x1, Pallas kernels, local(): pl.pallas_call(attend, out_shape=jax.ShapeDtypeStruct((4, tokens, mine),...  5.53 us
    pallas_call x1, Pallas kernels, local(): pl.pallas_call(attend_fresh, out_shape=carry, in_specs=[ANY] * 4, out_spe...  4.16 us
  transfers between devices with their start and end apart: 5, of which 2 were waited for; matrix products, arithmetic and copies ran while one was open for 0% of the time, Pallas kernels for 5%

profile of v8, /device:TPU:95, one launch (start us, length us, event | category | flops | bytes accessed | tf_op | source)
XLA Modules:
  0.0 125.1 jit_solution(4940965470544337376)
XLA Ops:
  0.0 2.4 %pack.1 = (bf16[128,1152]{1,0:T(8,128)(2,1)}, bf16[128,1152]{1,0:T(8,128)(2,1)}, bf16[128,1152]{1,0:T(8,128)(2,1)}, bf16[128,1152]{1,0:T(8,128)(2,1)}, bf16[8,16,768]{2,1,0:T(8,128)(2,1)}) custom-call(bf16[128,1536]{1,0:T(8,128)(2,1)} %qa.1, bf16[128,1536]{1,0:T(8,128)(2,1)} %ka.1, bf16[128,1536]{1,0:T(8,128)(2,1)} %va.1, bf16[16,384]{1,0:T(8,128)(2,1)} %ksa.1, ...), custom_call_target="tpu_custom_call" | custom-call | bytes 3145728 | tf_op jit(solution)/shard_map/pack/pallas_call | solution.py:198
  2.4 11.6 %all-to-all-start = ((bf16[8,16,768]{2,1,0:T(8,128)(2,1)}), bf16[8,16,768]{2,1,0:T(8,128)(2,1)S(1)}, u32[]{:S(2)}, u32[]{:S(2)}) async-start(bf16[8,16,768]{2,1,0:T(8,128)(2,1)} %get-tuple-element.17), calls=%async_computation | async-start | bytes 393216 | tf_op jit(solution)/shard_map/all_to_all | solution.py:210
  14.0 3.1 %collective-permute-start = (bf16[128,1152]{1,0:T(8,128)(2,1)}, bf16[128,1152]{1,0:T(8,128)(2,1)S(1)}, u32[]{:S(2)}, u32[]{:S(2)}) collective-permute-start(bf16[128,1152]{1,0:T(8,128)(2,1)} %get-tuple-element.13), channel_id=1, source_target_pairs={{0,1},{1,0},{2,3},{3,2},{4,5},{5,4},{6,7},{7,6},{8,9},{9,8},{10,11... | collective-permute-start | bytes 884744 | tf_op jit(solution)/shard_map/ppermute | solution.py:208
  17.2 7.9 %collective-permute-start.1 = (bf16[128,1152]{1,0:T(8,128)(2,1)}, bf16[128,1152]{1,0:T(8,128)(2,1)}, u32[]{:S(2)}, u32[]{:S(2)}) collective-permute-start(bf16[128,1152]{1,0:T(8,128)(2,1)} %get-tuple-element.14), channel_id=1, source_target_pairs={{0,2},{1,3},{2,0},{3,1},{4,6},{5,7},{6,4},{7,5},{8,10},{9,11},{10,... | collective-permute-start | bytes 884744 | tf_op jit(solution)/shard_map/ppermute | solution.py:209
  25.1 0.2 all-to-all-done
  25.3 1.8 %spread.1.first_ref = bf16[16,128,768]{2,1,0:T(8,128)(2,1)} custom-call(bf16[128,768]{1,0:T(8,128)(2,1)S(1)} %bitcast.3), custom_call_target="tpu_custom_call" | custom-call | bytes 3145728 | tf_op jit(solution)/shard_map/spread/pallas_call | solution.py:211
  27.1 6.5 %all-to-all-start.1 = ((bf16[16,128,768]{2,1,0:T(8,128)(2,1)}), bf16[16,128,768]{2,1,0:T(8,128)(2,1)S(1)}, u32[]{:S(2)}, u32[]{:S(2)}) async-start(bf16[16,128,768]{2,1,0:T(8,128)(2,1)} %spread.1.first_ref), calls=%async_computation.1 | async-start | bytes 6291456 | tf_op jit(solution)/shard_map/all_to_all | solution.py:242
  33.6 10.8 %collective-permute-start.2 = (bf16[128,1152]{1,0:T(8,128)(2,1)}, bf16[128,1152]{1,0:T(8,128)(2,1)S(1)}, u32[]{:S(2)}, u32[]{:S(2)}) collective-permute-start(bf16[128,1152]{1,0:T(8,128)(2,1)} %follow.1), channel_id=1, source_target_pairs={{0,3},{1,2},{2,1},{3,0},{4,7},{5,6},{6,5},{7,4},{8,11},{9,10},{10,... | collective-permute-start | bytes 884744 | tf_op jit(solution)/shard_map/ppermute | solution.py:231
  44.4 0.0 collective-permute-done.near_ref
  44.4 0.0 copy-start.1
  44.4 0.0 collective-permute-done.1.same_ref
  44.4 0.7 copy-done.1
  45.2 34.7 %collective-permute-done.2.p3 = bf16[128,1152]{1,0:T(8,128)(2,1)S(1)} collective-permute-done((bf16[128,1152]{1,0:T(8,128)(2,1)}, bf16[128,1152]{1,0:T(8,128)(2,1)S(1)}, u32[]{:S(2)}, u32[]{:S(2)}) %collective-permute-start.2) | collective-permute-done | bytes 294944 | tf_op jit(solution)/shard_map/ppermute | solution.py:231
  79.8 0.0 copy-start.2
  79.8 0.7 copy-done.2
  80.5 4.2 %attend_fresh.1.carry_ref = f32[512,896]{1,0:T(8,128)} custom-call(bf16[128,1152]{1,0:T(8,128)(2,1)} %get-tuple-element.12.p0, bf16[128,1152]{1,0:T(8,128)(2,1)} %get-tuple-element.15.p1, bf16[128,1152]{1,0:T(8,128)(2,1)} %get-tuple-element.16.p2, bf16[128,1152]{1,0:T(8,128)(2,1)} %copy-done.2), custom_call_target="tpu_custom_call" | custom-call | flops 1073741824 | bytes 3145728 | tf_op jit(solution)/shard_map/attend_fresh/pallas_call | solution.py:246
  84.7 0.0 all-to-all-done.1.pool_ref
  84.7 0.0 copy-start
  84.7 1.5 %copy-done = f32[512,896]{1,0:T(8,128)S(1)} copy-done((f32[512,896]{1,0:T(8,128)S(1)}, f32[512,896]{1,0:T(8,128)}, u32[]{:S(2)}) %copy-start) | copy-done | bytes 1835032
  86.2 5.5 %attend.1 = bf16[4,128,384]{2,1,0:T(8,128)(2,1)S(1)} custom-call(f32[512,896]{1,0:T(8,128)S(1)} %copy-done, bf16[16,128,768]{2,1,0:T(8,128)(2,1)S(1)} %all-to-all-done.1.pool_ref), custom_call_target="tpu_custom_call" | custom-call | flops 1610612736 | bytes 6291456 | tf_op jit(solution)/shard_map/attend/pallas_call | solution.py:263
  91.8 32.2 %all_to_all.15 = bf16[4,128,384]{2,1,0:T(8,128)(2,1)S(1)} all-to-all(bf16[4,128,384]{2,1,0:T(8,128)(2,1)S(1)} %attend.1), channel_id=1, replica_groups=mesh['y'=4,'x'=4,'zl'=8,'zh'=2,'core'=2] {'zh','core'}, dimensions={0} | all-to-all | bytes 786432 | tf_op jit(solution)/shard_map/all_to_all | solution.py:277
  123.9 0.2 copy.9
  124.2 0.9 copy.10
  (2 shorter events, 0.0 us)
Async XLA Ops:
  2.4 22.9 %all-to-all-start = ((bf16[8,16,768]{2,1,0:T(8,128)(2,1)}), bf16[8,16,768]{2,1,0:T(8,128)(2,1)S(1)}, u32[]{:S(2)}, u32[]{:S(2)}) async-start(bf16[8,16,768]{2,1,0:T(8,128)(2,1)} %get-tuple-element.17), calls=%async_computation | async-start | bytes 393216 | tf_op jit(solution)/shard_map/all_to_all | solution.py:210
  14.0 30.4 %collective-permute-start = (bf16[128,1152]{1,0:T(8,128)(2,1)}, bf16[128,1152]{1,0:T(8,128)(2,1)S(1)}, u32[]{:S(2)}, u32[]{:S(2)}) collective-permute-start(bf16[128,1152]{1,0:T(8,128)(2,1)} %get-tuple-element.13), channel_id=1, source_target_pairs={{0,1},{1,0},{2,3},{3,2},{4,5},{5,4},{6,7},{7,6},{8,9},{9,8},{10,11... | collective-permute-start | bytes 884744 | tf_op jit(solution)/shard_map/ppermute | solution.py:208
  17.2 27.3 %collective-permute-start.1 = (bf16[128,1152]{1,0:T(8,128)(2,1)}, bf16[128,1152]{1,0:T(8,128)(2,1)}, u32[]{:S(2)}, u32[]{:S(2)}) collective-permute-start(bf16[128,1152]{1,0:T(8,128)(2,1)} %get-tuple-element.14), channel_id=1, source_target_pairs={{0,2},{1,3},{2,0},{3,1},{4,6},{5,7},{6,4},{7,5},{8,10},{9,11},{10,... | collective-permute-start | bytes 884744 | tf_op jit(solution)/shard_map/ppermute | solution.py:209
  27.1 57.6 %all-to-all-start.1 = ((bf16[16,128,768]{2,1,0:T(8,128)(2,1)}), bf16[16,128,768]{2,1,0:T(8,128)(2,1)S(1)}, u32[]{:S(2)}, u32[]{:S(2)}) async-start(bf16[16,128,768]{2,1,0:T(8,128)(2,1)} %spread.1.first_ref), calls=%async_computation.1 | async-start | bytes 6291456 | tf_op jit(solution)/shard_map/all_to_all | solution.py:242
  33.6 46.2 %collective-permute-start.2 = (bf16[128,1152]{1,0:T(8,128)(2,1)}, bf16[128,1152]{1,0:T(8,128)(2,1)S(1)}, u32[]{:S(2)}, u32[]{:S(2)}) collective-permute-start(bf16[128,1152]{1,0:T(8,128)(2,1)} %follow.1), channel_id=1, source_target_pairs={{0,3},{1,2},{2,1},{3,0},{4,7},{5,6},{6,5},{7,4},{8,11},{9,10},{10,... | collective-permute-start | bytes 884744 | tf_op jit(solution)/shard_map/ppermute | solution.py:231
  44.4 0.7 copy-start.1
  79.8 0.7 copy-start.2
  84.7 1.5 %copy-start = (f32[512,896]{1,0:T(8,128)S(1)}, f32[512,896]{1,0:T(8,128)}, u32[]{:S(2)}) copy-start(f32[512,896]{1,0:T(8,128)} %attend_fresh.1.carry_ref) | copy-start | bytes 5505028

commit v9 on v8

--- a/solution.py
+++ b/solution.py
@@ -18,8 +18,7 @@
 LIMIT = 60 << 20
 SPREAD_LIMIT = 48 << 20
 ATTEND_LIMIT = 48 << 20
-FRESH_COST = 1 << 30
-ARRIVE_COST = 60 << 30
+EARLY_COST = 60 << 30
 BF16 = jnp.bfloat16
 ANY = pl.BlockSpec(memory_space=pl.ANY)
 VMEM = pl.BlockSpec(memory_space=pltpu.VMEM)
@@ -63,33 +62,32 @@
     pass
 
 
-def arrive(near_ref, same_ref, near_out, same_out):
-    pass
-
-
-def attend_fresh(p0, p1, p2, p3, out_ref, part_ref, carry_ref, s_ref, sem, sem_o):
-    tokens = part_ref.shape[1]
+def attend_early(p0, p1, p2, out_ref, kv_ref, part_ref, carry_ref, s_ref, sem, sem_o):
+    parts, tokens = part_ref.shape[:2]
     mine = part_ref.shape[2] // 3
     heads = mine // HD
-    loads = [pltpu.make_async_copy(ref, part_ref.at[i], sem.at[i]) for i, ref in enumerate((p0, p1, p2, p3))]
+    loads = [pltpu.make_async_copy(ref, part_ref.at[i], sem.at[i]) for i, ref in enumerate((p0, p1, p2))]
     stores = []
-    for i in range(4):
+    for i in range(parts):
         rows = pl.ds(i * tokens, tokens)
         stores.append(pltpu.make_async_copy(carry_ref.at[rows], out_ref.at[rows], sem_o.at[i]))
+    for i in range(parts):
+        rows = pl.ds(i * tokens, tokens)
+        stores.append(pltpu.make_async_copy(part_ref.at[i, :, mine:], kv_ref.at[rows], sem_o.at[parts + i]))
     for c in loads:
         c.start()
     lane = lax.broadcasted_iota(jnp.int32, (tokens, HD), 1)
-    steps = [(h, i) for i in range(4) for h in range(heads)]
+    steps = [(h, i) for i in range(parts) for h in range(heads)]
     tops, stats = {}, {}
 
     def scores(n):
         h, i = steps[n]
         q = part_ref[i, :, h * HD : (h + 1) * HD]
         top = jnp.full((tokens, HD), -jnp.inf, F32)
-        keys = part_ref[:, :, mine + h * HD : mine + (h + 1) * HD].reshape(4 * tokens, HD)
+        keys = part_ref[:, :, mine + h * HD : mine + (h + 1) * HD].reshape(parts * tokens, HD)
         s = lax.dot_general(q, keys, NT, preferred_element_type=F32)
         s_ref[n % 2] = s
-        for d in range(0, 4 * tokens, HD):
+        for d in range(0, parts * tokens, HD):
             top = jnp.maximum(top, s[:, d : d + HD])
         tops[n] = jnp.max(top, axis=1, keepdims=True)
         carry_ref[i * tokens : (i + 1) * tokens, h * HD : (h + 1) * HD] = q.astype(F32)
@@ -100,9 +98,9 @@
         top = tops.pop(n)
         w = jnp.exp2(s_ref[n % 2] * SCALE - top * SCALE)
         sums = jnp.zeros((tokens, HD), F32)
-        for d in range(0, 4 * tokens, HD):
+        for d in range(0, parts * tokens, HD):
             sums = sums + w[:, d : d + HD]
-        values = part_ref[:, :, 2 * mine + h * HD : 2 * mine + (h + 1) * HD].reshape(4 * tokens, HD)
+        values = part_ref[:, :, 2 * mine + h * HD : 2 * mine + (h + 1) * HD].reshape(parts * tokens, HD)
         acc = jnp.dot(w.astype(BF16), values, preferred_element_type=F32)
         carry_ref[rows, mine + h * HD : mine + (h + 1) * HD] = acc
         stat = jnp.where(lane == 2 * h, top, stats.get(i, 0.0))
@@ -113,6 +111,8 @@
 
     for c in loads:
         c.wait()
+    for c in stores[parts:]:
+        c.start()
     scores(0)
     for n in range(len(steps)):
         if n + 1 < len(steps):
@@ -122,7 +122,7 @@
         c.wait()
 
 
-def attend(carry_ref, pool_ref, out_ref, s_ref):
+def attend(carry_ref, kv_ref, last_ref, pool_ref, out_ref, s_ref):
     tokens, mine = out_ref.shape[1:]
     heads = mine // HD
     blocks, block = pool_ref.shape[0], pool_ref.shape[1]
@@ -137,13 +137,19 @@
     def own(b):
         return (col >= first - b * block) & (col < first - b * block + block // 8)
 
+    def extra(h, i, t):
+        late = [last_ref[:, (1 + t) * mine + h * HD : (1 + t) * mine + (h + 1) * HD]]
+        early = [kv_ref[:, t * mine + h * HD : t * mine + (h + 1) * HD]]
+        return early + late if i == 3 else late
+
     def scores(n):
         h, i = steps[n]
-        rows = slice(i * tokens, (i + 1) * tokens)
         cs = slice(h * HD, (h + 1) * HD)
-        q = carry_ref[rows, cs].astype(BF16)
-        before = carry_ref[rows, 2 * mine + 2 * h : 2 * mine + 2 * h + 1]
-        top = jnp.broadcast_to(before, (tokens, HD))
+        if i == 3:
+            q = last_ref[:, cs]
+        else:
+            q = carry_ref[i * tokens : (i + 1) * tokens, cs].astype(BF16)
+        top = jnp.full((tokens, HD), -jnp.inf, F32)
         for b in range(0, blocks, 4):
             keys = pool_ref[b : b + 4, :, cs].reshape(4 * block, HD)
             s = lax.dot_general(q, keys, NT, preferred_element_type=F32)
@@ -151,24 +157,40 @@
                 piece = jnp.where(own(b + d), -jnp.inf, s[:, d * block : (d + 1) * block])
                 s_ref[n % 2, :, (b + d) * block : (b + d + 1) * block] = piece
                 top = jnp.maximum(top, piece)
-        tops[n] = (before, jnp.max(top, axis=1, keepdims=True))
+        at = stale
+        for keys in extra(h, i, 0):
+            s = lax.dot_general(q, keys, NT, preferred_element_type=F32)
+            s_ref[n % 2, :, at : at + keys.shape[0]] = s
+            at += keys.shape[0]
+            for d in range(0, keys.shape[0], HD):
+                top = jnp.maximum(top, s[:, d : d + HD])
+        tops[n] = jnp.max(top, axis=1, keepdims=True)
 
     def weigh(n):
         h, i = steps[n]
         rows = slice(i * tokens, (i + 1) * tokens)
         cs = slice(mine + h * HD, mine + (h + 1) * HD)
-        before, top = tops.pop(n)
-        shrink = jnp.exp2((before - top) * SCALE)
+        top = tops.pop(n)
+        if i == 3:
+            acc = jnp.zeros((tokens, HD), F32)
+            total = jnp.zeros((tokens, 1), F32)
+        else:
+            before = carry_ref[rows, 2 * mine + 2 * h : 2 * mine + 2 * h + 1]
+            top = jnp.maximum(top, before)
+            shrink = jnp.exp2((before - top) * SCALE)
+            acc = carry_ref[rows, cs] * shrink
+            total = carry_ref[rows, 2 * mine + 2 * h + 1 : 2 * mine + 2 * h + 2] * shrink
         top = top * SCALE
         sums = jnp.zeros((tokens, HD), F32)
-        acc = carry_ref[rows, cs] * shrink
-        for b in range(0, blocks, 4):
-            w = jnp.exp2(s_ref[n % 2, :, b * block : (b + 4) * block] * SCALE - top)
-            for d in range(4):
-                sums = sums + w[:, d * block : (d + 1) * block]
-            values = pool_ref[b : b + 4, :, cs].reshape(4 * block, HD)
-            acc = acc + jnp.dot(w.astype(BF16), values, preferred_element_type=F32)
-        total = carry_ref[rows, 2 * mine + 2 * h + 1 : 2 * mine + 2 * h + 2] * shrink
+        values = [pool_ref[b : b + 4, :, cs].reshape(4 * block, HD) for b in range(0, blocks, 4)]
+        at = 0
+        for v in values + extra(h, i, 1):
+            width = v.shape[0]
+            w = jnp.exp2(s_ref[n % 2, :, at : at + width] * SCALE - top)
+            at += width
+            for d in range(0, width, HD):
+                sums = sums + w[:, d : d + HD]
+            acc = acc + jnp.dot(w.astype(BF16), v, preferred_element_type=F32)
         total = total + jnp.sum(sums, axis=1, keepdims=True)
         out_ref[places[i], :, h * HD : (h + 1) * HD] = (acc / total).astype(BF16)
 
@@ -229,41 +251,32 @@
         name="follow",
     )(planes, other)
     other = lax.ppermute(other, EVERY, flips(1, 1))
-    near, same = pl.pallas_call(
-        arrive,
-        out_shape=(part, part),
-        in_specs=[ANY, ANY],
+    pool = lax.all_to_all(planes, ("y", "x"), split_axis=0, concat_axis=0)
+
+    early = 3 * tokens
+    carry = jax.ShapeDtypeStruct((early, 2 * mine + HD), F32)
+    carry, kv = pl.pallas_call(
+        attend_early,
+        out_shape=(carry, jax.ShapeDtypeStruct((early, 2 * mine), BF16)),
+        in_specs=[ANY] * 3,
         out_specs=(ANY, ANY),
-        input_output_aliases={0: 0, 1: 1},
-        compiler_params=pltpu.CompilerParams(vmem_limit_bytes=LIMIT),
-        cost_estimate=pl.CostEstimate(flops=ARRIVE_COST, bytes_accessed=0, transcendentals=0),
-        name="arrive",
-    )(near, same)
-    pool = lax.all_to_all(planes, ("y", "x"), split_axis=0, concat_axis=0)
-
-    fresh = 4 * tokens
-    carry = jax.ShapeDtypeStruct((fresh, 2 * mine + HD), F32)
-    carry = pl.pallas_call(
-        attend_fresh,
-        out_shape=carry,
-        in_specs=[ANY] * 4,
-        out_specs=ANY,
         scratch_shapes=[
-            pltpu.VMEM((4, tokens, 3 * mine), BF16),
+            pltpu.VMEM((3, tokens, 3 * mine), BF16),
             pltpu.VMEM(carry.shape, F32),
-            pltpu.VMEM((2, tokens, fresh), F32),
-            dma((4,)),
-            dma((4,)),
+            pltpu.VMEM((2, tokens, early), F32),
+            dma((3,)),
+            dma((6,)),
         ],
         compiler_params=pltpu.CompilerParams(vmem_limit_bytes=LIMIT),
-        cost_estimate=pl.CostEstimate(flops=FRESH_COST, bytes_accessed=3 << 20, transcendentals=0),
-        name="attend_fresh",
-    )(own, near, same, other)
-    total_keys = 16 * 8 * pooled
+        cost_estimate=pl.CostEstimate(flops=EARLY_COST, bytes_accessed=3 << 20, transcendentals=0),
+        name="attend_early",
+    )(own, near, same)
+    fresh = 4 * tokens
+    total_keys = 16 * 8 * pooled + fresh
     out = pl.pallas_call(
         attend,
         out_shape=jax.ShapeDtypeStruct((4, tokens, mine), BF16),
-        in_specs=[VMEM, VMEM],
+        in_specs=[VMEM] * 4,
         out_specs=VMEM,
         scratch_shapes=[pltpu.VMEM((2, tokens, total_keys), F32)],
         compiler_params=pltpu.CompilerParams(vmem_limit_bytes=ATTEND_LIMIT),
@@ -273,7 +286,7 @@
             transcendentals=fresh * heads * total_keys,
         ),
         name="attend",
-    )(carry, pool)
+    )(carry, kv, other, pool)
     back = lax.all_to_all(out, ("zh", "core"), split_axis=0, concat_axis=0)
     return back.transpose(1, 0, 2).reshape(tokens, width)
 

time: 126 us -> 125 us (level)
  the two profiles are of different devices: /device:TPU:95 before, /device:TPU:128 now
where the time goes in v9:
time: 125 us; the launch traced here: 124 us
  waiting for transfers between devices  39 us (31%)
  starting transfers between devices  34.3 us (27%)
  blocking collectives  33.4 us (27%)
  Pallas kernels  13.6 us (11%)
  local copies, waits for them, and re-layouts  3.56 us (3%)
    all_to_all x1, blocking collectives, local(): back = lax.all_to_all(out, ('zh', 'core'), split_axis=0, concat_axis=0)  33.4 us
    all_to_all x1, waiting for transfers between devices, local(): pool = lax.all_to_all(planes, ('y', 'x'), split_axis=0, concat_axis=0)  25.4 us
    all_to_all x1, starting transfers between devices, local(): lax.all_to_all(copies, 'zl', split_axis=0, concat_axis=0)  11.3 us
    ppermute x1, waiting for transfers between devices, local(): same = lax.ppermute(same, EVERY, flips(1, 0))  11 us
    ppermute x1, starting transfers between devices, local(): same = lax.ppermute(same, EVERY, flips(1, 0))  8.22 us
    all_to_all x1, starting transfers between devices, local(): pool = lax.all_to_all(planes, ('y', 'x'), split_axis=0, concat_axis=0)  7.05 us
    ppermute x1, starting transfers between devices, local(): other = lax.ppermute(other, EVERY, flips(1, 1))  5.88 us
    pallas_call x1, Pallas kernels, local(): pl.pallas_call(attend, out_shape=jax.ShapeDtypeStruct((4, tokens, mine),...  5.77 us
  transfers between devices with their start and end apart: 5, of which 3 were waited for; matrix products, arithmetic and copies ran while one was open for 0% of the time, Pallas kernels for 4%

profile of v9, /device:TPU:128, one launch (start us, length us, event | category | flops | bytes accessed | tf_op | source)
XLA Modules:
  0.0 124.0 jit_solution(10713283124172352627)
XLA Ops:
  0.0 2.4 %pack.1 = (bf16[128,1152]{1,0:T(8,128)(2,1)}, bf16[128,1152]{1,0:T(8,128)(2,1)}, bf16[128,1152]{1,0:T(8,128)(2,1)}, bf16[128,1152]{1,0:T(8,128)(2,1)}, bf16[8,16,768]{2,1,0:T(8,128)(2,1)}) custom-call(bf16[128,1536]{1,0:T(8,128)(2,1)} %qa.1, bf16[128,1536]{1,0:T(8,128)(2,1)} %ka.1, bf16[128,1536]{1,0:T(8,128)(2,1)} %va.1, bf16[16,384]{1,0:T(8,128)(2,1)} %ksa.1, ...), custom_call_target="tpu_custom_call" | custom-call | bytes 3145728 | tf_op jit(solution)/shard_map/pack/pallas_call | solution.py:220
  2.4 11.3 %all-to-all-start = ((bf16[8,16,768]{2,1,0:T(8,128)(2,1)}), bf16[8,16,768]{2,1,0:T(8,128)(2,1)S(1)}, u32[]{:S(2)}, u32[]{:S(2)}) async-start(bf16[8,16,768]{2,1,0:T(8,128)(2,1)} %get-tuple-element.17), calls=%async_computation | async-start | bytes 393216 | tf_op jit(solution)/shard_map/all_to_all | solution.py:232
  13.7 1.9 %collective-permute-start = (bf16[128,1152]{1,0:T(8,128)(2,1)}, bf16[128,1152]{1,0:T(8,128)(2,1)}, u32[]{:S(2)}, u32[]{:S(2)}) collective-permute-start(bf16[128,1152]{1,0:T(8,128)(2,1)} %get-tuple-element.13), channel_id=1, source_target_pairs={{0,1},{1,0},{2,3},{3,2},{4,5},{5,4},{6,7},{7,6},{8,9},{9,8},{10,11... | collective-permute-start | bytes 884744 | tf_op jit(solution)/shard_map/ppermute | solution.py:230
  15.6 8.2 %collective-permute-start.1 = (bf16[128,1152]{1,0:T(8,128)(2,1)}, bf16[128,1152]{1,0:T(8,128)(2,1)}, u32[]{:S(2)}, u32[]{:S(2)}) collective-permute-start(bf16[128,1152]{1,0:T(8,128)(2,1)} %get-tuple-element.14), channel_id=1, source_target_pairs={{0,2},{1,3},{2,0},{3,1},{4,6},{5,7},{6,4},{7,5},{8,10},{9,11},{10,... | collective-permute-start | bytes 884744 | tf_op jit(solution)/shard_map/ppermute | solution.py:231
  23.9 0.0 all-to-all-done
  23.9 1.8 %spread.1.first_ref = bf16[16,128,768]{2,1,0:T(8,128)(2,1)} custom-call(bf16[128,768]{1,0:T(8,128)(2,1)S(1)} %bitcast.3), custom_call_target="tpu_custom_call" | custom-call | bytes 3145728 | tf_op jit(solution)/shard_map/spread/pallas_call | solution.py:233
  25.7 7.0 %all-to-all-start.1 = ((bf16[16,128,768]{2,1,0:T(8,128)(2,1)}), bf16[16,128,768]{2,1,0:T(8,128)(2,1)S(1)}, u32[]{:S(2)}, u32[]{:S(2)}) async-start(bf16[16,128,768]{2,1,0:T(8,128)(2,1)} %spread.1.first_ref), calls=%async_computation.1 | async-start | bytes 6291456 | tf_op jit(solution)/shard_map/all_to_all | solution.py:254
  32.7 5.9 %collective-permute-start.2 = (bf16[128,1152]{1,0:T(8,128)(2,1)}, bf16[128,1152]{1,0:T(8,128)(2,1)S(1)}, u32[]{:S(2)}, u32[]{:S(2)}) collective-permute-start(bf16[128,1152]{1,0:T(8,128)(2,1)} %follow.1), channel_id=1, source_target_pairs={{0,3},{1,2},{2,1},{3,0},{4,7},{5,6},{6,5},{7,4},{8,11},{9,10},{10,... | collective-permute-start | bytes 884744 | tf_op jit(solution)/shard_map/ppermute | solution.py:253
  38.6 0.0 collective-permute-done.p1
  38.6 11.0 %collective-permute-done.1.p2 = bf16[128,1152]{1,0:T(8,128)(2,1)} collective-permute-done((bf16[128,1152]{1,0:T(8,128)(2,1)}, bf16[128,1152]{1,0:T(8,128)(2,1)}, u32[]{:S(2)}, u32[]{:S(2)}) %collective-permute-start.1) | collective-permute-done | bytes 294944 | tf_op jit(solution)/shard_map/ppermute | solution.py:231
  49.7 3.6 %attend_early.1 = (f32[384,896]{1,0:T(8,128)}, bf16[384,768]{1,0:T(8,128)(2,1)}) custom-call(bf16[128,1152]{1,0:T(8,128)(2,1)} %get-tuple-element.12.p0, bf16[128,1152]{1,0:T(8,128)(2,1)} %collective-permute-done.p1, bf16[128,1152]{1,0:T(8,128)(2,1)} %collective-permute-done.1.p2), custom_call_target="tpu_custom_call" | custom-call | flops 64424509440 | bytes 3145728 | tf_op jit(solution)/shard_map/attend_early/pallas_call | solution.py:258
  53.3 2.5 %collective-permute-done.2.last_ref = bf16[128,1152]{1,0:T(8,128)(2,1)S(1)} collective-permute-done((bf16[128,1152]{1,0:T(8,128)(2,1)}, bf16[128,1152]{1,0:T(8,128)(2,1)S(1)}, u32[]{:S(2)}, u32[]{:S(2)}) %collective-permute-start.2) | collective-permute-done | bytes 294944 | tf_op jit(solution)/shard_map/ppermute | solution.py:253
  55.9 25.4 %all-to-all-done.1.pool_ref = bf16[16,128,768]{2,1,0:T(8,128)(2,1)S(1)} async-done(((bf16[16,128,768]{2,1,0:T(8,128)(2,1)}), bf16[16,128,768]{2,1,0:T(8,128)(2,1)S(1)}, u32[]{:S(2)}, u32[]{:S(2)}) %all-to-all-start.1) | async-done | bytes 3145760 | tf_op jit(solution)/shard_map/all_to_all | solution.py:254
  81.3 0.0 copy-start
  81.3 1.3 %copy-done = f32[384,896]{1,0:T(8,128)S(1)} copy-done((f32[384,896]{1,0:T(8,128)S(1)}, f32[384,896]{1,0:T(8,128)}, u32[]{:S(2)}) %copy-start) | copy-done | bytes 1376280
  82.6 0.0 copy-start.1
  82.6 1.1 copy-done.1
  83.7 5.8 %attend.1 = bf16[4,128,384]{2,1,0:T(8,128)(2,1)S(1)} custom-call(f32[384,896]{1,0:T(8,128)S(1)} %copy-done, bf16[384,768]{1,0:T(8,128)(2,1)S(1)} %copy-done.1, bf16[128,1152]{1,0:T(8,128)(2,1)S(1)} %collective-permute-done.2.last_ref, bf16[16,128,768]{2,1,0:T(8,128)(2,1)S(1)} %all-to-all-done.1.pool_ref), custom_call_target="tpu_custom_call" | custom-call | flops 2013265920 | bytes 6291456 | tf_op jit(solution)/shard_map/attend/pallas_call | solution.py:276
  89.5 33.4 %all_to_all.15 = bf16[4,128,384]{2,1,0:T(8,128)(2,1)S(1)} all-to-all(bf16[4,128,384]{2,1,0:T(8,128)(2,1)S(1)} %attend.1), channel_id=1, replica_groups=mesh['y'=4,'x'=4,'zl'=8,'zh'=2,'core'=2] {'zh','core'}, dimensions={0} | all-to-all | bytes 786432 | tf_op jit(solution)/shard_map/all_to_all | solution.py:290
  122.9 0.2 copy.7
  123.1 0.9 copy.8
  (1 shorter events, 0.0 us)
Async XLA Ops:
  2.4 21.4 %all-to-all-start = ((bf16[8,16,768]{2,1,0:T(8,128)(2,1)}), bf16[8,16,768]{2,1,0:T(8,128)(2,1)S(1)}, u32[]{:S(2)}, u32[]{:S(2)}) async-start(bf16[8,16,768]{2,1,0:T(8,128)(2,1)} %get-tuple-element.17), calls=%async_computation | async-start | bytes 393216 | tf_op jit(solution)/shard_map/all_to_all | solution.py:232
  13.7 24.9 %collective-permute-start = (bf16[128,1152]{1,0:T(8,128)(2,1)}, bf16[128,1152]{1,0:T(8,128)(2,1)}, u32[]{:S(2)}, u32[]{:S(2)}) collective-permute-start(bf16[128,1152]{1,0:T(8,128)(2,1)} %get-tuple-element.13), channel_id=1, source_target_pairs={{0,1},{1,0},{2,3},{3,2},{4,5},{5,4},{6,7},{7,6},{8,9},{9,8},{10,11... | collective-permute-start | bytes 884744 | tf_op jit(solution)/shard_map/ppermute | solution.py:230
  15.6 34.0 %collective-permute-start.1 = (bf16[128,1152]{1,0:T(8,128)(2,1)}, bf16[128,1152]{1,0:T(8,128)(2,1)}, u32[]{:S(2)}, u32[]{:S(2)}) collective-permute-start(bf16[128,1152]{1,0:T(8,128)(2,1)} %get-tuple-element.14), channel_id=1, source_target_pairs={{0,2},{1,3},{2,0},{3,1},{4,6},{5,7},{6,4},{7,5},{8,10},{9,11},{10,... | collective-permute-start | bytes 884744 | tf_op jit(solution)/shard_map/ppermute | solution.py:231
  25.7 55.6 %all-to-all-start.1 = ((bf16[16,128,768]{2,1,0:T(8,128)(2,1)}), bf16[16,128,768]{2,1,0:T(8,128)(2,1)S(1)}, u32[]{:S(2)}, u32[]{:S(2)}) async-start(bf16[16,128,768]{2,1,0:T(8,128)(2,1)} %spread.1.first_ref), calls=%async_computation.1 | async-start | bytes 6291456 | tf_op jit(solution)/shard_map/all_to_all | solution.py:254
  32.7 23.1 %collective-permute-start.2 = (bf16[128,1152]{1,0:T(8,128)(2,1)}, bf16[128,1152]{1,0:T(8,128)(2,1)S(1)}, u32[]{:S(2)}, u32[]{:S(2)}) collective-permute-start(bf16[128,1152]{1,0:T(8,128)(2,1)} %follow.1), channel_id=1, source_target_pairs={{0,3},{1,2},{2,1},{3,0},{4,7},{5,6},{6,5},{7,4},{8,11},{9,10},{10,... | collective-permute-start | bytes 884744 | tf_op jit(solution)/shard_map/ppermute | solution.py:253
  81.3 1.3 %copy-start = (f32[384,896]{1,0:T(8,128)S(1)}, f32[384,896]{1,0:T(8,128)}, u32[]{:S(2)}) copy-start(f32[384,896]{1,0:T(8,128)} %get-tuple-element.15.carry_ref) | copy-start | bytes 4128772
  82.6 1.1 copy-start.1

commit v10 on v9

--- a/solution.py
+++ b/solution.py
@@ -1,3 +1,4 @@
+import functools
 import math
 
 import jax
@@ -122,16 +123,16 @@
         c.wait()
 
 
-def attend(carry_ref, kv_ref, last_ref, pool_ref, out_ref, s_ref):
-    tokens, mine = out_ref.shape[1:]
+def attend(parts, carry_ref, kv_ref, last_ref, pool_ref, *refs):
+    outs, s_ref = refs[:-1], refs[-1]
+    tokens, mine = outs[0].shape
     heads = mine // HD
     blocks, block = pool_ref.shape[0], pool_ref.shape[1]
     stale = blocks * block
     here = lax.axis_index("y") * 4 + lax.axis_index("x")
     first = here * block + lax.axis_index("zl") * (block // 8)
     col = lax.broadcasted_iota(jnp.int32, (tokens, block), 1)
-    places = peers()
-    steps = [(h, i) for i in range(4) for h in range(heads)]
+    steps = [(h, i) for i in parts for h in range(heads)]
     tops = {}
 
     def own(b):
@@ -192,13 +193,19 @@
                 sums = sums + w[:, d : d + HD]
             acc = acc + jnp.dot(w.astype(BF16), v, preferred_element_type=F32)
         total = total + jnp.sum(sums, axis=1, keepdims=True)
-        out_ref[places[i], :, h * HD : (h + 1) * HD] = (acc / total).astype(BF16)
+        outs[parts.index(i)][:, h * HD : (h + 1) * HD] = (acc / total).astype(BF16)
 
     scores(0)
     for n in range(len(steps)):
         if n + 1 < len(steps):
             scores(n + 1)
         weigh(n)
+
+
+def unpack(p0, p1, p2, p3, out_ref):
+    mine = p0.shape[1]
+    for place, ref in zip(peers(), (p0, p1, p2, p3)):
+        out_ref[:, pl.ds(pl.multiple_of(place * mine, HD), mine)] = ref[...]
 
 
 def flips(zh, core):
@@ -273,22 +280,38 @@
     )(own, near, same)
     fresh = 4 * tokens
     total_keys = 16 * 8 * pooled + fresh
-    out = pl.pallas_call(
-        attend,
-        out_shape=jax.ShapeDtypeStruct((4, tokens, mine), BF16),
+    block = jax.ShapeDtypeStruct((tokens, mine), BF16)
+
+    def finish(parts):
+        return pl.pallas_call(
+            functools.partial(attend, parts),
+            out_shape=(block, block),
+            in_specs=[VMEM] * 4,
+            out_specs=(VMEM, VMEM),
+            scratch_shapes=[pltpu.VMEM((2, tokens, total_keys), F32)],
+            compiler_params=pltpu.CompilerParams(vmem_limit_bytes=ATTEND_LIMIT),
+            cost_estimate=pl.CostEstimate(
+                flops=2 * fresh * heads * total_keys * HD,
+                bytes_accessed=6 << 20,
+                transcendentals=fresh * heads * total_keys // 2,
+            ),
+            name="attend",
+        )(carry, kv, other, pool)
+
+    same, far = finish((2, 3))
+    same = lax.ppermute(same, EVERY, flips(1, 0))
+    far = lax.ppermute(far, EVERY, flips(1, 1))
+    own, near = finish((0, 1))
+    near = lax.ppermute(near, EVERY, flips(0, 1))
+    return pl.pallas_call(
+        unpack,
+        out_shape=jax.ShapeDtypeStruct((tokens, width), BF16),
         in_specs=[VMEM] * 4,
         out_specs=VMEM,
-        scratch_shapes=[pltpu.VMEM((2, tokens, total_keys), F32)],
-        compiler_params=pltpu.CompilerParams(vmem_limit_bytes=ATTEND_LIMIT),
-        cost_estimate=pl.CostEstimate(
-            flops=4 * fresh * heads * total_keys * HD,
-            bytes_accessed=6 << 20,
-            transcendentals=fresh * heads * total_keys,
-        ),
-        name="attend",
-    )(carry, kv, other, pool)
-    back = lax.all_to_all(out, ("zh", "core"), split_axis=0, concat_axis=0)
-    return back.transpose(1, 0, 2).reshape(tokens, width)
+        compiler_params=pltpu.CompilerParams(vmem_limit_bytes=SPREAD_LIMIT),
+        cost_estimate=pl.CostEstimate(flops=0, bytes_accessed=1 << 20, transcendentals=0),
+        name="unpack",
+    )(own, near, same, far)
 
 
 def solution(mesh):

time: 125 us -> 121 us (0.968)
  the two profiles are of different devices: /device:TPU:128 before, /device:TPU:28 now
where the time goes in v10:
time: 121 us
  waiting for transfers between devices  53.1 us (44%)
  starting transfers between devices  50.3 us (42%)
  Pallas kernels  14.8 us (12%)
  local copies, waits for them, and re-layouts  2.4 us (2%)
    ppermute x1, waiting for transfers between devices, local(): other = lax.ppermute(other, EVERY, flips(1, 1))  39.8 us
    ppermute x2, starting transfers between devices, local(): same = lax.ppermute(same, EVERY, flips(1, 0))  15.9 us
    all_to_all x1, starting transfers between devices, local(): lax.all_to_all(copies, 'zl', split_axis=0, concat_axis=0)  12.5 us
    ppermute x1, waiting for transfers between devices, local(): far = lax.ppermute(far, EVERY, flips(1, 1))  9.42 us
    all_to_all x1, starting transfers between devices, local(): pool = lax.all_to_all(planes, ('y', 'x'), split_axis=0, concat_axis=0)  7.13 us
    pallas_call x2, Pallas kernels, finish(): pl.pallas_call(functools.partial(attend, parts), out_shape=(block, block)...  6.18 us
    ppermute x1, starting transfers between devices, local(): far = lax.ppermute(far, EVERY, flips(1, 1))  6.06 us
    ppermute x2, starting transfers between devices, local(): near = lax.ppermute(near, EVERY, flips(0, 1))  4.75 us
  transfers between devices with their start and end apart: 8, of which 3 were waited for; matrix products, arithmetic and copies ran while one was open for 0% of the time, Pallas kernels for 7%

profile of v10, /device:TPU:28, one launch (start us, length us, event | category | flops | bytes accessed | tf_op | source)
XLA Modules:
  0.0 120.7 jit_solution(7165963163639151252)
XLA Ops:
  0.0 2.4 %pack.1 = (bf16[128,1152]{1,0:T(8,128)(2,1)}, bf16[128,1152]{1,0:T(8,128)(2,1)}, bf16[128,1152]{1,0:T(8,128)(2,1)}, bf16[128,1152]{1,0:T(8,128)(2,1)}, bf16[8,16,768]{2,1,0:T(8,128)(2,1)}) custom-call(bf16[128,1536]{1,0:T(8,128)(2,1)} %qa.1, bf16[128,1536]{1,0:T(8,128)(2,1)} %ka.1, bf16[128,1536]{1,0:T(8,128)(2,1)} %va.1, bf16[16,384]{1,0:T(8,128)(2,1)} %ksa.1, ...), custom_call_target="tpu_custom_call" | custom-call | bytes 3145728 | tf_op jit(solution)/shard_map/pack/pallas_call | solution.py:227
  2.4 12.5 %all-to-all-start = ((bf16[8,16,768]{2,1,0:T(8,128)(2,1)}), bf16[8,16,768]{2,1,0:T(8,128)(2,1)S(1)}, u32[]{:S(2)}, u32[]{:S(2)}) async-start(bf16[8,16,768]{2,1,0:T(8,128)(2,1)} %get-tuple-element.21), calls=%async_computation | async-start | bytes 393216 | tf_op jit(solution)/shard_map/all_to_all | solution.py:239
  15.0 1.9 %collective-permute-start = (bf16[128,1152]{1,0:T(8,128)(2,1)}, bf16[128,1152]{1,0:T(8,128)(2,1)}, u32[]{:S(2)}, u32[]{:S(2)}) collective-permute-start(bf16[128,1152]{1,0:T(8,128)(2,1)} %get-tuple-element.17), channel_id=1, source_target_pairs={{0,1},{1,0},{2,3},{3,2},{4,5},{5,4},{6,7},{7,6},{8,9},{9,8},{10,11... | collective-permute-start | bytes 884744 | tf_op jit(solution)/shard_map/ppermute | solution.py:237
  16.9 8.2 %collective-permute-start.1 = (bf16[128,1152]{1,0:T(8,128)(2,1)}, bf16[128,1152]{1,0:T(8,128)(2,1)}, u32[]{:S(2)}, u32[]{:S(2)}) collective-permute-start(bf16[128,1152]{1,0:T(8,128)(2,1)} %get-tuple-element.18), channel_id=1, source_target_pairs={{0,2},{1,3},{2,0},{3,1},{4,6},{5,7},{6,4},{7,5},{8,10},{9,11},{10,... | collective-permute-start | bytes 884744 | tf_op jit(solution)/shard_map/ppermute | solution.py:238
  25.1 3.9 %all-to-all-done = bf16[8,16,768]{2,1,0:T(8,128)(2,1)S(1)} async-done(((bf16[8,16,768]{2,1,0:T(8,128)(2,1)}), bf16[8,16,768]{2,1,0:T(8,128)(2,1)S(1)}, u32[]{:S(2)}, u32[]{:S(2)}) %all-to-all-start) | async-done | bytes 196640 | tf_op jit(solution)/shard_map/all_to_all | solution.py:239
  29.0 1.8 %spread.1.first_ref = bf16[16,128,768]{2,1,0:T(8,128)(2,1)} custom-call(bf16[128,768]{1,0:T(8,128)(2,1)S(1)} %bitcast.1), custom_call_target="tpu_custom_call" | custom-call | bytes 3145728 | tf_op jit(solution)/shard_map/spread/pallas_call | solution.py:240
  30.8 7.1 %all-to-all-start.1 = ((bf16[16,128,768]{2,1,0:T(8,128)(2,1)}), bf16[16,128,768]{2,1,0:T(8,128)(2,1)S(1)}, u32[]{:S(2)}, u32[]{:S(2)}) async-start(bf16[16,128,768]{2,1,0:T(8,128)(2,1)} %spread.1.first_ref), calls=%async_computation.1 | async-start | bytes 6291456 | tf_op jit(solution)/shard_map/all_to_all | solution.py:261
  37.9 3.9 %collective-permute-start.2 = (bf16[128,1152]{1,0:T(8,128)(2,1)}, bf16[128,1152]{1,0:T(8,128)(2,1)S(1)}, u32[]{:S(2)}, u32[]{:S(2)}) collective-permute-start(bf16[128,1152]{1,0:T(8,128)(2,1)} %follow.1), channel_id=1, source_target_pairs={{0,3},{1,2},{2,1},{3,0},{4,7},{5,6},{6,5},{7,4},{8,11},{9,10},{10,... | collective-permute-start | bytes 884744 | tf_op jit(solution)/shard_map/ppermute | solution.py:260
  41.8 0.0 collective-permute-done.p1
  41.8 0.0 collective-permute-done.1.p2
  41.8 3.6 %attend_early.1 = (f32[384,896]{1,0:T(8,128)}, bf16[384,768]{1,0:T(8,128)(2,1)}) custom-call(bf16[128,1152]{1,0:T(8,128)(2,1)} %get-tuple-element.16.p0, bf16[128,1152]{1,0:T(8,128)(2,1)} %collective-permute-done.p1, bf16[128,1152]{1,0:T(8,128)(2,1)} %collective-permute-done.1.p2), custom_call_target="tpu_custom_call" | custom-call | flops 64424509440 | bytes 3145728 | tf_op jit(solution)/shard_map/attend_early/pallas_call | solution.py:265
  45.5 39.8 %collective-permute-done.2.last_ref = bf16[128,1152]{1,0:T(8,128)(2,1)S(1)} collective-permute-done((bf16[128,1152]{1,0:T(8,128)(2,1)}, bf16[128,1152]{1,0:T(8,128)(2,1)S(1)}, u32[]{:S(2)}, u32[]{:S(2)}) %collective-permute-start.2) | collective-permute-done | bytes 294944 | tf_op jit(solution)/shard_map/ppermute | solution.py:260
  85.3 0.0 all-to-all-done.1.pool_ref
  85.3 1.3 %copy-done = f32[384,896]{1,0:T(8,128)S(1)} copy-done((f32[384,896]{1,0:T(8,128)S(1)}, f32[384,896]{1,0:T(8,128)}, u32[]{:S(2)}) %copy-start) | copy-done | bytes 1376280
  86.6 1.1 copy-done.1
  87.7 3.2 %attend.3 = (bf16[128,384]{1,0:T(8,128)(2,1)S(1)}, bf16[128,384]{1,0:T(8,128)(2,1)S(1)}) custom-call(f32[384,896]{1,0:T(8,128)S(1)} %copy-done, bf16[384,768]{1,0:T(8,128)(2,1)S(1)} %copy-done.1, bf16[128,1152]{1,0:T(8,128)(2,1)S(1)} %collective-permute-done.2.last_ref, bf16[16,128,768]{2,1,0:T(8,128)(2,1)S(1)} %all-to-all-done.1.pool_ref), custom_call_target="tpu_custom_call" | custom-call | flops 1006632960 | bytes 6291456 | tf_op jit(solution)/shard_map/attend/pallas_call | solution.py:286
  90.9 7.7 %collective-permute-start.4 = (bf16[128,384]{1,0:T(8,128)(2,1)S(1)}, bf16[128,384]{1,0:T(8,128)(2,1)S(1)}, u32[]{:S(2)}, u32[]{:S(2)}) collective-permute-start(bf16[128,384]{1,0:T(8,128)(2,1)S(1)} %get-tuple-element.25), channel_id=1, source_target_pairs={{0,2},{1,3},{2,0},{3,1},{4,6},{5,7},{6,4},{7,5},{8,10},{9,11},{10,... | collective-permute-start | bytes 294920 | tf_op jit(solution)/shard_map/ppermute | solution.py:302
  98.6 6.1 %collective-permute-start.5 = (bf16[128,384]{1,0:T(8,128)(2,1)S(1)}, bf16[128,384]{1,0:T(8,128)(2,1)S(1)}, u32[]{:S(2)}, u32[]{:S(2)}) collective-permute-start(bf16[128,384]{1,0:T(8,128)(2,1)S(1)} %get-tuple-element.26), channel_id=1, source_target_pairs={{0,3},{1,2},{2,1},{3,0},{4,7},{5,6},{6,5},{7,4},{8,11},{9,10},{10,... | collective-permute-start | bytes 294920 | tf_op jit(solution)/shard_map/ppermute | solution.py:303
  104.6 3.0 %attend.2 = (bf16[128,384]{1,0:T(8,128)(2,1)S(1)}, bf16[128,384]{1,0:T(8,128)(2,1)S(1)}) custom-call(f32[384,896]{1,0:T(8,128)S(1)} %copy-done, bf16[384,768]{1,0:T(8,128)(2,1)S(1)} %copy-done.1, bf16[128,1152]{1,0:T(8,128)(2,1)S(1)} %collective-permute-done.2.last_ref, bf16[16,128,768]{2,1,0:T(8,128)(2,1)S(1)} %all-to-all-done.1.pool_ref), custom_call_target="tpu_custom_call" | custom-call | flops 1006632960 | bytes 6291456 | tf_op jit(solution)/shard_map/attend/pallas_call | solution.py:286
  107.6 2.8 %collective-permute-start.3 = (bf16[128,384]{1,0:T(8,128)(2,1)S(1)}, bf16[128,384]{1,0:T(8,128)(2,1)S(1)}, u32[]{:S(2)}, u32[]{:S(2)}) collective-permute-start(bf16[128,384]{1,0:T(8,128)(2,1)S(1)} %get-tuple-element.24), channel_id=1, source_target_pairs={{0,1},{1,0},{2,3},{3,2},{4,5},{5,4},{6,7},{7,6},{8,9},{9,8},{10,11... | collective-permute-start | bytes 294920 | tf_op jit(solution)/shard_map/ppermute | solution.py:305
  110.5 0.0 collective-permute-done.4.p2
  110.5 9.4 %collective-permute-done.5.p3 = bf16[128,384]{1,0:T(8,128)(2,1)S(1)} collective-permute-done((bf16[128,384]{1,0:T(8,128)(2,1)S(1)}, bf16[128,384]{1,0:T(8,128)(2,1)S(1)}, u32[]{:S(2)}, u32[]{:S(2)}) %collective-permute-start.5) | collective-permute-done | bytes 98336 | tf_op jit(solution)/shard_map/ppermute | solution.py:303
  119.9 0.0 collective-permute-done.3.p1
  119.9 0.8 unpack.1
  (3 shorter events, 0.0 us)
Async XLA Ops:
  2.4 26.5 %all-to-all-start = ((bf16[8,16,768]{2,1,0:T(8,128)(2,1)}), bf16[8,16,768]{2,1,0:T(8,128)(2,1)S(1)}, u32[]{:S(2)}, u32[]{:S(2)}) async-start(bf16[8,16,768]{2,1,0:T(8,128)(2,1)} %get-tuple-element.21), calls=%async_computation | async-start | bytes 393216 | tf_op jit(solution)/shard_map/all_to_all | solution.py:239
  15.0 26.9 %collective-permute-start = (bf16[128,1152]{1,0:T(8,128)(2,1)}, bf16[128,1152]{1,0:T(8,128)(2,1)}, u32[]{:S(2)}, u32[]{:S(2)}) collective-permute-start(bf16[128,1152]{1,0:T(8,128)(2,1)} %get-tuple-element.17), channel_id=1, source_target_pairs={{0,1},{1,0},{2,3},{3,2},{4,5},{5,4},{6,7},{7,6},{8,9},{9,8},{10,11... | collective-permute-start | bytes 884744 | tf_op jit(solution)/shard_map/ppermute | solution.py:237
  16.9 24.9 %collective-permute-start.1 = (bf16[128,1152]{1,0:T(8,128)(2,1)}, bf16[128,1152]{1,0:T(8,128)(2,1)}, u32[]{:S(2)}, u32[]{:S(2)}) collective-permute-start(bf16[128,1152]{1,0:T(8,128)(2,1)} %get-tuple-element.18), channel_id=1, source_target_pairs={{0,2},{1,3},{2,0},{3,1},{4,6},{5,7},{6,4},{7,5},{8,10},{9,11},{10,... | collective-permute-start | bytes 884744 | tf_op jit(solution)/shard_map/ppermute | solution.py:238
  30.8 54.5 %all-to-all-start.1 = ((bf16[16,128,768]{2,1,0:T(8,128)(2,1)}), bf16[16,128,768]{2,1,0:T(8,128)(2,1)S(1)}, u32[]{:S(2)}, u32[]{:S(2)}) async-start(bf16[16,128,768]{2,1,0:T(8,128)(2,1)} %spread.1.first_ref), calls=%async_computation.1 | async-start | bytes 6291456 | tf_op jit(solution)/shard_map/all_to_all | solution.py:261
  37.9 47.4 %collective-permute-start.2 = (bf16[128,1152]{1,0:T(8,128)(2,1)}, bf16[128,1152]{1,0:T(8,128)(2,1)S(1)}, u32[]{:S(2)}, u32[]{:S(2)}) collective-permute-start(bf16[128,1152]{1,0:T(8,128)(2,1)} %follow.1), channel_id=1, source_target_pairs={{0,3},{1,2},{2,1},{3,0},{4,7},{5,6},{6,5},{7,4},{8,11},{9,10},{10,... | collective-permute-start | bytes 884744 | tf_op jit(solution)/shard_map/ppermute | solution.py:260
  85.3 1.3 %copy-start = (f32[384,896]{1,0:T(8,128)S(1)}, f32[384,896]{1,0:T(8,128)}, u32[]{:S(2)}) copy-start(f32[384,896]{1,0:T(8,128)} %get-tuple-element.19.carry_ref) | copy-start | bytes 4128772
  86.6 1.1 copy-start.1
  90.9 19.6 %collective-permute-start.4 = (bf16[128,384]{1,0:T(8,128)(2,1)S(1)}, bf16[128,384]{1,0:T(8,128)(2,1)S(1)}, u32[]{:S(2)}, u32[]{:S(2)}) collective-permute-start(bf16[128,384]{1,0:T(8,128)(2,1)S(1)} %get-tuple-element.25), channel_id=1, source_target_pairs={{0,2},{1,3},{2,0},{3,1},{4,6},{5,7},{6,4},{7,5},{8,10},{9,11},{10,... | collective-permute-start | bytes 294920 | tf_op jit(solution)/shard_map/ppermute | solution.py:302
  98.6 21.4 %collective-permute-start.5 = (bf16[128,384]{1,0:T(8,128)(2,1)S(1)}, bf16[128,384]{1,0:T(8,128)(2,1)S(1)}, u32[]{:S(2)}, u32[]{:S(2)}) collective-permute-start(bf16[128,384]{1,0:T(8,128)(2,1)S(1)} %get-tuple-element.26), channel_id=1, source_target_pairs={{0,3},{1,2},{2,1},{3,0},{4,7},{5,6},{6,5},{7,4},{8,11},{9,10},{10,... | collective-permute-start | bytes 294920 | tf_op jit(solution)/shard_map/ppermute | solution.py:303
  107.6 12.3 %collective-permute-start.3 = (bf16[128,384]{1,0:T(8,128)(2,1)S(1)}, bf16[128,384]{1,0:T(8,128)(2,1)S(1)}, u32[]{:S(2)}, u32[]{:S(2)}) collective-permute-start(bf16[128,384]{1,0:T(8,128)(2,1)S(1)} %get-tuple-element.24), channel_id=1, source_target_pairs={{0,1},{1,0},{2,3},{3,2},{4,5},{5,4},{6,7},{7,6},{8,9},{9,8},{10,11... | collective-permute-start | bytes 294920 | tf_op jit(solution)/shard_map/ppermute | solution.py:305

commit v11 on v10

--- a/solution.py
+++ b/solution.py
@@ -51,6 +51,10 @@
             part[:, t * mine : (t + 1) * mine] = ref[:, cols]
 
 
+def landed(same_ref, far_ref, same_out, far_out):
+    pass
+
+
 def spread(line_ref, out_ref, sem):
     copies = [pltpu.make_async_copy(line_ref, out_ref.at[j], sem.at[j]) for j in range(out_ref.shape[0])]
     for c in copies:
@@ -63,7 +67,7 @@
     pass
 
 
-def attend_early(p0, p1, p2, out_ref, kv_ref, part_ref, carry_ref, s_ref, sem, sem_o):
+def attend_early(p0, p1, p2, out_ref, far_ref, kv_ref, part_ref, carry_ref, s_ref, sem, sem_o):
     parts, tokens = part_ref.shape[:2]
     mine = part_ref.shape[2] // 3
     heads = mine // HD
@@ -71,7 +75,8 @@
     stores = []
     for i in range(parts):
         rows = pl.ds(i * tokens, tokens)
-        stores.append(pltpu.make_async_copy(carry_ref.at[rows], out_ref.at[rows], sem_o.at[i]))
+        to = far_ref if i == 2 else out_ref.at[rows]
+        stores.append(pltpu.make_async_copy(carry_ref.at[rows], to, sem_o.at[i]))
     for i in range(parts):
         rows = pl.ds(i * tokens, tokens)
         stores.append(pltpu.make_async_copy(part_ref.at[i, :, mine:], kv_ref.at[rows], sem_o.at[parts + i]))
@@ -138,10 +143,14 @@
     def own(b):
         return (col >= first - b * block) & (col < first - b * block + block // 8)
 
+    def place(i):
+        return slice((i - parts[0]) * tokens, (i - parts[0] + 1) * tokens)
+
     def extra(h, i, t):
         late = [last_ref[:, (1 + t) * mine + h * HD : (1 + t) * mine + (h + 1) * HD]]
-        early = [kv_ref[:, t * mine + h * HD : t * mine + (h + 1) * HD]]
-        return early + late if i == 3 else late
+        if i != 3:
+            return late
+        return [kv_ref[:, t * mine + h * HD : t * mine + (h + 1) * HD]] + late
 
     def scores(n):
         h, i = steps[n]
@@ -149,7 +158,7 @@
         if i == 3:
             q = last_ref[:, cs]
         else:
-            q = carry_ref[i * tokens : (i + 1) * tokens, cs].astype(BF16)
+            q = carry_ref[place(i), cs].astype(BF16)
         top = jnp.full((tokens, HD), -jnp.inf, F32)
         for b in range(0, blocks, 4):
             keys = pool_ref[b : b + 4, :, cs].reshape(4 * block, HD)
@@ -169,7 +178,7 @@
 
     def weigh(n):
         h, i = steps[n]
-        rows = slice(i * tokens, (i + 1) * tokens)
+        rows = place(i)
         cs = slice(mine + h * HD, mine + (h + 1) * HD)
         top = tops.pop(n)
         if i == 3:
@@ -262,11 +271,13 @@
 
     early = 3 * tokens
     carry = jax.ShapeDtypeStruct((early, 2 * mine + HD), F32)
-    carry, kv = pl.pallas_call(
+    rows = jax.ShapeDtypeStruct((2 * tokens, 2 * mine + HD), F32)
+    rows_far = jax.ShapeDtypeStruct((tokens, 2 * mine + HD), F32)
+    carry, carry_far, kv = pl.pallas_call(
         attend_early,
-        out_shape=(carry, jax.ShapeDtypeStruct((early, 2 * mine), BF16)),
+        out_shape=(rows, rows_far, jax.ShapeDtypeStruct((early, 2 * mine), BF16)),
         in_specs=[ANY] * 3,
-        out_specs=(ANY, ANY),
+        out_specs=(ANY, ANY, ANY),
         scratch_shapes=[
             pltpu.VMEM((3, tokens, 3 * mine), BF16),
             pltpu.VMEM(carry.shape, F32),
@@ -282,7 +293,7 @@
     total_keys = 16 * 8 * pooled + fresh
     block = jax.ShapeDtypeStruct((tokens, mine), BF16)
 
-    def finish(parts):
+    def finish(parts, carry, kv):
         return pl.pallas_call(
             functools.partial(attend, parts),
             out_shape=(block, block),
@@ -298,10 +309,21 @@
             name="attend",
         )(carry, kv, other, pool)
 
-    same, far = finish((2, 3))
+    same, far = finish((2, 3), carry_far, kv)
+    first = far
     same = lax.ppermute(same, EVERY, flips(1, 0))
     far = lax.ppermute(far, EVERY, flips(1, 1))
-    own, near = finish((0, 1))
+    same, far = pl.pallas_call(
+        landed,
+        out_shape=(block, block),
+        in_specs=[ANY] * 2,
+        out_specs=(ANY, ANY),
+        input_output_aliases={0: 0, 1: 1},
+        compiler_params=pltpu.CompilerParams(vmem_limit_bytes=SPREAD_LIMIT),
+        cost_estimate=pl.CostEstimate(flops=EARLY_COST, bytes_accessed=0, transcendentals=0),
+        name="landed",
+    )(same, far)
+    own, near = finish((0, 1), carry, first)
     near = lax.ppermute(near, EVERY, flips(0, 1))
     return pl.pallas_call(
         unpack,

time: 121 us -> 121 us (level)
    pallas_call x1 -> x2, Pallas kernels: 3.65 us -> 3.68 us  [the longest x1 3.68 us: local(): pl.pallas_call(attend_early, out_shape=(rows, rows_far, jax.ShapeDtypeStr...]
where the time goes in v11:
time: 121 us; the launch traced here: 120 us
  waiting for transfers between devices  53 us (44%)
  starting transfers between devices  50.3 us (42%)
  Pallas kernels  14.9 us (12%)
  local copies, waits for them, and re-layouts  2.17 us (2%)
    ppermute x1, waiting for transfers between devices, local(): other = lax.ppermute(other, EVERY, flips(1, 1))  39.7 us
    ppermute x2, starting transfers between devices, local(): same = lax.ppermute(same, EVERY, flips(1, 0))  15.9 us
    all_to_all x1, starting transfers between devices, local(): lax.all_to_all(copies, 'zl', split_axis=0, concat_axis=0)  12.5 us
    ppermute x1, waiting for transfers between devices, local(): far = lax.ppermute(far, EVERY, flips(1, 1))  9.4 us
    all_to_all x1, starting transfers between devices, local(): pool = lax.all_to_all(planes, ('y', 'x'), split_axis=0, concat_axis=0)  7.13 us
    pallas_call x2, Pallas kernels, finish(): pl.pallas_call(functools.partial(attend, parts), out_shape=(block, block)...  6.18 us
    ppermute x1, starting transfers between devices, local(): far = lax.ppermute(far, EVERY, flips(1, 1))  6.07 us
    ppermute x2, starting transfers between devices, local(): near = lax.ppermute(near, EVERY, flips(0, 1))  4.75 us
  transfers between devices with their start and end apart: 8, of which 3 were waited for; matrix products, arithmetic and copies ran while one was open for 0% of the time, Pallas kernels for 7%

profile of v11, /device:TPU:28, one launch (start us, length us, event | category | flops | bytes accessed | tf_op | source)
XLA Modules:
  0.0 120.4 jit_solution(9449098939315029161)
XLA Ops:
  0.0 2.4 %pack.1 = (bf16[128,1152]{1,0:T(8,128)(2,1)}, bf16[128,1152]{1,0:T(8,128)(2,1)}, bf16[128,1152]{1,0:T(8,128)(2,1)}, bf16[128,1152]{1,0:T(8,128)(2,1)}, bf16[8,16,768]{2,1,0:T(8,128)(2,1)}) custom-call(bf16[128,1536]{1,0:T(8,128)(2,1)} %qa.1, bf16[128,1536]{1,0:T(8,128)(2,1)} %ka.1, bf16[128,1536]{1,0:T(8,128)(2,1)} %va.1, bf16[16,384]{1,0:T(8,128)(2,1)} %ksa.1, ...), custom_call_target="tpu_custom_call" | custom-call | bytes 3145728 | tf_op jit(solution)/shard_map/pack/pallas_call | solution.py:236
  2.4 12.5 %all-to-all-start = ((bf16[8,16,768]{2,1,0:T(8,128)(2,1)}), bf16[8,16,768]{2,1,0:T(8,128)(2,1)S(1)}, u32[]{:S(2)}, u32[]{:S(2)}) async-start(bf16[8,16,768]{2,1,0:T(8,128)(2,1)} %get-tuple-element.25), calls=%async_computation | async-start | bytes 393216 | tf_op jit(solution)/shard_map/all_to_all | solution.py:248
  15.0 1.9 %collective-permute-start = (bf16[128,1152]{1,0:T(8,128)(2,1)}, bf16[128,1152]{1,0:T(8,128)(2,1)}, u32[]{:S(2)}, u32[]{:S(2)}) collective-permute-start(bf16[128,1152]{1,0:T(8,128)(2,1)} %get-tuple-element.20), channel_id=1, source_target_pairs={{0,1},{1,0},{2,3},{3,2},{4,5},{5,4},{6,7},{7,6},{8,9},{9,8},{10,11... | collective-permute-start | bytes 884744 | tf_op jit(solution)/shard_map/ppermute | solution.py:246
  16.9 8.2 %collective-permute-start.1 = (bf16[128,1152]{1,0:T(8,128)(2,1)}, bf16[128,1152]{1,0:T(8,128)(2,1)}, u32[]{:S(2)}, u32[]{:S(2)}) collective-permute-start(bf16[128,1152]{1,0:T(8,128)(2,1)} %get-tuple-element.21), channel_id=1, source_target_pairs={{0,2},{1,3},{2,0},{3,1},{4,6},{5,7},{6,4},{7,5},{8,10},{9,11},{10,... | collective-permute-start | bytes 884744 | tf_op jit(solution)/shard_map/ppermute | solution.py:247
  25.1 3.9 %all-to-all-done = bf16[8,16,768]{2,1,0:T(8,128)(2,1)S(1)} async-done(((bf16[8,16,768]{2,1,0:T(8,128)(2,1)}), bf16[8,16,768]{2,1,0:T(8,128)(2,1)S(1)}, u32[]{:S(2)}, u32[]{:S(2)}) %all-to-all-start) | async-done | bytes 196640 | tf_op jit(solution)/shard_map/all_to_all | solution.py:248
  29.0 1.8 %spread.1.first_ref = bf16[16,128,768]{2,1,0:T(8,128)(2,1)} custom-call(bf16[128,768]{1,0:T(8,128)(2,1)S(1)} %bitcast.1), custom_call_target="tpu_custom_call" | custom-call | bytes 3145728 | tf_op jit(solution)/shard_map/spread/pallas_call | solution.py:249
  30.8 7.1 %all-to-all-start.1 = ((bf16[16,128,768]{2,1,0:T(8,128)(2,1)}), bf16[16,128,768]{2,1,0:T(8,128)(2,1)S(1)}, u32[]{:S(2)}, u32[]{:S(2)}) async-start(bf16[16,128,768]{2,1,0:T(8,128)(2,1)} %spread.1.first_ref), calls=%async_computation.1 | async-start | bytes 6291456 | tf_op jit(solution)/shard_map/all_to_all | solution.py:270
  37.9 3.9 %collective-permute-start.2 = (bf16[128,1152]{1,0:T(8,128)(2,1)}, bf16[128,1152]{1,0:T(8,128)(2,1)S(1)}, u32[]{:S(2)}, u32[]{:S(2)}) collective-permute-start(bf16[128,1152]{1,0:T(8,128)(2,1)} %follow.1), channel_id=1, source_target_pairs={{0,3},{1,2},{2,1},{3,0},{4,7},{5,6},{6,5},{7,4},{8,11},{9,10},{10,... | collective-permute-start | bytes 884744 | tf_op jit(solution)/shard_map/ppermute | solution.py:269
  41.8 0.0 collective-permute-done.p1
  41.8 0.0 collective-permute-done.1.p2
  41.8 3.7 %attend_early.1 = (f32[256,896]{1,0:T(8,128)}, f32[128,896]{1,0:T(8,128)}, bf16[384,768]{1,0:T(8,128)(2,1)}) custom-call(bf16[128,1152]{1,0:T(8,128)(2,1)} %get-tuple-element.19.p0, bf16[128,1152]{1,0:T(8,128)(2,1)} %collective-permute-done.p1, bf16[128,1152]{1,0:T(8,128)(2,1)} %collective-permute-done.1.p2), custom_call_target="tpu_custom_call" | custom-call | flops 64424509440 | bytes 3145728 | tf_op jit(solution)/shard_map/attend_early/pallas_call | solution.py:276
  45.5 39.7 %collective-permute-done.2.last_ref = bf16[128,1152]{1,0:T(8,128)(2,1)S(1)} collective-permute-done((bf16[128,1152]{1,0:T(8,128)(2,1)}, bf16[128,1152]{1,0:T(8,128)(2,1)S(1)}, u32[]{:S(2)}, u32[]{:S(2)}) %collective-permute-start.2) | collective-permute-done | bytes 294944 | tf_op jit(solution)/shard_map/ppermute | solution.py:269
  85.3 0.0 all-to-all-done.1.pool_ref
  85.3 1.1 copy-done.1
  86.4 1.0 copy-done.2
  87.4 3.2 %attend.2 = (bf16[128,384]{1,0:T(8,128)(2,1)S(1)}, bf16[128,384]{1,0:T(8,128)(2,1)S(1)}) custom-call(f32[128,896]{1,0:T(8,128)S(1)} %copy-done.2, bf16[384,768]{1,0:T(8,128)(2,1)S(1)} %copy-done.1, bf16[128,1152]{1,0:T(8,128)(2,1)S(1)} %collective-permute-done.2.last_ref, bf16[16,128,768]{2,1,0:T(8,128)(2,1)S(1)} %all-to-all-done.1.pool_ref), custom_call_target="tpu_custom_call" | custom-call | flops 1006632960 | bytes 6291456 | tf_op jit(solution)/shard_map/attend/pallas_call | solution.py:297
  90.6 7.7 %collective-permute-start.4 = (bf16[128,384]{1,0:T(8,128)(2,1)S(1)}, bf16[128,384]{1,0:T(8,128)(2,1)S(1)}, u32[]{:S(2)}, u32[]{:S(2)}) collective-permute-start(bf16[128,384]{1,0:T(8,128)(2,1)S(1)} %get-tuple-element.30), channel_id=1, source_target_pairs={{0,2},{1,3},{2,0},{3,1},{4,6},{5,7},{6,4},{7,5},{8,10},{9,11},{10,... | collective-permute-start | bytes 294920 | tf_op jit(solution)/shard_map/ppermute | solution.py:314
  98.3 6.1 %collective-permute-start.5 = (bf16[128,384]{1,0:T(8,128)(2,1)S(1)}, bf16[128,384]{1,0:T(8,128)(2,1)S(1)}, u32[]{:S(2)}, u32[]{:S(2)}) collective-permute-start(bf16[128,384]{1,0:T(8,128)(2,1)S(1)} %get-tuple-element.27.kv_ref), channel_id=1, source_target_pairs={{0,3},{1,2},{2,1},{3,0},{4,7},{5,6},{6,5},{7,4},{8,11},{9,10},{10,... | collective-permute-start | bytes 294920 | tf_op jit(solution)/shard_map/ppermute | solution.py:315
  104.4 3.0 %attend.3 = (bf16[128,384]{1,0:T(8,128)(2,1)S(1)}, bf16[128,384]{1,0:T(8,128)(2,1)S(1)}) custom-call(f32[256,896]{1,0:T(8,128)S(1)} %copy-done, bf16[128,384]{1,0:T(8,128)(2,1)S(1)} %get-tuple-element.27.kv_ref, bf16[128,1152]{1,0:T(8,128)(2,1)S(1)} %collective-permute-done.2.last_ref, bf16[16,128,768]{2,1,0:T(8,128)(2,1)S(1)} %all-to-all-done.1.pool_ref), custom_call_target="tpu_custom_call" | custom-call | flops 1006632960 | bytes 6291456 | tf_op jit(solution)/shard_map/attend/pallas_call | solution.py:297
  107.4 2.8 %collective-permute-start.3 = (bf16[128,384]{1,0:T(8,128)(2,1)S(1)}, bf16[128,384]{1,0:T(8,128)(2,1)S(1)}, u32[]{:S(2)}, u32[]{:S(2)}) collective-permute-start(bf16[128,384]{1,0:T(8,128)(2,1)S(1)} %get-tuple-element.29), channel_id=1, source_target_pairs={{0,1},{1,0},{2,3},{3,2},{4,5},{5,4},{6,7},{7,6},{8,9},{9,8},{10,11... | collective-permute-start | bytes 294920 | tf_op jit(solution)/shard_map/ppermute | solution.py:327
  110.2 0.0 collective-permute-done.4.same_ref
  110.2 9.4 %collective-permute-done.5.far_ref = bf16[128,384]{1,0:T(8,128)(2,1)S(1)} collective-permute-done((bf16[128,384]{1,0:T(8,128)(2,1)S(1)}, bf16[128,384]{1,0:T(8,128)(2,1)S(1)}, u32[]{:S(2)}, u32[]{:S(2)}) %collective-permute-start.5) | collective-permute-done | bytes 98336 | tf_op jit(solution)/shard_map/ppermute | solution.py:315
  119.6 0.0 collective-permute-done.3.p1
  119.6 0.8 unpack.1
  (6 shorter events, 0.0 us)
Async XLA Ops:
  2.4 26.5 %all-to-all-start = ((bf16[8,16,768]{2,1,0:T(8,128)(2,1)}), bf16[8,16,768]{2,1,0:T(8,128)(2,1)S(1)}, u32[]{:S(2)}, u32[]{:S(2)}) async-start(bf16[8,16,768]{2,1,0:T(8,128)(2,1)} %get-tuple-element.25), calls=%async_computation | async-start | bytes 393216 | tf_op jit(solution)/shard_map/all_to_all | solution.py:248
  15.0 26.9 %collective-permute-start = (bf16[128,1152]{1,0:T(8,128)(2,1)}, bf16[128,1152]{1,0:T(8,128)(2,1)}, u32[]{:S(2)}, u32[]{:S(2)}) collective-permute-start(bf16[128,1152]{1,0:T(8,128)(2,1)} %get-tuple-element.20), channel_id=1, source_target_pairs={{0,1},{1,0},{2,3},{3,2},{4,5},{5,4},{6,7},{7,6},{8,9},{9,8},{10,11... | collective-permute-start | bytes 884744 | tf_op jit(solution)/shard_map/ppermute | solution.py:246
  16.9 25.0 %collective-permute-start.1 = (bf16[128,1152]{1,0:T(8,128)(2,1)}, bf16[128,1152]{1,0:T(8,128)(2,1)}, u32[]{:S(2)}, u32[]{:S(2)}) collective-permute-start(bf16[128,1152]{1,0:T(8,128)(2,1)} %get-tuple-element.21), channel_id=1, source_target_pairs={{0,2},{1,3},{2,0},{3,1},{4,6},{5,7},{6,4},{7,5},{8,10},{9,11},{10,... | collective-permute-start | bytes 884744 | tf_op jit(solution)/shard_map/ppermute | solution.py:247
  30.8 54.5 %all-to-all-start.1 = ((bf16[16,128,768]{2,1,0:T(8,128)(2,1)}), bf16[16,128,768]{2,1,0:T(8,128)(2,1)S(1)}, u32[]{:S(2)}, u32[]{:S(2)}) async-start(bf16[16,128,768]{2,1,0:T(8,128)(2,1)} %spread.1.first_ref), calls=%async_computation.1 | async-start | bytes 6291456 | tf_op jit(solution)/shard_map/all_to_all | solution.py:270
  37.9 47.4 %collective-permute-start.2 = (bf16[128,1152]{1,0:T(8,128)(2,1)}, bf16[128,1152]{1,0:T(8,128)(2,1)S(1)}, u32[]{:S(2)}, u32[]{:S(2)}) collective-permute-start(bf16[128,1152]{1,0:T(8,128)(2,1)} %follow.1), channel_id=1, source_target_pairs={{0,3},{1,2},{2,1},{3,0},{4,7},{5,6},{6,5},{7,4},{8,11},{9,10},{10,... | collective-permute-start | bytes 884744 | tf_op jit(solution)/shard_map/ppermute | solution.py:269
  85.3 19.1 %copy-start = (f32[256,896]{1,0:T(8,128)S(1)}, f32[256,896]{1,0:T(8,128)}, u32[]{:S(2)}) copy-start(f32[256,896]{1,0:T(8,128)} %get-tuple-element.22.carry_ref) | copy-start | bytes 2752516
  85.3 1.1 copy-start.1
  86.4 1.0 copy-start.2
  90.6 19.6 %collective-permute-start.4 = (bf16[128,384]{1,0:T(8,128)(2,1)S(1)}, bf16[128,384]{1,0:T(8,128)(2,1)S(1)}, u32[]{:S(2)}, u32[]{:S(2)}) collective-permute-start(bf16[128,384]{1,0:T(8,128)(2,1)S(1)} %get-tuple-element.30), channel_id=1, source_target_pairs={{0,2},{1,3},{2,0},{3,1},{4,6},{5,7},{6,4},{7,5},{8,10},{9,11},{10,... | collective-permute-start | bytes 294920 | tf_op jit(solution)/shard_map/ppermute | solution.py:314
  98.3 21.4 %collective-permute-start.5 = (bf16[128,384]{1,0:T(8,128)(2,1)S(1)}, bf16[128,384]{1,0:T(8,128)(2,1)S(1)}, u32[]{:S(2)}, u32[]{:S(2)}) collective-permute-start(bf16[128,384]{1,0:T(8,128)(2,1)S(1)} %get-tuple-element.27.kv_ref), channel_id=1, source_target_pairs={{0,3},{1,2},{2,1},{3,0},{4,7},{5,6},{6,5},{7,4},{8,11},{9,10},{10,... | collective-permute-start | bytes 294920 | tf_op jit(solution)/shard_map/ppermute | solution.py:315
  107.4 12.3 %collective-permute-start.3 = (bf16[128,384]{1,0:T(8,128)(2,1)S(1)}, bf16[128,384]{1,0:T(8,128)(2,1)S(1)}, u32[]{:S(2)}, u32[]{:S(2)}) collective-permute-start(bf16[128,384]{1,0:T(8,128)(2,1)S(1)} %get-tuple-element.29), channel_id=1, source_target_pairs={{0,1},{1,0},{2,3},{3,2},{4,5},{5,4},{6,7},{7,6},{8,9},{9,8},{10,11... | collective-permute-start | bytes 294920 | tf_op jit(solution)/shard_map/ppermute | solution.py:327
